TPU v7x, 32 devices: a whole 2x2x4 slice. The times are simulated.
32 devices in a mesh: chan: 16 (over z, y, core), win: 2 (over x).
Axes of the slice: x: 2, y: 2, z: 4, core: 2. Of those that a mesh axis runs over, the one named last changes fastest.
Arguments:
- traces: bfloat16 [24, 1024, 4096], P('win', 'chan'), may hold values from -6 to 6
- quality: int32 [1024], P('chan'), may hold values 0 or 1
- fold_block: int32 [1024, 1], replicated, may hold values from 0 to 15; in each aligned block of 64 rows (0 to 63, 64 to 127, ...) at most 8 rows name the same one
- fold_offset: int32 [1024], replicated, may hold values from 0 to 63
Outputs:
- neighbour_lags: float32 [1024, 64, 256], P(('chan', 'win'))
- fold_lags: float32 [1024, 256], P(('chan', 'win'))
Inputs may be any that keep to these rules, and one draw needn't show every extreme that they name: `fold_block`: within each aligned block of 64 channels no block number appears more than 8 times.
All inputs are finite; a program needn't handle non-finite values. No bound on the sum of `quality` on one device may be relied on, other than what follows from the above.
Results may differ from a plain program's by a relative error of at most 0.0052.
Values may be sent and summed in bfloat16 or wider, within the bound.
No kernel may reach another device: no remote copies, remote signals or barrier semaphores. Data moves between devices by JAX's collectives and lax.ppermute only.
A program may use at most 128 MiB of HBM per device.

v0:
```python
import functools
import math

import jax
import jax.numpy as jnp
import numpy as np
from jax import lax
from jax.experimental import pallas as pl
from jax.experimental.pallas import tpu as pltpu
from jax.sharding import PartitionSpec as P

F = 256
H = F // 2
BAND_LO = 32
NLAG = 256
REACH = 64
CAP = 8
SPAN = REACH + 8
smooth_reach = 4
ROW_STEPS = 3
VMEM_LIMIT = 32 * 1024 * 1024
SPECTRA_VMEM_LIMIT = 56 * 1024 * 1024


def lane_residues():
    return np.concatenate([np.arange(0, H, 2), np.arange(1, H, 2)])


def bin_order():
    residues = lane_residues()
    first = (residues - BAND_LO) % F
    second = (-residues - BAND_LO) % F
    second[0] = (H - BAND_LO) % F
    return first, second


def forward_table(length):
    samples = np.arange(length // 2, dtype=np.int64)[:, None]
    parts = []
    for parity in range(2):
        for bins in bin_order():
            bins = bins[parity * H // 2 : (parity + 1) * H // 2]
            angles = (samples * (bins + BAND_LO)[None, :] % length) * (2.0 * math.pi / length)
            parts += [np.cos(angles), -np.sin(angles)]
    return np.concatenate(parts, axis=1).astype(np.float32).astype(jnp.bfloat16)


def inverse_tables(factor):
    shifts = (np.arange(NLAG) + NLAG // 2)[None, :]
    residues = lane_residues()[:, None]
    angles = (residues * shifts % NLAG) * (2.0 * math.pi / NLAG)
    sign = np.where(shifts[0] % 2 == 0, 1.0, -1.0)
    real, imag = np.cos(angles), -np.sin(angles)
    real[0] = (1.0 + sign) / 2.0
    imag[0] = (1.0 - sign) / 2.0
    table = np.concatenate([real, imag], axis=0) * factor
    high = table.astype(np.float32).astype(jnp.bfloat16)
    low = (table - high.astype(np.float64)).astype(np.float32).astype(jnp.bfloat16)
    return high, low


def lag_transform(stacks, high, low):
    top = stacks.astype(jnp.bfloat16)
    rest = (stacks - top.astype(jnp.float32)).astype(jnp.bfloat16)
    dot = functools.partial(jnp.dot, preferred_element_type=jnp.float32)
    return dot(top, high) + (dot(rest, high) + dot(top, low))


def fold_columns(first, second, imag):
    lane = lax.broadcasted_iota(jnp.int32, first.shape, first.ndim - 1)
    return first + second, jnp.where(lane == 0, first - second, imag)


def lanes_of(shape):
    return lax.broadcasted_iota(jnp.int32, shape, len(shape) - 1)


def rows_of(shape):
    return lax.broadcasted_iota(jnp.int32, shape, len(shape) - 2)


def band_matrix():
    def bins(index):
        lane = index & (H - 1)
        residue = jnp.where(lane < H // 2, 2 * lane, 2 * lane - H + 1)
        residue = jnp.where(index < H, residue, jnp.where(lane == 0, H, F - residue))
        return (residue - BAND_LO + F) & (F - 1)

    apart = bins(rows_of((F, F))) - bins(lanes_of((F, F)))
    return (jnp.abs(apart) <= smooth_reach).astype(jnp.float32).astype(jnp.bfloat16)


def exact_dot(left, right):
    return jnp.dot(left.astype(jnp.bfloat16), right.astype(jnp.bfloat16), preferred_element_type=jnp.float32)


def slot_selector(owners, places, device, ch_dev):
    height, width = owners.shape
    per_row = width // ch_dev
    wanted = (owners == device).astype(jnp.float32)
    before = rows_of((width, width))
    after = lanes_of((width, width))
    earlier = ((before < after) & (before // ch_dev == after // ch_dev)).astype(jnp.float32)
    ranks = exact_dot(wanted, earlier)
    slots = jnp.where(wanted > 0, ranks, float(CAP))
    count = height * per_row * 2 * CAP
    to_row = (rows_of((count, height)) // (2 * CAP * per_row) == lanes_of((count, height))).astype(jnp.float32)
    row_slots = exact_dot(to_row, slots)
    row_places = exact_dot(to_row, places.astype(jnp.float32))
    shape = (count, width)
    row = rows_of(shape)
    mine = (row_slots == (row % CAP).astype(jnp.float32)) & (lanes_of(shape) // ch_dev == row // (2 * CAP) % per_row)
    place = jnp.sum(jnp.where(mine, row_places + 1.0, 0.0), axis=1, keepdims=True).astype(jnp.int32) - 1
    shape = (count, 2 * ch_dev)
    half = rows_of(shape) // CAP % 2
    lane = lanes_of(shape)
    return ((lane == place + ch_dev * half) & (place >= 0)).astype(jnp.float32).astype(jnp.bfloat16)


def spectra_kernel(traces_ref, table_ref, quality_ref, whitened_ref, band_ref, keep_ref):
    rows, length = traces_ref.shape
    ch_dev = quality_ref.shape[1]

    @pl.when(pl.program_id(0) == 0)
    def _():
        band_ref[...] = band_matrix()
        shape = (rows, ch_dev)
        keep = jnp.sum(
            jnp.where(rows_of(shape) % ch_dev == lanes_of(shape), quality_ref[...].astype(jnp.float32), 0.0),
            axis=1, keepdims=True,
        )
        keep_ref[...] = jnp.broadcast_to(keep, keep_ref.shape)

    early, late = traces_ref[:, : length // 2], traces_ref[:, length // 2 :]
    even = jnp.dot(early + late, table_ref[:, :F], preferred_element_type=jnp.float32)
    odd = jnp.dot(early - late, table_ref[:, F:], preferred_element_type=jnp.float32)
    part = H // 2
    parts = [
        jnp.concatenate([even[:, q * part : (q + 1) * part], odd[:, q * part : (q + 1) * part]], axis=1)
        for q in range(4)
    ]
    energy = jnp.concatenate(
        [parts[0] * parts[0] + parts[1] * parts[1], parts[2] * parts[2] + parts[3] * parts[3]], axis=1
    )
    top = energy.astype(jnp.bfloat16)
    rest = (energy - top.astype(jnp.float32)).astype(jnp.bfloat16)
    band = band_ref[...]
    smooth = jnp.dot(top, band, preferred_element_type=jnp.float32) + jnp.dot(
        rest, band, preferred_element_type=jnp.float32
    )
    water = jnp.sum(energy, axis=1, keepdims=True) * (1.0 / F)
    scaling = lax.rsqrt(smooth * (1.0 / (2.0 * smooth_reach + 1.0)) + (0.1 * water + 1e-06))
    keep = keep_ref[...]
    near, far = scaling[:, :H] * keep, scaling[:, H:] * keep
    white = [parts[0] * near, parts[1] * near, parts[2] * far, parts[3] * far]
    for q in range(4):
        whitened_ref[:, q * H : (q + 1) * H] = white[q].astype(jnp.bfloat16)


def select_kernel(where_ref, whitened_ref, owners_ref, places_ref, outgoing_ref, selector):
    rows = selector.shape[1]

    @pl.when(pl.program_id(0) == 0)
    def _():
        selector[...] = slot_selector(owners_ref[...], places_ref[...], where_ref[0], rows // 2)

    count, slots, columns = outgoing_ref.shape
    for n in range(slots // (2 * CAP)):
        sent = jnp.dot(
            selector[...], whitened_ref[rows * n : rows * (n + 1), :], preferred_element_type=jnp.float32
        ).astype(jnp.bfloat16)
        outgoing_ref[:, 2 * CAP * n : 2 * CAP * (n + 1), :] = sent.reshape(count, 2 * CAP, columns)


def vmem_spec():
    return pl.BlockSpec(memory_space=pltpu.VMEM)


def smem_spec():
    return pl.BlockSpec(memory_space=pltpu.SMEM)


def whole(array):
    return pl.BlockSpec(array.shape, lambda s: (0,) * array.ndim)


def spectra_call(traces, quality):
    rows, length = traces.shape
    block = rows // ROW_STEPS
    table = jnp.asarray(forward_table(length))
    return pl.pallas_call(
        spectra_kernel,
        grid=(ROW_STEPS,),
        in_specs=[pl.BlockSpec((block, length), lambda s: (s, 0)), whole(table), whole(quality)],
        out_specs=pl.BlockSpec((block, 2 * F), lambda s: (s, 0)),
        out_shape=jax.ShapeDtypeStruct((rows, 2 * F), jnp.bfloat16),
        scratch_shapes=[pltpu.VMEM((F, F), jnp.bfloat16), pltpu.VMEM((block, H), jnp.float32)],
        compiler_params=pltpu.CompilerParams(vmem_limit_bytes=SPECTRA_VMEM_LIMIT),
        cost_estimate=pl.CostEstimate(
            flops=rows * length * 2 * F, bytes_accessed=2 * (rows + F) * length, transcendentals=rows * F
        ),
        name="spectra",
    )(traces, table, quality)


def select_call(where, whitened, owners, places, chan_count, ch_dev):
    rows, columns = whitened.shape
    block = rows // ROW_STEPS
    slots = block // (2 * ch_dev) * 2 * CAP
    return pl.pallas_call(
        select_kernel,
        grid=(ROW_STEPS,),
        in_specs=[smem_spec(), pl.BlockSpec((block, columns), lambda s: (s, 0)), whole(owners), whole(places)],
        out_specs=pl.BlockSpec((chan_count, slots, columns), lambda s: (0, s, 0)),
        out_shape=jax.ShapeDtypeStruct((chan_count, ROW_STEPS * slots, columns), jnp.bfloat16),
        scratch_shapes=[pltpu.VMEM((chan_count * 2 * CAP, 2 * ch_dev), jnp.bfloat16)],
        compiler_params=pltpu.CompilerParams(vmem_limit_bytes=VMEM_LIMIT),
        cost_estimate=pl.CostEstimate(
            flops=4 * rows * chan_count * 2 * CAP * columns, bytes_accessed=2 * rows * columns * 3, transcendentals=0
        ),
        name="select",
    )(where, whitened, owners, places)


def cross_kernel(last, with_sum, local_windows, where_ref, first_ref, second_ref, *refs):
    refs = list(refs)
    sum_ref = refs.pop(0) if with_sum else None
    if last:
        high_ref, low_ref, out_ref, wide, spread, total = refs
    else:
        out_ref, wide, spread = refs
        total = out_ref
    windows, own_count = spread.shape[:2]
    ch_dev = wide.shape[1] // 2
    base = pl.multiple_of(where_ref[1] * own_count, 8)

    def widen(w, carry):
        if local_windows:
            wide[w, :ch_dev, :] = first_ref[w].astype(jnp.float32)
            wide[w, ch_dev:, :] = second_ref[w].astype(jnp.float32)
        else:
            shared = ch_dev - own_count
            wide[w, shared:ch_dev, :] = first_ref[w].astype(jnp.float32)
            rows = second_ref[w].astype(jnp.float32)
            for tile in range(ch_dev // 8):
                at = base + 8 * tile
                at = pl.multiple_of(jnp.where(at < shared, at, at + own_count), 8)
                wide[w, pl.ds(at, 8), :] = rows[8 * tile : 8 * tile + 8]
        for tile in range(own_count // 8):
            rows = wide[w, pl.ds(pl.multiple_of(base + 8 * tile, 8), 8), :]
            for i in range(8):
                for q in range(4):
                    spread[w, 8 * tile + i, q] = jnp.broadcast_to(rows[i : i + 1, q * H : (q + 1) * H], (8, H))
        return carry

    lax.fori_loop(0, windows, widen, 0)

    group, tiles = 4, 3
    rounds = SPAN // (8 * tiles)

    def block(index, carry):
        g = index // rounds
        j = index % rounds
        start = pl.multiple_of(base + 8 * (g // 2) + 8 * tiles * j, 8)

        def add_window(w, sums):
            sums = list(sums)
            right = [
                [wide[w, pl.ds(pl.multiple_of(start + 8 * t, 8), 8), q * H : (q + 1) * H] for q in range(4)]
                for t in range(tiles)
            ]
            for i in range(group):
                left = [spread[w, group * g + i, q] for q in range(4)]
                for t in range(tiles):
                    at = 3 * (i * tiles + t)
                    r = right[t]
                    sums[at] = sums[at] + (left[0] * r[0] + left[1] * r[1])
                    sums[at + 1] = sums[at + 1] + (left[2] * r[2] + left[3] * r[3])
                    sums[at + 2] = sums[at + 2] + ((left[1] * r[0] - left[0] * r[1]) + (left[2] * r[3] - left[3] * r[2]))
            return tuple(sums)

        zero = jnp.zeros((8, H), jnp.float32)
        sums = lax.fori_loop(0, windows, add_window, (zero,) * (3 * group * tiles), unroll=2)
        for i in range(group):
            for t in range(tiles):
                at = 3 * (i * tiles + t)
                real, imag = fold_columns(sums[at], sums[at + 1], sums[at + 2])
                where = pl.ds(pl.multiple_of(8 * tiles * j + 8 * t, 8), 8)
                if with_sum:
                    real = real + sum_ref[group * g + i, where, :H]
                    imag = imag + sum_ref[group * g + i, where, H:]
                total[group * g + i, where, :H] = real
                total[group * g + i, where, H:] = imag
        return carry

    lax.fori_loop(0, own_count // group * rounds, block, 0)

    if last:

        def finish(eight, carry):
            first = pl.multiple_of(8 * eight, 8)
            stacks = total[pl.ds(first, 8)].reshape(8 * SPAN, F)
            lagged = lag_transform(stacks, high_ref[...], low_ref[...]).reshape(8, SPAN, NLAG)
            for i in range(8):
                out_ref[first + i] = lagged[i, i + 1 : i + 1 + REACH, :]
            return carry

        lax.fori_loop(0, own_count // 8, finish, 0)


def cross_call(where, first, second, ch_dev, own_count, sums, tables, local_windows):
    windows, _, columns = first.shape
    last = tables is not None
    with_sum = sums is not None
    operands = [where, first, second]
    if with_sum:
        operands.append(sums)
    scratch = [
        pltpu.VMEM((windows, 2 * ch_dev, columns), jnp.float32),
        pltpu.VMEM((windows, own_count, 4, 8, H), jnp.float32),
    ]
    if last:
        operands += list(tables)
        scratch.append(pltpu.VMEM((own_count, SPAN, F), jnp.float32))
    shape = (own_count, REACH, NLAG) if last else (own_count, SPAN, F)
    return pl.pallas_call(
        functools.partial(cross_kernel, last, with_sum, local_windows),
        in_specs=[smem_spec()] + [vmem_spec()] * (len(operands) - 1),
        out_specs=vmem_spec(),
        out_shape=jax.ShapeDtypeStruct(shape, jnp.float32),
        scratch_shapes=scratch,
        compiler_params=pltpu.CompilerParams(vmem_limit_bytes=VMEM_LIMIT),
        cost_estimate=pl.CostEstimate(
            flops=10_000_000_000, bytes_accessed=4 * windows * ch_dev * columns + 4 * own_count * SPAN * F, transcendentals=0
        ),
        name="cross",
    )(*operands)


def fold_kernel(where_ref, incoming_ref, own_ref, owners_ref, high_ref, low_ref, out_ref, sums, picker):
    step = pl.program_id(0)
    rows = own_ref.shape[0]
    ch_dev = rows // 2

    @pl.when(step == 0)
    def _():
        sums[...] = jnp.zeros_like(sums)
        owners = owners_ref[...].astype(jnp.float32)
        per_row = owners.shape[1] // ch_dev
        device = where_ref[0]
        line = jnp.sum(jnp.where(rows_of(owners.shape) == device // per_row, owners, 0.0), axis=0, keepdims=True)
        shape = (rows, owners.shape[1])
        line = jnp.broadcast_to(line, shape)
        first = device % per_row * ch_dev
        place = first + rows_of(shape) % ch_dev
        lane = lanes_of(shape)
        owner = jnp.sum(jnp.where(lane == place, line, 0.0), axis=1, keepdims=True)
        earlier = (lane >= first) & (lane < place) & (line == owner)
        rank = jnp.sum(earlier.astype(jnp.float32), axis=1, keepdims=True)
        source = (2 * CAP * owner + rank).astype(jnp.int32)
        shape = picker.shape
        target = source + CAP * (rows_of(shape) // ch_dev)
        picker[...] = (lanes_of(shape) == target).astype(jnp.float32).astype(jnp.bfloat16)

    count, slots, columns = incoming_ref.shape
    right = jnp.dot(
        picker[...], incoming_ref[...].reshape(count * slots, columns), preferred_element_type=jnp.float32
    )
    left = own_ref[...].astype(jnp.float32)
    l = [left[:, q * H : (q + 1) * H] for q in range(4)]
    r = [right[:, q * H : (q + 1) * H] for q in range(4)]
    first = l[0] * r[0] + l[1] * r[1]
    second = l[2] * r[2] + l[3] * r[3]
    imag = (l[1] * r[0] - l[0] * r[1]) + (l[2] * r[3] - l[3] * r[2])
    for n, term in enumerate((first, second, imag)):
        sums[n] += term[:ch_dev] + term[ch_dev:]

    @pl.when(step == pl.num_programs(0) - 1)
    def _():
        stacks = jnp.concatenate(fold_columns(sums[0], sums[1], sums[2]), axis=1)
        out_ref[...] = lag_transform(stacks, high_ref[...], low_ref[...])


def fold_call(where, incoming, own, owners, ch_dev, tables):
    count, slots, columns = incoming.shape
    rows = 2 * ch_dev
    pairs = own.shape[0] // rows
    return pl.pallas_call(
        fold_kernel,
        grid=(pairs,),
        in_specs=[
            smem_spec(),
            pl.BlockSpec((count, slots // pairs, columns), lambda s: (0, s, 0)),
            pl.BlockSpec((rows, columns), lambda s: (s, 0)),
            whole(owners),
            whole(tables[0]),
            whole(tables[1]),
        ],
        out_specs=pl.BlockSpec((ch_dev, NLAG), lambda s: (0, 0)),
        out_shape=jax.ShapeDtypeStruct((ch_dev, NLAG), jnp.float32),
        scratch_shapes=[
            pltpu.VMEM((3, ch_dev, H), jnp.float32),
            pltpu.VMEM((rows, count * slots // pairs), jnp.bfloat16),
        ],
        compiler_params=pltpu.CompilerParams(vmem_limit_bytes=VMEM_LIMIT),
        cost_estimate=pl.CostEstimate(
            flops=2 * rows * pairs * count * 2 * CAP * columns,
            bytes_accessed=2 * (incoming.size + own.size),
            transcendentals=0,
        ),
        name="fold",
    )(where, incoming, own, owners, *tables)


def from_above(block):
    count = lax.axis_size("chan")
    return lax.ppermute(block, "chan", [(i, i - 1) for i in range(1, count)])


def round_win(block, shift):
    count = lax.axis_size("win")
    return lax.ppermute(block, "win", [(i, (i + shift) % count) for i in range(count)])


def local(traces, quality, fold_block, fold_offset):
    win_dev, ch_dev, length = traces.shape
    chan_count = lax.axis_size("chan")
    win_count = lax.axis_size("win")
    window_part = lax.axis_index("win")
    own_count = ch_dev // win_count
    shared = ch_dev - own_count
    where = jnp.stack([lax.axis_index("chan"), window_part]).astype(jnp.int32)
    tables = [jnp.asarray(t) for t in inverse_tables(1.0 / math.sqrt(F * win_dev * win_count))]
    owners = fold_block.reshape(-1, 2 * ch_dev)
    places = fold_offset.reshape(-1, 2 * ch_dev)
    flat = spectra_call(traces.reshape(win_dev * ch_dev, length), quality.reshape(1, ch_dev))
    whitened = flat.reshape(win_dev, ch_dev, 2 * F)
    upper = from_above(whitened)
    common = [round_win(whitened[:, shared:], shift) for shift in range(1, win_count)]
    outgoing = select_call(where, flat, owners, places, chan_count, ch_dev)
    incoming = lax.all_to_all(outgoing, "chan", split_axis=0, concat_axis=0, tiled=True)
    offered = jnp.concatenate([whitened[:, :shared], upper], axis=1)
    special = [
        round_win(
            lax.dynamic_slice_in_dim(offered, (window_part + shift) % win_count * own_count, ch_dev, 1), shift
        )
        for shift in range(1, win_count)
    ]
    arrived = [(whitened, upper)] + list(zip(common, special))
    sums = None
    for n, (first, second) in enumerate(arrived):
        ends = tables if n == win_count - 1 else None
        sums = cross_call(where, first, second, ch_dev, own_count, sums, ends, n == 0)
    share = fold_call(where, incoming, flat, owners, ch_dev, tables)
    fold = lax.dynamic_slice_in_dim(share, window_part * own_count, own_count, 0)
    for shift in range(1, win_count):
        target = (window_part + shift) % win_count * own_count
        fold = fold + round_win(lax.dynamic_slice_in_dim(share, target, own_count, 0), shift)
    return (sums, fold)


def solution(mesh):
    in_specs = (P("win", "chan", None), P("chan"), P(), P())
    out_specs = (P(("chan", "win"), None, None), P(("chan", "win"), None))
    return jax.shard_map(local, mesh=mesh, in_specs=in_specs, out_specs=out_specs, check_vma=False)
```

profile of v0, /device:TPU:13, one launch (start us, length us, event | category | flops | bytes accessed | tf_op | source)
XLA Modules:
  0.0 96.1 jit_solution(7940182975485502424)
XLA Ops:
  0.6 0.1 pad_add_fusion.where_ref
  0.7 0.0 copy-start.5
  0.7 0.0 copy-start.6
  0.7 7.0 %spectra.1.whitened_ref.own_ref = bf16[768,512]{1,0:T(8,128)(2,1)} custom-call(bf16[768,4096]{1,0:T(8,128)(2,1)} %bitcast.13, bf16[2048,512]{1,0:T(8,128)(2,1)} %constant.39.clone.table_ref, s32[1,64]{1,0:T(1,128)} %bitcast.14), custom_call_target="tpu_custom_call" | custom-call | flops 1610612736 | bytes 8388608 | tf_op jit(solution)/shard_map/spectra/pallas_call | solution.py:191
  7.7 0.0 copy-done.5
  7.7 0.0 copy-done.6
  7.7 0.0 copy-start
  7.7 1.1 %copy-done = bf16[768,512]{1,0:T(8,128)(2,1)S(1)} copy-done((bf16[768,512]{1,0:T(8,128)(2,1)S(1)}, bf16[768,512]{1,0:T(8,128)(2,1)}, u32[]{:S(2)}) %copy-start) | copy-done | bytes 786456
  8.8 1.9 %select.3 = bf16[16,96,512]{2,1,0:T(8,128)(2,1)S(1)} custom-call(s32[2]{0:T(128)S(1)} %pad_add_fusion.where_ref, bf16[768,512]{1,0:T(8,128)(2,1)S(1)} %copy-done, s32[8,128]{1,0:T(8,128)S(1)} %bitcast.10, s32[8,128]{1,0:T(8,128)S(1)} %bitcast.12), custom_call_target="tpu_custom_call" | custom-call | flops 402653184 | bytes 2359296 | tf_op jit(solution)/shard_map/select/pallas_call | solution.py:210
  10.7 0.0 copy-start.2
  10.7 1.1 %copy-done.2 = bf16[16,96,512]{2,1,0:T(8,128)(2,1)} copy-done((bf16[16,96,512]{2,1,0:T(8,128)(2,1)}, bf16[16,96,512]{2,1,0:T(8,128)(2,1)S(1)}, u32[]{:S(2)}) %copy-start.2) | copy-done | bytes 1572888
  11.8 0.0 copy-start.1
  11.8 6.7 %all-to-all-start = ((bf16[16,96,512]{2,1,0:T(8,128)(2,1)}), bf16[16,96,512]{2,1,0:T(8,128)(2,1)S(1)}, u32[]{:S(2)}, u32[]{:S(2)}) async-start(bf16[16,96,512]{2,1,0:T(8,128)(2,1)} %copy-done.2), calls=%async_computation | async-start | bytes 3145728 | tf_op jit(solution)/shard_map/all_to_all | solution.py:441
  18.5 0.0 copy-done.1
  18.5 2.3 %collective-permute-start.1 = (bf16[12,64,512]{2,1,0:T(8,128)(2,1)S(1)}, bf16[12,64,512]{2,1,0:T(8,128)(2,1)S(1)}, u32[]{:S(2)}, u32[]{:S(2)}) collective-permute-start(bf16[12,64,512]{2,1,0:T(8,128)(2,1)S(1)} %bitcast.7), channel_id=1, source_target_pairs={{2,0},{4,2},{6,4},{8,6},{10,8},{12,10},{14,12},{16,14},{18,16},{20... | collective-permute-start | bytes 2359304 | tf_op jit(solution)/shard_map/ppermute | solution.py:417
  20.8 0.8 fusion.1
  21.6 1.2 %collective-permute-start = (bf16[12,32,512]{2,1,0:T(8,128)(2,1)}, bf16[12,32,512]{2,1,0:T(8,128)(2,1)}, u32[]{:S(2)}, u32[]{:S(2)}) collective-permute-start(bf16[12,32,512]{2,1,0:T(8,128)(2,1)} %get-tuple-element.3), channel_id=1, source_target_pairs={{0,1},{1,0},{2,3},{3,2},{4,5},{5,4},{6,7},{7,6},{8,9},{9,8},{10,11... | collective-permute-start | bytes 1179656 | tf_op jit(solution)/shard_map/ppermute | solution.py:422
  22.8 40.3 %collective-permute-done.1.second_ref = bf16[12,64,512]{2,1,0:T(8,128)(2,1)S(1)} collective-permute-done((bf16[12,64,512]{2,1,0:T(8,128)(2,1)S(1)}, bf16[12,64,512]{2,1,0:T(8,128)(2,1)S(1)}, u32[]{:S(2)}, u32[]{:S(2)}) %collective-permute-start.1) | collective-permute-done | bytes 786464 | tf_op jit(solution)/shard_map/ppermute | solution.py:417
  63.1 1.1 %fusion = bf16[12,64,512]{2,1,0:T(8,128)(2,1)} fusion(s32[]{:T(128)S(6)} %select_n.19, bf16[12,32,512]{2,1,0:T(8,128)(2,1)S(1)} %get-tuple-element.2, bf16[12,64,512]{2,1,0:T(8,128)(2,1)S(1)} %collective-permute-done.1.second_ref), kind=kLoop, calls=%fused_computation.2 | loop fusion | flops 1572864 | bytes 1966084 | tf_op jit(solution)/shard_map/concatenate | solution.py:442
  64.2 0.0 copy-start.3
  64.2 0.0 copy-start.4
  64.3 1.2 %collective-permute-start.2 = (bf16[12,64,512]{2,1,0:T(8,128)(2,1)}, bf16[12,64,512]{2,1,0:T(8,128)(2,1)}, u32[]{:S(2)}, u32[]{:S(2)}) collective-permute-start(bf16[12,64,512]{2,1,0:T(8,128)(2,1)} %fusion), channel_id=1, source_target_pairs={{0,1},{1,0},{2,3},{3,2},{4,5},{5,4},{6,7},{7,6},{8,9},{9,8},{10,11... | collective-permute-start | bytes 2359304 | tf_op jit(solution)/shard_map/ppermute | solution.py:422
  65.5 11.0 %cross.2.refs_0_ = f32[32,72,256]{2,1,0:T(8,128)S(1)} custom-call(s32[2]{0:T(128)S(1)} %pad_add_fusion.where_ref, bf16[12,64,512]{2,1,0:T(8,128)(2,1)S(1)} %bitcast.9, bf16[12,64,512]{2,1,0:T(8,128)(2,1)S(1)} %collective-permute-done.1.second_ref), custom_call_target="tpu_custom_call" | custom-call | flops 10000000000 | bytes 3932160 | tf_op jit(solution)/shard_map/cross/pallas_call | solution.py:326
  76.5 0.0 copy-start.7
  76.5 1.4 %copy-done.7 = f32[32,72,256]{2,1,0:T(8,128)} copy-done((f32[32,72,256]{2,1,0:T(8,128)}, f32[32,72,256]{2,1,0:T(8,128)S(1)}, u32[]{:S(2)}) %copy-start.7) | copy-done | bytes 2359320
  77.9 0.0 all-to-all-done.incoming_ref
  77.9 0.0 copy-done.3
  77.9 0.0 copy-done.4
  77.9 0.0 copy-start.8
  77.9 2.4 %fold.1 = f32[64,256]{1,0:T(8,128)S(1)} custom-call(s32[2]{0:T(128)S(1)} %pad_add_fusion.where_ref, bf16[16,96,512]{2,1,0:T(8,128)(2,1)S(1)} %all-to-all-done.incoming_ref, bf16[768,512]{1,0:T(8,128)(2,1)S(1)} %copy-done.1, s32[8,128]{1,0:T(8,128)S(1)} %bitcast.11, bf16[256,256]{1,0:T(8,128)(2,1)S(1)} %copy-done.4, bf16[256,256]{1,0:T(8,128)(2,1)S(1)} %copy-done.3), custom_call_target="tpu_custom_call" | custom-call | flops 201326592 | bytes 2359296 | tf_op jit(solution)/shard_map/fold/pallas_call | solution.py:388
  80.4 0.3 collective-permute-start.3
  80.7 0.0 collective-permute-done.first_ref
  80.7 0.0 collective-permute-done.2.second_ref
  80.7 0.0 copy-done.8
  80.7 14.8 %cross.3 = f32[32,64,256]{2,1,0:T(8,128)} custom-call(s32[2]{0:T(128)S(1)} %pad_add_fusion.where_ref, bf16[12,32,512]{2,1,0:T(8,128)(2,1)} %collective-permute-done.first_ref, bf16[12,64,512]{2,1,0:T(8,128)(2,1)} %collective-permute-done.2.second_ref, f32[32,72,256]{2,1,0:T(8,128)S(1)} %copy-done.8, bf16[256,256]{1,0:T(8,128)(2,1)S(1)} %copy-done.4, ...), custom_call_target="tpu_custom_call" | custom-call | flops 10000000000 | bytes 3932160 | tf_op jit(solution)/shard_map/cross/pallas_call | solution.py:326
  95.5 0.0 collective-permute-done.3
  95.5 0.6 dynamic-slice_add_fusion
  (1 shorter events, 0.0 us)
Async XLA Ops:
  0.7 7.0 %copy-start.5 = (s32[1024,1]{0,1:T(1,128)S(1)}, s32[1024,1]{0,1:T(1,128)}, u32[]{:S(2)}) copy-start(s32[1024,1]{0,1:T(1,128)} %param.9) | copy-start | bytes 12292
  0.7 7.0 %copy-start.6 = (s32[1024]{0:T(1024)S(1)}, s32[1024]{0:T(1024)}, u32[]{:S(2)}) copy-start(s32[1024]{0:T(1024)} %param.10) | copy-start | bytes 12292
  7.7 1.1 %copy-start = (bf16[768,512]{1,0:T(8,128)(2,1)S(1)}, bf16[768,512]{1,0:T(8,128)(2,1)}, u32[]{:S(2)}) copy-start(bf16[768,512]{1,0:T(8,128)(2,1)} %spectra.1.whitened_ref.own_ref) | copy-start | bytes 2359300
  10.7 1.1 %copy-start.2 = (bf16[16,96,512]{2,1,0:T(8,128)(2,1)}, bf16[16,96,512]{2,1,0:T(8,128)(2,1)S(1)}, u32[]{:S(2)}) copy-start(bf16[16,96,512]{2,1,0:T(8,128)(2,1)S(1)} %select.3) | copy-start | bytes 4718596
  11.8 6.7 %copy-start.1 = (bf16[768,512]{1,0:T(8,128)(2,1)S(1)}, bf16[768,512]{1,0:T(8,128)(2,1)}, u32[]{:S(2)}) copy-start(bf16[768,512]{1,0:T(8,128)(2,1)} %spectra.1.whitened_ref.own_ref) | copy-start | bytes 2359300
  11.8 66.1 %all-to-all-start = ((bf16[16,96,512]{2,1,0:T(8,128)(2,1)}), bf16[16,96,512]{2,1,0:T(8,128)(2,1)S(1)}, u32[]{:S(2)}, u32[]{:S(2)}) async-start(bf16[16,96,512]{2,1,0:T(8,128)(2,1)} %copy-done.2), calls=%async_computation | async-start | bytes 3145728 | tf_op jit(solution)/shard_map/all_to_all | solution.py:441
  18.5 44.6 %collective-permute-start.1 = (bf16[12,64,512]{2,1,0:T(8,128)(2,1)S(1)}, bf16[12,64,512]{2,1,0:T(8,128)(2,1)S(1)}, u32[]{:S(2)}, u32[]{:S(2)}) collective-permute-start(bf16[12,64,512]{2,1,0:T(8,128)(2,1)S(1)} %bitcast.7), channel_id=1, source_target_pairs={{2,0},{4,2},{6,4},{8,6},{10,8},{12,10},{14,12},{16,14},{18,16},{20... | collective-permute-start | bytes 2359304 | tf_op jit(solution)/shard_map/ppermute | solution.py:417
  21.6 59.0 %collective-permute-start = (bf16[12,32,512]{2,1,0:T(8,128)(2,1)}, bf16[12,32,512]{2,1,0:T(8,128)(2,1)}, u32[]{:S(2)}, u32[]{:S(2)}) collective-permute-start(bf16[12,32,512]{2,1,0:T(8,128)(2,1)} %get-tuple-element.3), channel_id=1, source_target_pairs={{0,1},{1,0},{2,3},{3,2},{4,5},{5,4},{6,7},{7,6},{8,9},{9,8},{10,11... | collective-permute-start | bytes 1179656 | tf_op jit(solution)/shard_map/ppermute | solution.py:422
  64.2 13.7 %copy-start.3 = (bf16[256,256]{1,0:T(8,128)(2,1)S(1)}, bf16[256,256]{1,0:T(8,128)(2,1)}, u32[]{:S(2)}) copy-start(bf16[256,256]{1,0:T(8,128)(2,1)} %constant.38.clone.refs_2_.low_ref) | copy-start | bytes 393220
  64.2 13.7 %copy-start.4 = (bf16[256,256]{1,0:T(8,128)(2,1)S(1)}, bf16[256,256]{1,0:T(8,128)(2,1)}, u32[]{:S(2)}) copy-start(bf16[256,256]{1,0:T(8,128)(2,1)} %constant.37.clone.refs_1_.high_ref) | copy-start | bytes 393220
  64.3 16.4 %collective-permute-start.2 = (bf16[12,64,512]{2,1,0:T(8,128)(2,1)}, bf16[12,64,512]{2,1,0:T(8,128)(2,1)}, u32[]{:S(2)}, u32[]{:S(2)}) collective-permute-start(bf16[12,64,512]{2,1,0:T(8,128)(2,1)} %fusion), channel_id=1, source_target_pairs={{0,1},{1,0},{2,3},{3,2},{4,5},{5,4},{6,7},{7,6},{8,9},{9,8},{10,11... | collective-permute-start | bytes 2359304 | tf_op jit(solution)/shard_map/ppermute | solution.py:422
  76.5 1.4 %copy-start.7 = (f32[32,72,256]{2,1,0:T(8,128)}, f32[32,72,256]{2,1,0:T(8,128)S(1)}, u32[]{:S(2)}) copy-start(f32[32,72,256]{2,1,0:T(8,128)S(1)} %cross.2.refs_0_) | copy-start | bytes 7077892
  77.9 2.8 %copy-start.8 = (f32[32,72,256]{2,1,0:T(8,128)S(1)}, f32[32,72,256]{2,1,0:T(8,128)}, u32[]{:S(2)}) copy-start(f32[32,72,256]{2,1,0:T(8,128)} %copy-done.7) | copy-start | bytes 7077892
  80.4 15.1 %collective-permute-start.3 = (f32[32,256]{1,0:T(8,128)S(1)}, f32[32,256]{1,0:T(8,128)S(1)}, u32[]{:S(2)}, u32[]{:S(2)}) collective-permute-start(f32[32,256]{1,0:T(8,128)S(1)} %constant_dynamic-slice_fusion), channel_id=1, source_target_pairs={{0,1},{1,0},{2,3},{3,2},{4,5},{5,4},{6,7},{7,6},{8,9},{9,8},{10,11... | collective-permute-start | bytes 98312 | tf_op jit(solution)/shard_map/ppermute | solution.py:422
where the time goes:
time: 96.4 us; the launch traced here: 96.1 us
  waiting for transfers between devices  40.3 us (42%)
  Pallas kernels  37.1 us (38%)
  starting transfers between devices  11.7 us (12%)
  local copies, waits for them, and re-layouts  4.54 us (5%)
  other arithmetic  1.8 us (2%)
    ppermute x1, waiting for transfers between devices, from_above(): return lax.ppermute(block, 'chan', [(i, i - 1) for i in range(1, count)])  40.3 us
    pallas_call x2, Pallas kernels, cross_call(): pl.pallas_call(functools.partial(cross_kernel, last, with_sum, local_wind...  25.8 us
    pallas_call x1, Pallas kernels, spectra_call(): pl.pallas_call(spectra_kernel, grid=(ROW_STEPS,), in_specs=[pl.BlockSpec(...  6.97 us
    all_to_all x1, starting transfers between devices, local(): lax.all_to_all(outgoing, 'chan', split_axis=0, concat_axis=0, tiled=True)  6.69 us
    unnamed x18, local copies, waits for them, and re-layouts  3.71 us
    ppermute x3, starting transfers between devices, round_win(): lax.ppermute(block, 'win', [(i, (i + shift) % count) for i in range(count)])  2.74 us
    pallas_call x1, Pallas kernels, fold_call(): pl.pallas_call(fold_kernel, grid=(pairs,), in_specs=[smem_spec(), pl.Bloc...  2.4 us
    ppermute x1, starting transfers between devices, from_above(): return lax.ppermute(block, 'chan', [(i, i - 1) for i in range(1, count)])  2.27 us
  transfers between devices with their start and end apart: 5, of which 1 were waited for; matrix products, arithmetic and copies ran while one was open for 2% of the time, Pallas kernels for 29%

commit v1 on v0

--- a/solution.py
+++ b/solution.py
@@ -18,16 +18,14 @@
 SPAN = REACH + 8
 smooth_reach = 4
 ROW_STEPS = 3
-VMEM_LIMIT = 32 * 1024 * 1024
-SPECTRA_VMEM_LIMIT = 56 * 1024 * 1024
-
-
-def lane_residues():
-    return np.concatenate([np.arange(0, H, 2), np.arange(1, H, 2)])
+K_STEPS = 4
+VMEM_LIMIT = 24 * 1024 * 1024
+FOLD_VMEM_LIMIT = 16 * 1024 * 1024
+SPECTRA_VMEM_LIMIT = 48 * 1024 * 1024
 
 
 def bin_order():
-    residues = lane_residues()
+    residues = np.arange(H)
     first = (residues - BAND_LO) % F
     second = (-residues - BAND_LO) % F
     second[0] = (H - BAND_LO) % F
@@ -35,19 +33,17 @@
 
 
 def forward_table(length):
-    samples = np.arange(length // 2, dtype=np.int64)[:, None]
+    samples = np.arange(length, dtype=np.int64)[:, None]
     parts = []
-    for parity in range(2):
-        for bins in bin_order():
-            bins = bins[parity * H // 2 : (parity + 1) * H // 2]
-            angles = (samples * (bins + BAND_LO)[None, :] % length) * (2.0 * math.pi / length)
-            parts += [np.cos(angles), -np.sin(angles)]
+    for bins in bin_order():
+        angles = (samples * (bins + BAND_LO)[None, :] % length) * (2.0 * math.pi / length)
+        parts += [np.cos(angles), -np.sin(angles)]
     return np.concatenate(parts, axis=1).astype(np.float32).astype(jnp.bfloat16)
 
 
 def inverse_tables(factor):
     shifts = (np.arange(NLAG) + NLAG // 2)[None, :]
-    residues = lane_residues()[:, None]
+    residues = np.arange(H)[:, None]
     angles = (residues * shifts % NLAG) * (2.0 * math.pi / NLAG)
     sign = np.where(shifts[0] % 2 == 0, 1.0, -1.0)
     real, imag = np.cos(angles), -np.sin(angles)
@@ -82,8 +78,7 @@
 def band_matrix():
     def bins(index):
         lane = index & (H - 1)
-        residue = jnp.where(lane < H // 2, 2 * lane, 2 * lane - H + 1)
-        residue = jnp.where(index < H, residue, jnp.where(lane == 0, H, F - residue))
+        residue = jnp.where(index < H, lane, jnp.where(lane == 0, H, F - lane))
         return (residue - BAND_LO + F) & (F - 1)
 
     apart = bins(rows_of((F, F))) - bins(lanes_of((F, F)))
@@ -117,44 +112,60 @@
     return ((lane == place + ch_dev * half) & (place >= 0)).astype(jnp.float32).astype(jnp.bfloat16)
 
 
-def spectra_kernel(traces_ref, table_ref, quality_ref, whitened_ref, band_ref, keep_ref):
-    rows, length = traces_ref.shape
+def spectra_kernel(traces_ref, table_ref, quality_ref, whitened_ref, traces, table, sems):
+    row_parts, chunks, rows, depth = traces.shape
     ch_dev = quality_ref.shape[1]
 
-    @pl.when(pl.program_id(0) == 0)
-    def _():
-        band_ref[...] = band_matrix()
-        shape = (rows, ch_dev)
-        keep = jnp.sum(
-            jnp.where(rows_of(shape) % ch_dev == lanes_of(shape), quality_ref[...].astype(jnp.float32), 0.0),
-            axis=1, keepdims=True,
+    def traces_copy(part, k):
+        source = traces_ref.at[pl.ds(part * rows, rows), pl.ds(k * depth, depth)]
+        return pltpu.make_async_copy(source, traces.at[part, k], sems.at[part, k])
+
+    def table_copy(k):
+        return pltpu.make_async_copy(table_ref.at[pl.ds(k * depth, depth), :], table.at[k], sems.at[row_parts, k])
+
+    for part in range(row_parts):
+        for k in range(chunks):
+            traces_copy(part, k).start()
+            if part == 0:
+                table_copy(k).start()
+
+    band = band_matrix()
+    shape = (rows, ch_dev)
+    keep = jnp.sum(
+        jnp.where(rows_of(shape) % ch_dev == lanes_of(shape), quality_ref[...].astype(jnp.float32), 0.0),
+        axis=1, keepdims=True,
+    )
+
+    def whiten(part, carry):
+        spectra = None
+        for k in range(chunks):
+            traces_copy(part, k).wait()
+
+            @pl.when(part == 0)
+            def _():
+                table_copy(k).wait()
+
+            product = jnp.dot(traces[part, k], table[k], preferred_element_type=jnp.float32)
+            spectra = product if spectra is None else spectra + product
+        parts = [spectra[:, q * H : (q + 1) * H] for q in range(4)]
+        energy = jnp.concatenate(
+            [parts[0] * parts[0] + parts[1] * parts[1], parts[2] * parts[2] + parts[3] * parts[3]], axis=1
         )
-        keep_ref[...] = jnp.broadcast_to(keep, keep_ref.shape)
-
-    early, late = traces_ref[:, : length // 2], traces_ref[:, length // 2 :]
-    even = jnp.dot(early + late, table_ref[:, :F], preferred_element_type=jnp.float32)
-    odd = jnp.dot(early - late, table_ref[:, F:], preferred_element_type=jnp.float32)
-    part = H // 2
-    parts = [
-        jnp.concatenate([even[:, q * part : (q + 1) * part], odd[:, q * part : (q + 1) * part]], axis=1)
-        for q in range(4)
-    ]
-    energy = jnp.concatenate(
-        [parts[0] * parts[0] + parts[1] * parts[1], parts[2] * parts[2] + parts[3] * parts[3]], axis=1
-    )
-    top = energy.astype(jnp.bfloat16)
-    rest = (energy - top.astype(jnp.float32)).astype(jnp.bfloat16)
-    band = band_ref[...]
-    smooth = jnp.dot(top, band, preferred_element_type=jnp.float32) + jnp.dot(
-        rest, band, preferred_element_type=jnp.float32
-    )
-    water = jnp.sum(energy, axis=1, keepdims=True) * (1.0 / F)
-    scaling = lax.rsqrt(smooth * (1.0 / (2.0 * smooth_reach + 1.0)) + (0.1 * water + 1e-06))
-    keep = keep_ref[...]
-    near, far = scaling[:, :H] * keep, scaling[:, H:] * keep
-    white = [parts[0] * near, parts[1] * near, parts[2] * far, parts[3] * far]
-    for q in range(4):
-        whitened_ref[:, q * H : (q + 1) * H] = white[q].astype(jnp.bfloat16)
+        top = energy.astype(jnp.bfloat16)
+        rest = (energy - top.astype(jnp.float32)).astype(jnp.bfloat16)
+        smooth = jnp.dot(top, band, preferred_element_type=jnp.float32) + jnp.dot(
+            rest, band, preferred_element_type=jnp.float32
+        )
+        water = jnp.sum(energy, axis=1, keepdims=True) * (1.0 / F)
+        scaling = lax.rsqrt(smooth * (1.0 / (2.0 * smooth_reach + 1.0)) + (0.1 * water + 1e-06)) * keep
+        near, far = scaling[:, :H], scaling[:, H:]
+        white = [parts[0] * near, parts[1] * near, parts[2] * far, parts[3] * far]
+        at = pl.ds(pl.multiple_of(part * rows, rows), rows)
+        for q in range(4):
+            whitened_ref[at, q * H : (q + 1) * H] = white[q].astype(jnp.bfloat16)
+        return carry
+
+    lax.fori_loop(0, row_parts, whiten, 0)
 
 
 def select_kernel(where_ref, whitened_ref, owners_ref, places_ref, outgoing_ref, selector):
@@ -186,21 +197,36 @@
 
 def spectra_call(traces, quality):
     rows, length = traces.shape
-    block = rows // ROW_STEPS
-    table = jnp.asarray(forward_table(length))
+    part, depth = rows // ROW_STEPS, length // K_STEPS
+    anywhere = pl.BlockSpec(memory_space=pl.ANY)
     return pl.pallas_call(
         spectra_kernel,
-        grid=(ROW_STEPS,),
-        in_specs=[pl.BlockSpec((block, length), lambda s: (s, 0)), whole(table), whole(quality)],
-        out_specs=pl.BlockSpec((block, 2 * F), lambda s: (s, 0)),
+        in_specs=[anywhere, anywhere, vmem_spec()],
+        out_specs=vmem_spec(),
         out_shape=jax.ShapeDtypeStruct((rows, 2 * F), jnp.bfloat16),
-        scratch_shapes=[pltpu.VMEM((F, F), jnp.bfloat16), pltpu.VMEM((block, H), jnp.float32)],
+        scratch_shapes=[
+            pltpu.VMEM((ROW_STEPS, K_STEPS, part, depth), jnp.bfloat16),
+            pltpu.VMEM((K_STEPS, depth, 2 * F), jnp.bfloat16),
+            pltpu.SemaphoreType.DMA((ROW_STEPS + 1, K_STEPS)),
+        ],
         compiler_params=pltpu.CompilerParams(vmem_limit_bytes=SPECTRA_VMEM_LIMIT),
         cost_estimate=pl.CostEstimate(
-            flops=rows * length * 2 * F, bytes_accessed=2 * (rows + F) * length, transcendentals=rows * F
+            flops=2 * rows * length * 2 * F, bytes_accessed=2 * (rows + 2 * F) * length, transcendentals=rows * F
         ),
         name="spectra",
-    )(traces, table, quality)
+    )(traces, jnp.asarray(forward_table(length)), quality)
+
+
+def after(first, second):
+    anywhere = pl.BlockSpec(memory_space=pl.ANY)
+    return pl.pallas_call(
+        lambda first_ref, second_ref, out_ref: None,
+        in_specs=[anywhere, anywhere],
+        out_specs=anywhere,
+        out_shape=jax.ShapeDtypeStruct(first.shape, first.dtype),
+        input_output_aliases={0: 0},
+        name="after",
+    )(first, second)
 
 
 def select_call(where, whitened, owners, places, chan_count, ch_dev):
@@ -214,7 +240,7 @@
         out_specs=pl.BlockSpec((chan_count, slots, columns), lambda s: (0, s, 0)),
         out_shape=jax.ShapeDtypeStruct((chan_count, ROW_STEPS * slots, columns), jnp.bfloat16),
         scratch_shapes=[pltpu.VMEM((chan_count * 2 * CAP, 2 * ch_dev), jnp.bfloat16)],
-        compiler_params=pltpu.CompilerParams(vmem_limit_bytes=VMEM_LIMIT),
+        compiler_params=pltpu.CompilerParams(vmem_limit_bytes=SPECTRA_VMEM_LIMIT),
         cost_estimate=pl.CostEstimate(
             flops=4 * rows * chan_count * 2 * CAP * columns, bytes_accessed=2 * rows * columns * 3, transcendentals=0
         ),
@@ -402,7 +428,7 @@
             pltpu.VMEM((3, ch_dev, H), jnp.float32),
             pltpu.VMEM((rows, count * slots // pairs), jnp.bfloat16),
         ],
-        compiler_params=pltpu.CompilerParams(vmem_limit_bytes=VMEM_LIMIT),
+        compiler_params=pltpu.CompilerParams(vmem_limit_bytes=FOLD_VMEM_LIMIT),
         cost_estimate=pl.CostEstimate(
             flops=2 * rows * pairs * count * 2 * CAP * columns,
             bytes_accessed=2 * (incoming.size + own.size),
@@ -438,7 +464,7 @@
     upper = from_above(whitened)
     common = [round_win(whitened[:, shared:], shift) for shift in range(1, win_count)]
     outgoing = select_call(where, flat, owners, places, chan_count, ch_dev)
-    incoming = lax.all_to_all(outgoing, "chan", split_axis=0, concat_axis=0, tiled=True)
+    incoming = lax.all_to_all(after(outgoing, upper), "chan", split_axis=0, concat_axis=0, tiled=True)
     offered = jnp.concatenate([whitened[:, :shared], upper], axis=1)
     special = [
         round_win(

time: 96.4 us -> 85.8 us (0.89)
  the two profiles are of different devices: /device:TPU:13 before, /device:TPU:16 now
where the time goes in v1:
time: 85.8 us; the launch traced here: 85.5 us
  Pallas kernels  36.5 us (43%)
  waiting for transfers between devices  26.4 us (31%)
  starting transfers between devices  12.9 us (15%)
  local copies, waits for them, and re-layouts  7.15 us (8%)
  other arithmetic  1.8 us (2%)
    pallas_call x2, Pallas kernels, cross_call(): pl.pallas_call(functools.partial(cross_kernel, last, with_sum, local_wind...  25.8 us
    all_to_all x1, waiting for transfers between devices, local(): lax.all_to_all(after(outgoing, upper), 'chan', split_axis=0, concat_axis=...  20 us
    all_to_all x1, starting transfers between devices, local(): lax.all_to_all(after(outgoing, upper), 'chan', split_axis=0, concat_axis=...  6.57 us
    pallas_call x1, Pallas kernels, spectra_call(): pl.pallas_call(spectra_kernel, in_specs=[anywhere, anywhere, vmem_spec()]...  6.46 us
    ppermute x1, waiting for transfers between devices, from_above(): return lax.ppermute(block, 'chan', [(i, i - 1) for i in range(1, count)])  6.37 us
    unnamed x22, local copies, waits for them, and re-layouts  6.32 us
    ppermute x3, starting transfers between devices, round_win(): lax.ppermute(block, 'win', [(i, (i + shift) % count) for i in range(count)])  3.58 us
    ppermute x1, starting transfers between devices, from_above(): return lax.ppermute(block, 'chan', [(i, i - 1) for i in range(1, count)])  2.75 us
  transfers between devices with their start and end apart: 5, of which 2 were waited for; matrix products, arithmetic and copies ran while one was open for 2% of the time, Pallas kernels for 35%

profile of v1, /device:TPU:16, one launch (start us, length us, event | category | flops | bytes accessed | tf_op | source)
XLA Modules:
  0.0 85.5 jit_solution(8703368924700734654)
XLA Ops:
  0.6 0.0 copy-start.7
  0.6 0.6 copy-done.7
  1.3 0.0 copy-start.8
  1.3 2.2 %copy-done.8 = bf16[4096,512]{1,0:T(8,128)(2,1)S(1)} copy-done((bf16[4096,512]{1,0:T(8,128)(2,1)S(1)}, bf16[4096,512]{1,0:T(8,128)(2,1)}, u32[]{:S(2)}) %copy-start.8) | copy-done | bytes 4194328
  3.5 0.0 copy-start.5
  3.5 0.0 copy-start.6
  3.5 6.5 %spectra.1.whitened_ref.own_ref = bf16[768,512]{1,0:T(8,128)(2,1)S(1)} custom-call(bf16[768,4096]{1,0:T(8,128)(2,1)} %bitcast.14, bf16[4096,512]{1,0:T(8,128)(2,1)S(1)} %copy-done.8, s32[1,64]{1,0:T(1,128)S(1)} %bitcast.13), custom_call_target="tpu_custom_call" | custom-call | flops 3221225472 | bytes 10485760 | tf_op jit(solution)/shard_map/spectra/pallas_call | solution.py:202
  9.9 2.8 %collective-permute-start.1 = (bf16[12,64,512]{2,1,0:T(8,128)(2,1)S(1)}, bf16[12,64,512]{2,1,0:T(8,128)(2,1)S(1)}, u32[]{:S(2)}, u32[]{:S(2)}) collective-permute-start(bf16[12,64,512]{2,1,0:T(8,128)(2,1)S(1)} %bitcast.7), channel_id=1, source_target_pairs={{2,0},{4,2},{6,4},{8,6},{10,8},{12,10},{14,12},{16,14},{18,16},{20... | collective-permute-start | bytes 2359304 | tf_op jit(solution)/shard_map/ppermute | solution.py:443
  12.7 0.1 pad_add_fusion.where_ref
  12.8 0.0 copy-done.5
  12.8 0.0 copy-done.6
  12.8 1.9 %select.3.first_ref = bf16[16,96,512]{2,1,0:T(8,128)(2,1)S(1)} custom-call(s32[2]{0:T(128)S(1)} %pad_add_fusion.where_ref, bf16[768,512]{1,0:T(8,128)(2,1)S(1)} %spectra.1.whitened_ref.own_ref, s32[8,128]{1,0:T(8,128)S(1)} %bitcast.10, s32[8,128]{1,0:T(8,128)S(1)} %bitcast.12), custom_call_target="tpu_custom_call" | custom-call | flops 402653184 | bytes 2359296 | tf_op jit(solution)/shard_map/select/pallas_call | solution.py:236
  14.7 0.0 copy-start
  14.7 1.1 %copy-done = bf16[16,96,512]{2,1,0:T(8,128)(2,1)} copy-done((bf16[16,96,512]{2,1,0:T(8,128)(2,1)}, bf16[16,96,512]{2,1,0:T(8,128)(2,1)S(1)}, u32[]{:S(2)}) %copy-start) | copy-done | bytes 1572888
  15.8 6.4 %collective-permute-done.1.second_ref = bf16[12,64,512]{2,1,0:T(8,128)(2,1)S(1)} collective-permute-done((bf16[12,64,512]{2,1,0:T(8,128)(2,1)S(1)}, bf16[12,64,512]{2,1,0:T(8,128)(2,1)S(1)}, u32[]{:S(2)}, u32[]{:S(2)}) %collective-permute-start.1) | collective-permute-done | bytes 786464 | tf_op jit(solution)/shard_map/ppermute | solution.py:443
  22.2 0.0 copy-start.1
  22.2 0.9 %copy-done.1 = bf16[12,64,512]{2,1,0:T(8,128)(2,1)} copy-done((bf16[12,64,512]{2,1,0:T(8,128)(2,1)}, bf16[12,64,512]{2,1,0:T(8,128)(2,1)S(1)}, u32[]{:S(2)}) %copy-start.1) | copy-done | bytes 786456
  23.1 6.6 %all-to-all-start = ((bf16[16,96,512]{2,1,0:T(8,128)(2,1)}), bf16[16,96,512]{2,1,0:T(8,128)(2,1)S(1)}, u32[]{:S(2)}, u32[]{:S(2)}) async-start(bf16[16,96,512]{2,1,0:T(8,128)(2,1)} %after.1), calls=%async_computation | async-start | bytes 3145728 | tf_op jit(solution)/shard_map/all_to_all | solution.py:467
  29.7 0.0 copy-start.2
  29.7 0.8 fusion.1
  30.5 1.5 %collective-permute-start = (bf16[12,32,512]{2,1,0:T(8,128)(2,1)}, bf16[12,32,512]{2,1,0:T(8,128)(2,1)}, u32[]{:S(2)}, u32[]{:S(2)}) collective-permute-start(bf16[12,32,512]{2,1,0:T(8,128)(2,1)} %get-tuple-element.3), channel_id=1, source_target_pairs={{0,1},{1,0},{2,3},{3,2},{4,5},{5,4},{6,7},{7,6},{8,9},{9,8},{10,11... | collective-permute-start | bytes 1179656 | tf_op jit(solution)/shard_map/ppermute | solution.py:448
  32.0 0.0 copy-done.2
  32.0 1.1 %fusion = bf16[12,64,512]{2,1,0:T(8,128)(2,1)} fusion(s32[]{:T(128)S(6)} %select_n.19, bf16[12,32,512]{2,1,0:T(8,128)(2,1)S(1)} %get-tuple-element.2, bf16[12,64,512]{2,1,0:T(8,128)(2,1)S(1)} %copy-done.2), kind=kLoop, calls=%fused_computation.2 | loop fusion | flops 1572864 | bytes 1966084 | tf_op jit(solution)/shard_map/concatenate | solution.py:468
  33.1 0.0 copy-start.3
  33.1 0.0 copy-start.4
  33.1 0.5 collective-permute-start.2
  33.6 11.0 %cross.2.refs_0_ = f32[32,72,256]{2,1,0:T(8,128)S(1)} custom-call(s32[2]{0:T(128)S(1)} %pad_add_fusion.where_ref, bf16[12,64,512]{2,1,0:T(8,128)(2,1)S(1)} %bitcast.9, bf16[12,64,512]{2,1,0:T(8,128)(2,1)S(1)} %copy-done.2), custom_call_target="tpu_custom_call" | custom-call | flops 10000000000 | bytes 3932160 | tf_op jit(solution)/shard_map/cross/pallas_call | solution.py:352
  44.7 0.0 copy-start.9
  44.7 1.4 %copy-done.9 = f32[32,72,256]{2,1,0:T(8,128)} copy-done((f32[32,72,256]{2,1,0:T(8,128)}, f32[32,72,256]{2,1,0:T(8,128)S(1)}, u32[]{:S(2)}) %copy-start.9) | copy-done | bytes 2359320
  46.1 20.0 %all-to-all-done.incoming_ref = bf16[16,96,512]{2,1,0:T(8,128)(2,1)S(1)} async-done(((bf16[16,96,512]{2,1,0:T(8,128)(2,1)}), bf16[16,96,512]{2,1,0:T(8,128)(2,1)S(1)}, u32[]{:S(2)}, u32[]{:S(2)}) %all-to-all-start) | async-done | bytes 1572896 | tf_op jit(solution)/shard_map/all_to_all | solution.py:467
  66.1 0.0 copy-done.3
  66.1 0.0 copy-done.4
  66.1 0.0 copy-start.10
  66.1 2.4 %fold.1 = f32[64,256]{1,0:T(8,128)S(1)} custom-call(s32[2]{0:T(128)S(1)} %pad_add_fusion.where_ref, bf16[16,96,512]{2,1,0:T(8,128)(2,1)S(1)} %all-to-all-done.incoming_ref, bf16[768,512]{1,0:T(8,128)(2,1)S(1)} %spectra.1.whitened_ref.own_ref, s32[8,128]{1,0:T(8,128)S(1)} %bitcast.11, bf16[256,256]{1,0:T(8,128)(2,1)S(1)} %copy-done.3, ...), custom_call_target="tpu_custom_call" | custom-call | flops 201326592 | bytes 2359296 | tf_op jit(solution)/shard_map/fold/pallas_call | solution.py:414
  68.5 1.6 %collective-permute-start.3 = (f32[32,256]{1,0:T(8,128)S(1)}, f32[32,256]{1,0:T(8,128)S(1)}, u32[]{:S(2)}, u32[]{:S(2)}) collective-permute-start(f32[32,256]{1,0:T(8,128)S(1)} %constant_dynamic-slice_fusion), channel_id=1, source_target_pairs={{0,1},{1,0},{2,3},{3,2},{4,5},{5,4},{6,7},{7,6},{8,9},{9,8},{10,11... | collective-permute-start | bytes 98312 | tf_op jit(solution)/shard_map/ppermute | solution.py:448
  70.1 0.0 collective-permute-done.first_ref
  70.1 0.0 collective-permute-done.2.second_ref
  70.1 0.0 copy-done.10
  70.1 14.8 %cross.3 = f32[32,64,256]{2,1,0:T(8,128)} custom-call(s32[2]{0:T(128)S(1)} %pad_add_fusion.where_ref, bf16[12,32,512]{2,1,0:T(8,128)(2,1)} %collective-permute-done.first_ref, bf16[12,64,512]{2,1,0:T(8,128)(2,1)} %collective-permute-done.2.second_ref, f32[32,72,256]{2,1,0:T(8,128)S(1)} %copy-done.10, bf16[256,256]{1,0:T(8,128)(2,1)S(1)} %copy-done.3, ...), custom_call_target="tpu_custom_call" | custom-call | flops 10000000000 | bytes 3932160 | tf_op jit(solution)/shard_map/cross/pallas_call | solution.py:352
  84.9 0.0 collective-permute-done.3
  84.9 0.6 dynamic-slice_add_fusion
  (2 shorter events, 0.0 us)
Async XLA Ops:
  0.6 0.7 copy-start.7
  1.3 2.2 %copy-start.8 = (bf16[4096,512]{1,0:T(8,128)(2,1)S(1)}, bf16[4096,512]{1,0:T(8,128)(2,1)}, u32[]{:S(2)}) copy-start(bf16[4096,512]{1,0:T(8,128)(2,1)} %constant.39.clone.table_ref) | copy-start | bytes 12582916
  3.5 9.3 %copy-start.5 = (s32[1024,1]{0,1:T(1,128)S(1)}, s32[1024,1]{0,1:T(1,128)}, u32[]{:S(2)}) copy-start(s32[1024,1]{0,1:T(1,128)} %param.9) | copy-start | bytes 12292
  3.5 9.3 %copy-start.6 = (s32[1024]{0:T(1024)S(1)}, s32[1024]{0:T(1024)}, u32[]{:S(2)}) copy-start(s32[1024]{0:T(1024)} %param.10) | copy-start | bytes 12292
  9.9 12.2 %collective-permute-start.1 = (bf16[12,64,512]{2,1,0:T(8,128)(2,1)S(1)}, bf16[12,64,512]{2,1,0:T(8,128)(2,1)S(1)}, u32[]{:S(2)}, u32[]{:S(2)}) collective-permute-start(bf16[12,64,512]{2,1,0:T(8,128)(2,1)S(1)} %bitcast.7), channel_id=1, source_target_pairs={{2,0},{4,2},{6,4},{8,6},{10,8},{12,10},{14,12},{16,14},{18,16},{20... | collective-permute-start | bytes 2359304 | tf_op jit(solution)/shard_map/ppermute | solution.py:443
  14.7 1.1 %copy-start = (bf16[16,96,512]{2,1,0:T(8,128)(2,1)}, bf16[16,96,512]{2,1,0:T(8,128)(2,1)S(1)}, u32[]{:S(2)}) copy-start(bf16[16,96,512]{2,1,0:T(8,128)(2,1)S(1)} %select.3.first_ref) | copy-start | bytes 4718596
  22.2 0.9 %copy-start.1 = (bf16[12,64,512]{2,1,0:T(8,128)(2,1)}, bf16[12,64,512]{2,1,0:T(8,128)(2,1)S(1)}, u32[]{:S(2)}) copy-start(bf16[12,64,512]{2,1,0:T(8,128)(2,1)S(1)} %collective-permute-done.1.second_ref) | copy-start | bytes 2359300
  23.1 43.0 %all-to-all-start = ((bf16[16,96,512]{2,1,0:T(8,128)(2,1)}), bf16[16,96,512]{2,1,0:T(8,128)(2,1)S(1)}, u32[]{:S(2)}, u32[]{:S(2)}) async-start(bf16[16,96,512]{2,1,0:T(8,128)(2,1)} %after.1), calls=%async_computation | async-start | bytes 3145728 | tf_op jit(solution)/shard_map/all_to_all | solution.py:467
  29.7 2.3 %copy-start.2 = (bf16[12,64,512]{2,1,0:T(8,128)(2,1)S(1)}, bf16[12,64,512]{2,1,0:T(8,128)(2,1)}, u32[]{:S(2)}) copy-start(bf16[12,64,512]{2,1,0:T(8,128)(2,1)} %copy-done.1) | copy-start | bytes 2359300
  30.5 39.6 %collective-permute-start = (bf16[12,32,512]{2,1,0:T(8,128)(2,1)}, bf16[12,32,512]{2,1,0:T(8,128)(2,1)}, u32[]{:S(2)}, u32[]{:S(2)}) collective-permute-start(bf16[12,32,512]{2,1,0:T(8,128)(2,1)} %get-tuple-element.3), channel_id=1, source_target_pairs={{0,1},{1,0},{2,3},{3,2},{4,5},{5,4},{6,7},{7,6},{8,9},{9,8},{10,11... | collective-permute-start | bytes 1179656 | tf_op jit(solution)/shard_map/ppermute | solution.py:448
  33.1 33.0 %copy-start.3 = (bf16[256,256]{1,0:T(8,128)(2,1)S(1)}, bf16[256,256]{1,0:T(8,128)(2,1)}, u32[]{:S(2)}) copy-start(bf16[256,256]{1,0:T(8,128)(2,1)} %constant.37.clone.refs_1_.high_ref) | copy-start | bytes 393220
  33.1 33.0 %copy-start.4 = (bf16[256,256]{1,0:T(8,128)(2,1)S(1)}, bf16[256,256]{1,0:T(8,128)(2,1)}, u32[]{:S(2)}) copy-start(bf16[256,256]{1,0:T(8,128)(2,1)} %constant.38.clone.refs_2_.low_ref) | copy-start | bytes 393220
  33.1 37.0 %collective-permute-start.2 = (bf16[12,64,512]{2,1,0:T(8,128)(2,1)}, bf16[12,64,512]{2,1,0:T(8,128)(2,1)}, u32[]{:S(2)}, u32[]{:S(2)}) collective-permute-start(bf16[12,64,512]{2,1,0:T(8,128)(2,1)} %fusion), channel_id=1, source_target_pairs={{0,1},{1,0},{2,3},{3,2},{4,5},{5,4},{6,7},{7,6},{8,9},{9,8},{10,11... | collective-permute-start | bytes 2359304 | tf_op jit(solution)/shard_map/ppermute | solution.py:448
  44.7 1.4 %copy-start.9 = (f32[32,72,256]{2,1,0:T(8,128)}, f32[32,72,256]{2,1,0:T(8,128)S(1)}, u32[]{:S(2)}) copy-start(f32[32,72,256]{2,1,0:T(8,128)S(1)} %cross.2.refs_0_) | copy-start | bytes 7077892
  66.1 4.0 %copy-start.10 = (f32[32,72,256]{2,1,0:T(8,128)S(1)}, f32[32,72,256]{2,1,0:T(8,128)}, u32[]{:S(2)}) copy-start(f32[32,72,256]{2,1,0:T(8,128)} %copy-done.9) | copy-start | bytes 7077892
  68.5 16.4 %collective-permute-start.3 = (f32[32,256]{1,0:T(8,128)S(1)}, f32[32,256]{1,0:T(8,128)S(1)}, u32[]{:S(2)}, u32[]{:S(2)}) collective-permute-start(f32[32,256]{1,0:T(8,128)S(1)} %constant_dynamic-slice_fusion), channel_id=1, source_target_pairs={{0,1},{1,0},{2,3},{3,2},{4,5},{5,4},{6,7},{7,6},{8,9},{9,8},{10,11... | collective-permute-start | bytes 98312 | tf_op jit(solution)/shard_map/ppermute | solution.py:448

commit v2 on v1

--- a/solution.py
+++ b/solution.py
@@ -21,7 +21,7 @@
 K_STEPS = 4
 VMEM_LIMIT = 24 * 1024 * 1024
 FOLD_VMEM_LIMIT = 16 * 1024 * 1024
-SPECTRA_VMEM_LIMIT = 48 * 1024 * 1024
+SPECTRA_VMEM_LIMIT = 59 * 1024 * 1024
 
 
 def bin_order():
@@ -215,18 +215,6 @@
         ),
         name="spectra",
     )(traces, jnp.asarray(forward_table(length)), quality)
-
-
-def after(first, second):
-    anywhere = pl.BlockSpec(memory_space=pl.ANY)
-    return pl.pallas_call(
-        lambda first_ref, second_ref, out_ref: None,
-        in_specs=[anywhere, anywhere],
-        out_specs=anywhere,
-        out_shape=jax.ShapeDtypeStruct(first.shape, first.dtype),
-        input_output_aliases={0: 0},
-        name="after",
-    )(first, second)
 
 
 def select_call(where, whitened, owners, places, chan_count, ch_dev):
@@ -363,7 +351,7 @@
     )(*operands)
 
 
-def fold_kernel(where_ref, incoming_ref, own_ref, owners_ref, high_ref, low_ref, out_ref, sums, picker):
+def fold_kernel(where_ref, incoming_ref, own_ref, owners_ref, high_ref, low_ref, earlier_ref, out_ref, sums, picker):
     step = pl.program_id(0)
     rows = own_ref.shape[0]
     ch_dev = rows // 2
@@ -407,7 +395,7 @@
         out_ref[...] = lag_transform(stacks, high_ref[...], low_ref[...])
 
 
-def fold_call(where, incoming, own, owners, ch_dev, tables):
+def fold_call(where, incoming, own, owners, ch_dev, tables, earlier):
     count, slots, columns = incoming.shape
     rows = 2 * ch_dev
     pairs = own.shape[0] // rows
@@ -421,6 +409,7 @@
             whole(owners),
             whole(tables[0]),
             whole(tables[1]),
+            pl.BlockSpec(memory_space=pl.ANY),
         ],
         out_specs=pl.BlockSpec((ch_dev, NLAG), lambda s: (0, 0)),
         out_shape=jax.ShapeDtypeStruct((ch_dev, NLAG), jnp.float32),
@@ -435,7 +424,7 @@
             transcendentals=0,
         ),
         name="fold",
-    )(where, incoming, own, owners, *tables)
+    )(where, incoming, own, owners, *tables, earlier)
 
 
 def from_above(block):
@@ -464,7 +453,7 @@
     upper = from_above(whitened)
     common = [round_win(whitened[:, shared:], shift) for shift in range(1, win_count)]
     outgoing = select_call(where, flat, owners, places, chan_count, ch_dev)
-    incoming = lax.all_to_all(after(outgoing, upper), "chan", split_axis=0, concat_axis=0, tiled=True)
+    incoming = lax.all_to_all(outgoing, "chan", split_axis=0, concat_axis=0, tiled=True)
     offered = jnp.concatenate([whitened[:, :shared], upper], axis=1)
     special = [
         round_win(
@@ -477,7 +466,7 @@
     for n, (first, second) in enumerate(arrived):
         ends = tables if n == win_count - 1 else None
         sums = cross_call(where, first, second, ch_dev, own_count, sums, ends, n == 0)
-    share = fold_call(where, incoming, flat, owners, ch_dev, tables)
+    share = fold_call(where, incoming, flat, owners, ch_dev, tables, sums)
     fold = lax.dynamic_slice_in_dim(share, window_part * own_count, own_count, 0)
     for shift in range(1, win_count):
         target = (window_part + shift) % win_count * own_count

time: 85.8 us -> 100 us (1.17)
  the two profiles are of different devices: /device:TPU:16 before, /device:TPU:13 now
where the time goes in v2:
time: 100 us; the launch traced here: 99.6 us
  waiting for transfers between devices  42.8 us (43%)
  Pallas kernels  40.5 us (40%)
  starting transfers between devices  11.8 us (12%)
  local copies, waits for them, and re-layouts  2.43 us (2%)
  other arithmetic  1.41 us (1%)
    ppermute x1, waiting for transfers between devices, from_above(): return lax.ppermute(block, 'chan', [(i, i - 1) for i in range(1, count)])  40.3 us
    pallas_call x2, Pallas kernels, cross_call(): pl.pallas_call(functools.partial(cross_kernel, last, with_sum, local_wind...  25.6 us
    pallas_call x1, Pallas kernels, spectra_call(): pl.pallas_call(spectra_kernel, in_specs=[anywhere, anywhere, vmem_spec()]...  8.63 us
    all_to_all x1, starting transfers between devices, local(): lax.all_to_all(outgoing, 'chan', split_axis=0, concat_axis=0, tiled=True)  6.69 us
    pallas_call x1, Pallas kernels, select_call(): pl.pallas_call(select_kernel, grid=(ROW_STEPS,), in_specs=[smem_spec(), p...  3.9 us
    ppermute x3, starting transfers between devices, round_win(): lax.ppermute(block, 'win', [(i, (i + shift) % count) for i in range(count)])  2.81 us
    ppermute x3, waiting for transfers between devices, round_win(): lax.ppermute(block, 'win', [(i, (i + shift) % count) for i in range(count)])  2.51 us
    pallas_call x1, Pallas kernels, fold_call(): pl.pallas_call(fold_kernel, grid=(pairs,), in_specs=[smem_spec(), pl.Bloc...  2.38 us
  transfers between devices with their start and end apart: 5, of which 2 were waited for; matrix products, arithmetic and copies ran while one was open for 1% of the time, Pallas kernels for 26%

profile of v2, /device:TPU:13, one launch (start us, length us, event | category | flops | bytes accessed | tf_op | source)
XLA Modules:
  0.0 99.6 jit_solution(17520028184993604734)
XLA Ops:
  0.6 0.6 pad_add_fusion.where_ref
  1.2 8.6 %spectra.1.whitened_ref.own_ref = bf16[768,512]{1,0:T(8,128)(2,1)} custom-call(bf16[768,4096]{1,0:T(8,128)(2,1)} %bitcast.13, bf16[4096,512]{1,0:T(8,128)(2,1)} %constant.39.clone.table_ref, s32[1,64]{1,0:T(1,128)} %bitcast.14), custom_call_target="tpu_custom_call" | custom-call | flops 3221225472 | bytes 10485760 | tf_op jit(solution)/shard_map/spectra/pallas_call | solution.py:202
  9.9 3.9 %select.3 = bf16[16,96,512]{2,1,0:T(8,128)(2,1)} custom-call(s32[2]{0:T(128)} %pad_add_fusion.where_ref, bf16[768,512]{1,0:T(8,128)(2,1)} %spectra.1.whitened_ref.own_ref, s32[8,128]{1,0:T(8,128)} %bitcast.10, s32[8,128]{1,0:T(8,128)} %bitcast.12), custom_call_target="tpu_custom_call" | custom-call | flops 402653184 | bytes 2359296 | tf_op jit(solution)/shard_map/select/pallas_call | solution.py:224
  13.8 0.0 copy-start
  13.8 6.7 %all-to-all-start = ((bf16[16,96,512]{2,1,0:T(8,128)(2,1)}), bf16[16,96,512]{2,1,0:T(8,128)(2,1)S(1)}, u32[]{:S(2)}, u32[]{:S(2)}) async-start(bf16[16,96,512]{2,1,0:T(8,128)(2,1)} %select.3), calls=%async_computation | async-start | bytes 3145728 | tf_op jit(solution)/shard_map/all_to_all | solution.py:456
  20.5 0.0 copy-done
  20.5 0.0 copy-start.5
  20.5 2.3 %collective-permute-start.1 = (bf16[12,64,512]{2,1,0:T(8,128)(2,1)S(1)}, bf16[12,64,512]{2,1,0:T(8,128)(2,1)S(1)}, u32[]{:S(2)}, u32[]{:S(2)}) collective-permute-start(bf16[12,64,512]{2,1,0:T(8,128)(2,1)S(1)} %bitcast.7), channel_id=1, source_target_pairs={{2,0},{4,2},{6,4},{8,6},{10,8},{12,10},{14,12},{16,14},{18,16},{20... | collective-permute-start | bytes 2359304 | tf_op jit(solution)/shard_map/ppermute | solution.py:432
  22.8 0.8 fusion.1
  23.6 1.2 %collective-permute-start = (bf16[12,32,512]{2,1,0:T(8,128)(2,1)}, bf16[12,32,512]{2,1,0:T(8,128)(2,1)}, u32[]{:S(2)}, u32[]{:S(2)}) collective-permute-start(bf16[12,32,512]{2,1,0:T(8,128)(2,1)} %get-tuple-element.3), channel_id=1, source_target_pairs={{0,1},{1,0},{2,3},{3,2},{4,5},{5,4},{6,7},{7,6},{8,9},{9,8},{10,11... | collective-permute-start | bytes 1179656 | tf_op jit(solution)/shard_map/ppermute | solution.py:437
  24.8 40.3 %collective-permute-done.1.second_ref = bf16[12,64,512]{2,1,0:T(8,128)(2,1)S(1)} collective-permute-done((bf16[12,64,512]{2,1,0:T(8,128)(2,1)S(1)}, bf16[12,64,512]{2,1,0:T(8,128)(2,1)S(1)}, u32[]{:S(2)}, u32[]{:S(2)}) %collective-permute-start.1) | collective-permute-done | bytes 786464 | tf_op jit(solution)/shard_map/ppermute | solution.py:432
  65.1 0.2 fusion
  65.3 0.0 copy-start.2
  65.3 0.0 copy-start.3
  65.3 1.3 %collective-permute-start.2 = (bf16[12,64,512]{2,1,0:T(8,128)(2,1)S(1)}, bf16[12,64,512]{2,1,0:T(8,128)(2,1)S(1)}, u32[]{:S(2)}, u32[]{:S(2)}) collective-permute-start(bf16[12,64,512]{2,1,0:T(8,128)(2,1)S(1)} %fusion), channel_id=1, source_target_pairs={{0,1},{1,0},{2,3},{3,2},{4,5},{5,4},{6,7},{7,6},{8,9},{9,8},{10,11... | collective-permute-start | bytes 2359304 | tf_op jit(solution)/shard_map/ppermute | solution.py:437
  66.6 0.0 copy-done.5
  66.6 11.0 %cross.2.refs_0_ = f32[32,72,256]{2,1,0:T(8,128)S(1)} custom-call(s32[2]{0:T(128)S(1)} %copy-done.5, bf16[12,64,512]{2,1,0:T(8,128)(2,1)S(1)} %bitcast.9, bf16[12,64,512]{2,1,0:T(8,128)(2,1)S(1)} %collective-permute-done.1.second_ref), custom_call_target="tpu_custom_call" | custom-call | flops 10000000000 | bytes 3932160 | tf_op jit(solution)/shard_map/cross/pallas_call | solution.py:340
  77.6 0.0 copy-start.4
  77.6 0.0 collective-permute-done.first_ref
  77.6 0.0 collective-permute-done.2.second_ref
  77.6 0.0 copy-done.2
  77.6 0.0 copy-done.3
  77.6 14.5 %cross.3.earlier_ref = f32[32,64,256]{2,1,0:T(8,128)} custom-call(s32[2]{0:T(128)S(1)} %copy-done.5, bf16[12,32,512]{2,1,0:T(8,128)(2,1)} %collective-permute-done.first_ref, bf16[12,64,512]{2,1,0:T(8,128)(2,1)S(1)} %collective-permute-done.2.second_ref, f32[32,72,256]{2,1,0:T(8,128)S(1)} %cross.2.refs_0_, bf16[256,256]{1,0:T(8,128)(2,1)S(1)} %copy-done.3, ...), custom_call_target="tpu_custom_call" | custom-call | flops 10000000000 | bytes 3932160 | tf_op jit(solution)/shard_map/cross/pallas_call | solution.py:340
  92.2 0.0 all-to-all-done.incoming_ref
  92.2 0.0 copy-done.4
  92.2 0.0 copy-start.1
  92.2 1.6 %copy-done.1 = f32[32,64,256]{2,1,0:T(8,128)S(1)} copy-done((f32[32,64,256]{2,1,0:T(8,128)S(1)}, f32[32,64,256]{2,1,0:T(8,128)}, u32[]{:S(2)}) %copy-start.1) | copy-done | bytes 2097176
  93.8 2.4 %fold.1 = f32[64,256]{1,0:T(8,128)S(1)} custom-call(s32[2]{0:T(128)S(1)} %copy-done.5, bf16[16,96,512]{2,1,0:T(8,128)(2,1)S(1)} %all-to-all-done.incoming_ref, bf16[768,512]{1,0:T(8,128)(2,1)S(1)} %copy-done, s32[8,128]{1,0:T(8,128)S(1)} %bitcast.11, bf16[256,256]{1,0:T(8,128)(2,1)S(1)} %copy-done.3, bf16[256,256]{1,0:T(8,128)(2,1)S(1)} %copy-done.2, ...), custom_call_target="tpu_custom_call" | custom-call | flops 201326592 | bytes 2359296 | tf_op jit(solution)/shard_map/fold/pallas_call | solution.py:402
  96.2 0.3 collective-permute-start.3
  96.5 2.5 %collective-permute-done.3 = f32[32,256]{1,0:T(8,128)S(1)} collective-permute-done((f32[32,256]{1,0:T(8,128)S(1)}, f32[32,256]{1,0:T(8,128)S(1)}, u32[]{:S(2)}, u32[]{:S(2)}) %collective-permute-start.3) | collective-permute-done | bytes 32800 | tf_op jit(solution)/shard_map/ppermute | solution.py:437
  99.0 0.6 dynamic-slice_add_fusion
  (1 shorter events, 0.0 us)
Async XLA Ops:
  13.8 6.7 %copy-start = (bf16[768,512]{1,0:T(8,128)(2,1)S(1)}, bf16[768,512]{1,0:T(8,128)(2,1)}, u32[]{:S(2)}) copy-start(bf16[768,512]{1,0:T(8,128)(2,1)} %spectra.1.whitened_ref.own_ref) | copy-start | bytes 2359300
  13.8 78.4 %all-to-all-start = ((bf16[16,96,512]{2,1,0:T(8,128)(2,1)}), bf16[16,96,512]{2,1,0:T(8,128)(2,1)S(1)}, u32[]{:S(2)}, u32[]{:S(2)}) async-start(bf16[16,96,512]{2,1,0:T(8,128)(2,1)} %select.3), calls=%async_computation | async-start | bytes 3145728 | tf_op jit(solution)/shard_map/all_to_all | solution.py:456
  20.5 46.1 %copy-start.5 = (s32[2]{0:T(128)S(1)}, s32[2]{0:T(128)}, u32[]{:S(2)}) copy-start(s32[2]{0:T(128)} %pad_add_fusion.where_ref) | copy-start | bytes 28
  20.5 44.6 %collective-permute-start.1 = (bf16[12,64,512]{2,1,0:T(8,128)(2,1)S(1)}, bf16[12,64,512]{2,1,0:T(8,128)(2,1)S(1)}, u32[]{:S(2)}, u32[]{:S(2)}) collective-permute-start(bf16[12,64,512]{2,1,0:T(8,128)(2,1)S(1)} %bitcast.7), channel_id=1, source_target_pairs={{2,0},{4,2},{6,4},{8,6},{10,8},{12,10},{14,12},{16,14},{18,16},{20... | collective-permute-start | bytes 2359304 | tf_op jit(solution)/shard_map/ppermute | solution.py:432
  23.6 54.1 %collective-permute-start = (bf16[12,32,512]{2,1,0:T(8,128)(2,1)}, bf16[12,32,512]{2,1,0:T(8,128)(2,1)}, u32[]{:S(2)}, u32[]{:S(2)}) collective-permute-start(bf16[12,32,512]{2,1,0:T(8,128)(2,1)} %get-tuple-element.3), channel_id=1, source_target_pairs={{0,1},{1,0},{2,3},{3,2},{4,5},{5,4},{6,7},{7,6},{8,9},{9,8},{10,11... | collective-permute-start | bytes 1179656 | tf_op jit(solution)/shard_map/ppermute | solution.py:437
  65.3 12.4 %copy-start.2 = (bf16[256,256]{1,0:T(8,128)(2,1)S(1)}, bf16[256,256]{1,0:T(8,128)(2,1)}, u32[]{:S(2)}) copy-start(bf16[256,256]{1,0:T(8,128)(2,1)} %constant.38.clone.refs_2_.low_ref) | copy-start | bytes 393220
  65.3 12.4 %copy-start.3 = (bf16[256,256]{1,0:T(8,128)(2,1)S(1)}, bf16[256,256]{1,0:T(8,128)(2,1)}, u32[]{:S(2)}) copy-start(bf16[256,256]{1,0:T(8,128)(2,1)} %constant.37.clone.refs_1_.high_ref) | copy-start | bytes 393220
  65.3 12.3 %collective-permute-start.2 = (bf16[12,64,512]{2,1,0:T(8,128)(2,1)S(1)}, bf16[12,64,512]{2,1,0:T(8,128)(2,1)S(1)}, u32[]{:S(2)}, u32[]{:S(2)}) collective-permute-start(bf16[12,64,512]{2,1,0:T(8,128)(2,1)S(1)} %fusion), channel_id=1, source_target_pairs={{0,1},{1,0},{2,3},{3,2},{4,5},{5,4},{6,7},{7,6},{8,9},{9,8},{10,11... | collective-permute-start | bytes 2359304 | tf_op jit(solution)/shard_map/ppermute | solution.py:437
  77.6 14.6 %copy-start.4 = (s32[1024,1]{0,1:T(1,128)S(1)}, s32[1024,1]{0,1:T(1,128)}, u32[]{:S(2)}) copy-start(s32[1024,1]{0,1:T(1,128)} %param.9) | copy-start | bytes 12292
  92.2 1.6 %copy-start.1 = (f32[32,64,256]{2,1,0:T(8,128)S(1)}, f32[32,64,256]{2,1,0:T(8,128)}, u32[]{:S(2)}) copy-start(f32[32,64,256]{2,1,0:T(8,128)} %cross.3.earlier_ref) | copy-start | bytes 6291460
  96.2 2.8 %collective-permute-start.3 = (f32[32,256]{1,0:T(8,128)S(1)}, f32[32,256]{1,0:T(8,128)S(1)}, u32[]{:S(2)}, u32[]{:S(2)}) collective-permute-start(f32[32,256]{1,0:T(8,128)S(1)} %constant_dynamic-slice_fusion), channel_id=1, source_target_pairs={{0,1},{1,0},{2,3},{3,2},{4,5},{5,4},{6,7},{7,6},{8,9},{9,8},{10,11... | collective-permute-start | bytes 98312 | tf_op jit(solution)/shard_map/ppermute | solution.py:437

commit v3 on v2

--- a/solution.py
+++ b/solution.py
@@ -18,10 +18,10 @@
 SPAN = REACH + 8
 smooth_reach = 4
 ROW_STEPS = 3
-K_STEPS = 4
+QUARTERS = 4
 VMEM_LIMIT = 24 * 1024 * 1024
 FOLD_VMEM_LIMIT = 16 * 1024 * 1024
-SPECTRA_VMEM_LIMIT = 59 * 1024 * 1024
+SPECTRA_VMEM_LIMIT = 50 * 1024 * 1024
 
 
 def bin_order():
@@ -33,7 +33,7 @@
 
 
 def forward_table(length):
-    samples = np.arange(length, dtype=np.int64)[:, None]
+    samples = np.arange(length // 4, dtype=np.int64)[:, None]
     parts = []
     for bins in bin_order():
         angles = (samples * (bins + BAND_LO)[None, :] % length) * (2.0 * math.pi / length)
@@ -112,6 +112,22 @@
     return ((lane == place + ch_dev * half) & (place >= 0)).astype(jnp.float32).astype(jnp.bfloat16)
 
 
+def turned_sum(quarters, real, imag, negative):
+    rows = quarters[0].shape[0]
+    lane = lanes_of((rows, H))
+    residue = ((F - lane) if negative else lane) & 3
+    sign = jnp.where((residue & 1) == 0, 1.0, -1.0)
+    straight = jnp.where(residue == 0, 1.0, jnp.where(residue == 2, -1.0, 0.0))
+    turned = jnp.where(residue == 1, 1.0, jnp.where(residue == 3, -1.0, 0.0))
+    re = [quarter[:, real * H : (real + 1) * H] for quarter in quarters]
+    im = [quarter[:, imag * H : (imag + 1) * H] for quarter in quarters]
+    odd_re, odd_im = re[1] + sign * re[3], im[1] + sign * im[3]
+    return (
+        re[0] + sign * re[2] + (straight * odd_re + turned * odd_im),
+        im[0] + sign * im[2] + (straight * odd_im - turned * odd_re),
+    )
+
+
 def spectra_kernel(traces_ref, table_ref, quality_ref, whitened_ref, traces, table, sems):
     row_parts, chunks, rows, depth = traces.shape
     ch_dev = quality_ref.shape[1]
@@ -120,14 +136,11 @@
         source = traces_ref.at[pl.ds(part * rows, rows), pl.ds(k * depth, depth)]
         return pltpu.make_async_copy(source, traces.at[part, k], sems.at[part, k])
 
-    def table_copy(k):
-        return pltpu.make_async_copy(table_ref.at[pl.ds(k * depth, depth), :], table.at[k], sems.at[row_parts, k])
-
+    table_copy = pltpu.make_async_copy(table_ref, table, sems.at[row_parts, 0])
+    table_copy.start()
     for part in range(row_parts):
         for k in range(chunks):
             traces_copy(part, k).start()
-            if part == 0:
-                table_copy(k).start()
 
     band = band_matrix()
     shape = (rows, ch_dev)
@@ -137,17 +150,15 @@
     )
 
     def whiten(part, carry):
-        spectra = None
+        @pl.when(part == 0)
+        def _():
+            table_copy.wait()
+
+        quarters = []
         for k in range(chunks):
             traces_copy(part, k).wait()
-
-            @pl.when(part == 0)
-            def _():
-                table_copy(k).wait()
-
-            product = jnp.dot(traces[part, k], table[k], preferred_element_type=jnp.float32)
-            spectra = product if spectra is None else spectra + product
-        parts = [spectra[:, q * H : (q + 1) * H] for q in range(4)]
+            quarters.append(jnp.dot(traces[part, k], table[...], preferred_element_type=jnp.float32))
+        parts = turned_sum(quarters, 0, 1, False) + turned_sum(quarters, 2, 3, True)
         energy = jnp.concatenate(
             [parts[0] * parts[0] + parts[1] * parts[1], parts[2] * parts[2] + parts[3] * parts[3]], axis=1
         )
@@ -197,7 +208,7 @@
 
 def spectra_call(traces, quality):
     rows, length = traces.shape
-    part, depth = rows // ROW_STEPS, length // K_STEPS
+    part, depth = rows // ROW_STEPS, length // QUARTERS
     anywhere = pl.BlockSpec(memory_space=pl.ANY)
     return pl.pallas_call(
         spectra_kernel,
@@ -205,13 +216,13 @@
         out_specs=vmem_spec(),
         out_shape=jax.ShapeDtypeStruct((rows, 2 * F), jnp.bfloat16),
         scratch_shapes=[
-            pltpu.VMEM((ROW_STEPS, K_STEPS, part, depth), jnp.bfloat16),
-            pltpu.VMEM((K_STEPS, depth, 2 * F), jnp.bfloat16),
-            pltpu.SemaphoreType.DMA((ROW_STEPS + 1, K_STEPS)),
+            pltpu.VMEM((ROW_STEPS, QUARTERS, part, depth), jnp.bfloat16),
+            pltpu.VMEM((depth, 2 * F), jnp.bfloat16),
+            pltpu.SemaphoreType.DMA((ROW_STEPS + 1, QUARTERS)),
         ],
         compiler_params=pltpu.CompilerParams(vmem_limit_bytes=SPECTRA_VMEM_LIMIT),
         cost_estimate=pl.CostEstimate(
-            flops=2 * rows * length * 2 * F, bytes_accessed=2 * (rows + 2 * F) * length, transcendentals=rows * F
+            flops=2 * rows * length * 2 * F, bytes_accessed=2 * rows * length, transcendentals=rows * F
         ),
         name="spectra",
     )(traces, jnp.asarray(forward_table(length)), quality)
@@ -240,7 +251,8 @@
     refs = list(refs)
     sum_ref = refs.pop(0) if with_sum else None
     if last:
-        high_ref, low_ref, out_ref, wide, spread, total = refs
+        high_ref, low_ref, out_ref, done_ref, wide, spread, total = refs
+        done_ref[...] = jnp.zeros_like(done_ref)
     else:
         out_ref, wide, spread = refs
         total = out_ref
@@ -337,15 +349,18 @@
         operands += list(tables)
         scratch.append(pltpu.VMEM((own_count, SPAN, F), jnp.float32))
     shape = (own_count, REACH, NLAG) if last else (own_count, SPAN, F)
+    out_shape = [jax.ShapeDtypeStruct(shape, jnp.float32)]
+    if last:
+        out_shape.append(jax.ShapeDtypeStruct((8, H), jnp.float32))
     return pl.pallas_call(
         functools.partial(cross_kernel, last, with_sum, local_windows),
         in_specs=[smem_spec()] + [vmem_spec()] * (len(operands) - 1),
-        out_specs=vmem_spec(),
-        out_shape=jax.ShapeDtypeStruct(shape, jnp.float32),
+        out_specs=[vmem_spec()] * len(out_shape),
+        out_shape=out_shape,
         scratch_shapes=scratch,
         compiler_params=pltpu.CompilerParams(vmem_limit_bytes=VMEM_LIMIT),
         cost_estimate=pl.CostEstimate(
-            flops=10_000_000_000, bytes_accessed=4 * windows * ch_dev * columns + 4 * own_count * SPAN * F, transcendentals=0
+            flops=30_000_000_000, bytes_accessed=4 * windows * ch_dev * columns + 4 * own_count * SPAN * F, transcendentals=0
         ),
         name="cross",
     )(*operands)
@@ -465,8 +480,8 @@
     sums = None
     for n, (first, second) in enumerate(arrived):
         ends = tables if n == win_count - 1 else None
-        sums = cross_call(where, first, second, ch_dev, own_count, sums, ends, n == 0)
-    share = fold_call(where, incoming, flat, owners, ch_dev, tables, sums)
+        sums, *done = cross_call(where, first, second, ch_dev, own_count, sums, ends, n == 0)
+    share = fold_call(where, incoming, flat, owners, ch_dev, tables, done[0])
     fold = lax.dynamic_slice_in_dim(share, window_part * own_count, own_count, 0)
     for shift in range(1, win_count):
         target = (window_part + shift) % win_count * own_count

time: 100 us -> 67.6 us (0.68)
  the two profiles are of different devices: /device:TPU:13 before, /device:TPU:0 now
where the time goes in v3:
time: 67.6 us; the launch traced here: 66.8 us
  Pallas kernels  37.6 us (56%)
  starting transfers between devices  12.3 us (18%)
  waiting for transfers between devices  11.3 us (17%)
  local copies, waits for them, and re-layouts  3.88 us (6%)
  other arithmetic  0.91 us (1%)
  between operations  0.78 us (1%)
    pallas_call x2, Pallas kernels, cross_call(): pl.pallas_call(functools.partial(cross_kernel, last, with_sum, local_wind...  25.6 us
    ppermute x3, waiting for transfers between devices, round_win(): lax.ppermute(block, 'win', [(i, (i + shift) % count) for i in range(count)])  11.3 us
    pallas_call x1, Pallas kernels, spectra_call(): pl.pallas_call(spectra_kernel, in_specs=[anywhere, anywhere, vmem_spec()]...  7.77 us
    all_to_all x1, starting transfers between devices, local(): lax.all_to_all(outgoing, 'chan', split_axis=0, concat_axis=0, tiled=True)  6.55 us
    ppermute x3, starting transfers between devices, round_win(): lax.ppermute(block, 'win', [(i, (i + shift) % count) for i in range(count)])  4.48 us
    unnamed x14, local copies, waits for them, and re-layouts  3.06 us
    pallas_call x1, Pallas kernels, fold_call(): pl.pallas_call(fold_kernel, grid=(pairs,), in_specs=[smem_spec(), pl.Bloc...  2.37 us
    pallas_call x1, Pallas kernels, select_call(): pl.pallas_call(select_kernel, grid=(ROW_STEPS,), in_specs=[smem_spec(), p...  1.88 us
  transfers between devices with their start and end apart: 5, of which 2 were waited for; matrix products, arithmetic and copies ran while one was open for 2% of the time, Pallas kernels for 41%

profile of v3, /device:TPU:0, one launch (start us, length us, event | category | flops | bytes accessed | tf_op | source)
XLA Modules:
  0.0 66.8 jit_solution(2671936394376557662)
XLA Ops:
  0.6 0.0 copy-start.5
  0.6 0.6 copy-done.5
  1.3 0.0 copy-start.6
  1.3 1.2 %copy-done.6 = bf16[1024,512]{1,0:T(8,128)(2,1)S(1)} copy-done((bf16[1024,512]{1,0:T(8,128)(2,1)S(1)}, bf16[1024,512]{1,0:T(8,128)(2,1)}, u32[]{:S(2)}) %copy-start.6) | copy-done | bytes 1048600
  2.5 7.8 %spectra.1.whitened_ref.own_ref = bf16[768,512]{1,0:T(8,128)(2,1)S(1)} custom-call(bf16[768,4096]{1,0:T(8,128)(2,1)} %bitcast.14, bf16[1024,512]{1,0:T(8,128)(2,1)S(1)} %copy-done.6, s32[1,64]{1,0:T(1,128)S(1)} %bitcast.13), custom_call_target="tpu_custom_call" | custom-call | flops 3221225472 | bytes 6291456 | tf_op jit(solution)/shard_map/spectra/pallas_call | solution.py:213
  10.3 0.0 copy-start.3
  10.3 0.0 copy-start.4
  10.3 1.3 %collective-permute-start.1 = (bf16[12,64,512]{2,1,0:T(8,128)(2,1)S(1)}, bf16[12,64,512]{2,1,0:T(8,128)(2,1)S(1)}, u32[]{:S(2)}, u32[]{:S(2)}) collective-permute-start(bf16[12,64,512]{2,1,0:T(8,128)(2,1)S(1)} %bitcast.7), channel_id=1, source_target_pairs={{2,0},{4,2},{6,4},{8,6},{10,8},{12,10},{14,12},{16,14},{18,16},{20... | collective-permute-start | bytes 2359304 | tf_op jit(solution)/shard_map/ppermute | solution.py:447
  11.6 0.8 %fusion.1 = (bf16[12,32,512]{2,1,0:T(8,128)(2,1)S(1)}, bf16[12,32,512]{2,1,0:T(8,128)(2,1)}) fusion(bf16[12,64,512]{2,1,0:T(8,128)(2,1)S(1)} %bitcast.8), kind=kLoop, calls=%fused_computation.6 | loop fusion | bytes 1572864 | tf_op jit(solution)/shard_map/slice | solution.py:472
  12.4 2.9 %collective-permute-start = (bf16[12,32,512]{2,1,0:T(8,128)(2,1)}, bf16[12,32,512]{2,1,0:T(8,128)(2,1)}, u32[]{:S(2)}, u32[]{:S(2)}) collective-permute-start(bf16[12,32,512]{2,1,0:T(8,128)(2,1)} %get-tuple-element.7), channel_id=1, source_target_pairs={{0,1},{1,0},{2,3},{3,2},{4,5},{5,4},{6,7},{7,6},{8,9},{9,8},{10,11... | collective-permute-start | bytes 1179656 | tf_op jit(solution)/shard_map/ppermute | solution.py:452
  15.4 0.1 pad_add_fusion.where_ref
  15.4 0.0 copy-done.3
  15.4 0.0 copy-done.4
  15.4 1.9 %select.3 = bf16[16,96,512]{2,1,0:T(8,128)(2,1)S(1)} custom-call(s32[2]{0:T(128)S(1)} %pad_add_fusion.where_ref, bf16[768,512]{1,0:T(8,128)(2,1)S(1)} %spectra.1.whitened_ref.own_ref, s32[8,128]{1,0:T(8,128)S(1)} %bitcast.10, s32[8,128]{1,0:T(8,128)S(1)} %bitcast.12), custom_call_target="tpu_custom_call" | custom-call | flops 402653184 | bytes 2359296 | tf_op jit(solution)/shard_map/select/pallas_call | solution.py:235
  17.3 0.0 copy-start
  17.3 1.2 %copy-done = bf16[16,96,512]{2,1,0:T(8,128)(2,1)} copy-done((bf16[16,96,512]{2,1,0:T(8,128)(2,1)}, bf16[16,96,512]{2,1,0:T(8,128)(2,1)S(1)}, u32[]{:S(2)}) %copy-start) | copy-done | bytes 1572888
  18.5 6.6 %all-to-all-start = ((bf16[16,96,512]{2,1,0:T(8,128)(2,1)}), bf16[16,96,512]{2,1,0:T(8,128)(2,1)S(1)}, u32[]{:S(2)}, u32[]{:S(2)}) async-start(bf16[16,96,512]{2,1,0:T(8,128)(2,1)} %copy-done), calls=%async_computation | async-start | bytes 3145728 | tf_op jit(solution)/shard_map/all_to_all | solution.py:471
  25.1 0.0 collective-permute-done.1.second_ref
  25.1 0.2 fusion
  25.3 0.0 copy-start.1
  25.3 0.0 copy-start.2
  25.3 0.6 collective-permute-start.2
  25.9 11.0 %cross.2.refs_0_ = f32[32,72,256]{2,1,0:T(8,128)S(1)} custom-call(s32[2]{0:T(128)S(1)} %pad_add_fusion.where_ref, bf16[12,64,512]{2,1,0:T(8,128)(2,1)S(1)} %bitcast.9, bf16[12,64,512]{2,1,0:T(8,128)(2,1)S(1)} %collective-permute-done.1.second_ref), custom_call_target="tpu_custom_call" | custom-call | flops 30000001024 | bytes 3932160 | tf_op jit(solution)/shard_map/cross/pallas_call | solution.py:355
  37.0 0.0 collective-permute-done.first_ref
  37.0 8.2 %collective-permute-done.2.second_ref = bf16[12,64,512]{2,1,0:T(8,128)(2,1)S(1)} collective-permute-done((bf16[12,64,512]{2,1,0:T(8,128)(2,1)S(1)}, bf16[12,64,512]{2,1,0:T(8,128)(2,1)S(1)}, u32[]{:S(2)}, u32[]{:S(2)}) %collective-permute-start.2) | collective-permute-done | bytes 786464 | tf_op jit(solution)/shard_map/ppermute | solution.py:452
  45.2 0.0 copy-done.1
  45.2 0.0 copy-done.2
  45.2 14.5 %cross.3 = (f32[32,64,256]{2,1,0:T(8,128)}, f32[8,128]{1,0:T(8,128)S(1)}) custom-call(s32[2]{0:T(128)S(1)} %pad_add_fusion.where_ref, bf16[12,32,512]{2,1,0:T(8,128)(2,1)} %collective-permute-done.first_ref, bf16[12,64,512]{2,1,0:T(8,128)(2,1)S(1)} %collective-permute-done.2.second_ref, f32[32,72,256]{2,1,0:T(8,128)S(1)} %cross.2.refs_0_, ...), custom_call_target="tpu_custom_call" | custom-call | flops 30000001024 | bytes 3932160 | tf_op jit(solution)/shard_map/cross/pallas_call | solution.py:355
  59.8 0.0 all-to-all-done.incoming_ref
  59.8 2.4 %fold.1 = f32[64,256]{1,0:T(8,128)S(1)} custom-call(s32[2]{0:T(128)S(1)} %pad_add_fusion.where_ref, bf16[16,96,512]{2,1,0:T(8,128)(2,1)S(1)} %all-to-all-done.incoming_ref, bf16[768,512]{1,0:T(8,128)(2,1)S(1)} %spectra.1.whitened_ref.own_ref, s32[8,128]{1,0:T(8,128)S(1)} %bitcast.11, bf16[256,256]{1,0:T(8,128)(2,1)S(1)} %copy-done.2, ...), custom_call_target="tpu_custom_call" | custom-call | flops 201326592 | bytes 2359296 | tf_op jit(solution)/shard_map/fold/pallas_call | solution.py:417
  62.2 0.9 %collective-permute-start.3 = (f32[32,256]{1,0:T(8,128)S(1)}, f32[32,256]{1,0:T(8,128)S(1)}, u32[]{:S(2)}, u32[]{:S(2)}) collective-permute-start(f32[32,256]{1,0:T(8,128)S(1)} %constant_dynamic-slice_fusion), channel_id=1, source_target_pairs={{0,1},{1,0},{2,3},{3,2},{4,5},{5,4},{6,7},{7,6},{8,9},{9,8},{10,11... | collective-permute-start | bytes 98312 | tf_op jit(solution)/shard_map/ppermute | solution.py:452
  63.1 3.0 %collective-permute-done.3 = f32[32,256]{1,0:T(8,128)S(1)} collective-permute-done((f32[32,256]{1,0:T(8,128)S(1)}, f32[32,256]{1,0:T(8,128)S(1)}, u32[]{:S(2)}, u32[]{:S(2)}) %collective-permute-start.3) | collective-permute-done | bytes 32800 | tf_op jit(solution)/shard_map/ppermute | solution.py:452
  66.2 0.6 dynamic-slice_add_fusion
  (1 shorter events, 0.0 us)
Async XLA Ops:
  0.6 0.7 copy-start.5
  1.3 1.2 %copy-start.6 = (bf16[1024,512]{1,0:T(8,128)(2,1)S(1)}, bf16[1024,512]{1,0:T(8,128)(2,1)}, u32[]{:S(2)}) copy-start(bf16[1024,512]{1,0:T(8,128)(2,1)} %constant.39.clone.table_ref) | copy-start | bytes 3145732
  10.3 5.1 %copy-start.3 = (s32[1024,1]{0,1:T(1,128)S(1)}, s32[1024,1]{0,1:T(1,128)}, u32[]{:S(2)}) copy-start(s32[1024,1]{0,1:T(1,128)} %param.9) | copy-start | bytes 12292
  10.3 5.1 %copy-start.4 = (s32[1024]{0:T(1024)S(1)}, s32[1024]{0:T(1024)}, u32[]{:S(2)}) copy-start(s32[1024]{0:T(1024)} %param.10) | copy-start | bytes 12292
  10.3 14.8 %collective-permute-start.1 = (bf16[12,64,512]{2,1,0:T(8,128)(2,1)S(1)}, bf16[12,64,512]{2,1,0:T(8,128)(2,1)S(1)}, u32[]{:S(2)}, u32[]{:S(2)}) collective-permute-start(bf16[12,64,512]{2,1,0:T(8,128)(2,1)S(1)} %bitcast.7), channel_id=1, source_target_pairs={{2,0},{4,2},{6,4},{8,6},{10,8},{12,10},{14,12},{16,14},{18,16},{20... | collective-permute-start | bytes 2359304 | tf_op jit(solution)/shard_map/ppermute | solution.py:447
  12.4 24.6 %collective-permute-start = (bf16[12,32,512]{2,1,0:T(8,128)(2,1)}, bf16[12,32,512]{2,1,0:T(8,128)(2,1)}, u32[]{:S(2)}, u32[]{:S(2)}) collective-permute-start(bf16[12,32,512]{2,1,0:T(8,128)(2,1)} %get-tuple-element.7), channel_id=1, source_target_pairs={{0,1},{1,0},{2,3},{3,2},{4,5},{5,4},{6,7},{7,6},{8,9},{9,8},{10,11... | collective-permute-start | bytes 1179656 | tf_op jit(solution)/shard_map/ppermute | solution.py:452
  17.3 1.2 %copy-start = (bf16[16,96,512]{2,1,0:T(8,128)(2,1)}, bf16[16,96,512]{2,1,0:T(8,128)(2,1)S(1)}, u32[]{:S(2)}) copy-start(bf16[16,96,512]{2,1,0:T(8,128)(2,1)S(1)} %select.3) | copy-start | bytes 4718596
  18.5 41.3 %all-to-all-start = ((bf16[16,96,512]{2,1,0:T(8,128)(2,1)}), bf16[16,96,512]{2,1,0:T(8,128)(2,1)S(1)}, u32[]{:S(2)}, u32[]{:S(2)}) async-start(bf16[16,96,512]{2,1,0:T(8,128)(2,1)} %copy-done), calls=%async_computation | async-start | bytes 3145728 | tf_op jit(solution)/shard_map/all_to_all | solution.py:471
  25.3 19.9 %copy-start.1 = (bf16[256,256]{1,0:T(8,128)(2,1)S(1)}, bf16[256,256]{1,0:T(8,128)(2,1)}, u32[]{:S(2)}) copy-start(bf16[256,256]{1,0:T(8,128)(2,1)} %constant.38.clone.refs_2_.low_ref) | copy-start | bytes 393220
  25.3 19.9 %copy-start.2 = (bf16[256,256]{1,0:T(8,128)(2,1)S(1)}, bf16[256,256]{1,0:T(8,128)(2,1)}, u32[]{:S(2)}) copy-start(bf16[256,256]{1,0:T(8,128)(2,1)} %constant.37.clone.refs_1_.high_ref) | copy-start | bytes 393220
  25.3 19.9 %collective-permute-start.2 = (bf16[12,64,512]{2,1,0:T(8,128)(2,1)S(1)}, bf16[12,64,512]{2,1,0:T(8,128)(2,1)S(1)}, u32[]{:S(2)}, u32[]{:S(2)}) collective-permute-start(bf16[12,64,512]{2,1,0:T(8,128)(2,1)S(1)} %fusion), channel_id=1, source_target_pairs={{0,1},{1,0},{2,3},{3,2},{4,5},{5,4},{6,7},{7,6},{8,9},{9,8},{10,11... | collective-permute-start | bytes 2359304 | tf_op jit(solution)/shard_map/ppermute | solution.py:452
  62.2 4.0 %collective-permute-start.3 = (f32[32,256]{1,0:T(8,128)S(1)}, f32[32,256]{1,0:T(8,128)S(1)}, u32[]{:S(2)}, u32[]{:S(2)}) collective-permute-start(f32[32,256]{1,0:T(8,128)S(1)} %constant_dynamic-slice_fusion), channel_id=1, source_target_pairs={{0,1},{1,0},{2,3},{3,2},{4,5},{5,4},{6,7},{7,6},{8,9},{9,8},{10,11... | collective-permute-start | bytes 98312 | tf_op jit(solution)/shard_map/ppermute | solution.py:452

commit v4 on v3

--- a/solution.py
+++ b/solution.py
@@ -15,7 +15,8 @@
 NLAG = 256
 REACH = 64
 CAP = 8
-SPAN = REACH + 8
+SPAN = REACH + 16
+FLUSH = 4
 smooth_reach = 4
 ROW_STEPS = 3
 QUARTERS = 4
@@ -128,9 +129,9 @@
     )
 
 
-def spectra_kernel(traces_ref, table_ref, quality_ref, whitened_ref, traces, table, sems):
+def spectra_kernel(traces_ref, table_ref, quality_ref, whitened_ref, traces, table, quality, sems):
     row_parts, chunks, rows, depth = traces.shape
-    ch_dev = quality_ref.shape[1]
+    ch_dev = quality.shape[1]
 
     def traces_copy(part, k):
         source = traces_ref.at[pl.ds(part * rows, rows), pl.ds(k * depth, depth)]
@@ -138,14 +139,17 @@
 
     table_copy = pltpu.make_async_copy(table_ref, table, sems.at[row_parts, 0])
     table_copy.start()
+    quality_copy = pltpu.make_async_copy(quality_ref, quality, sems.at[row_parts, 1])
+    quality_copy.start()
     for part in range(row_parts):
         for k in range(chunks):
             traces_copy(part, k).start()
 
     band = band_matrix()
+    quality_copy.wait()
     shape = (rows, ch_dev)
     keep = jnp.sum(
-        jnp.where(rows_of(shape) % ch_dev == lanes_of(shape), quality_ref[...].astype(jnp.float32), 0.0),
+        jnp.where(rows_of(shape) % ch_dev == lanes_of(shape), quality[...].astype(jnp.float32), 0.0),
         axis=1, keepdims=True,
     )
 
@@ -179,8 +183,11 @@
     lax.fori_loop(0, row_parts, whiten, 0)
 
 
-def select_kernel(where_ref, whitened_ref, owners_ref, places_ref, outgoing_ref, selector):
+def select_kernel(where_ref, whitened_ref, owners_ref, places_ref, outgoing_ref, common_ref, selector):
     rows = selector.shape[1]
+    ch_dev, shared = rows // 2, rows // 2 - common_ref.shape[1]
+    for w in range(common_ref.shape[0]):
+        common_ref[w] = whitened_ref[ch_dev * w + shared : ch_dev * (w + 1), :]
 
     @pl.when(pl.program_id(0) == 0)
     def _():
@@ -212,12 +219,13 @@
     anywhere = pl.BlockSpec(memory_space=pl.ANY)
     return pl.pallas_call(
         spectra_kernel,
-        in_specs=[anywhere, anywhere, vmem_spec()],
+        in_specs=[anywhere, anywhere, anywhere],
         out_specs=vmem_spec(),
         out_shape=jax.ShapeDtypeStruct((rows, 2 * F), jnp.bfloat16),
         scratch_shapes=[
             pltpu.VMEM((ROW_STEPS, QUARTERS, part, depth), jnp.bfloat16),
             pltpu.VMEM((depth, 2 * F), jnp.bfloat16),
+            pltpu.VMEM(quality.shape, jnp.int32),
             pltpu.SemaphoreType.DMA((ROW_STEPS + 1, QUARTERS)),
         ],
         compiler_params=pltpu.CompilerParams(vmem_limit_bytes=SPECTRA_VMEM_LIMIT),
@@ -228,7 +236,7 @@
     )(traces, jnp.asarray(forward_table(length)), quality)
 
 
-def select_call(where, whitened, owners, places, chan_count, ch_dev):
+def select_call(where, whitened, owners, places, chan_count, ch_dev, own_count):
     rows, columns = whitened.shape
     block = rows // ROW_STEPS
     slots = block // (2 * ch_dev) * 2 * CAP
@@ -236,8 +244,14 @@
         select_kernel,
         grid=(ROW_STEPS,),
         in_specs=[smem_spec(), pl.BlockSpec((block, columns), lambda s: (s, 0)), whole(owners), whole(places)],
-        out_specs=pl.BlockSpec((chan_count, slots, columns), lambda s: (0, s, 0)),
-        out_shape=jax.ShapeDtypeStruct((chan_count, ROW_STEPS * slots, columns), jnp.bfloat16),
+        out_specs=[
+            pl.BlockSpec((chan_count, slots, columns), lambda s: (0, s, 0)),
+            pl.BlockSpec((block // ch_dev, own_count, columns), lambda s: (s, 0, 0)),
+        ],
+        out_shape=[
+            jax.ShapeDtypeStruct((chan_count, ROW_STEPS * slots, columns), jnp.bfloat16),
+            jax.ShapeDtypeStruct((rows // ch_dev, own_count, columns), jnp.bfloat16),
+        ],
         scratch_shapes=[pltpu.VMEM((chan_count * 2 * CAP, 2 * ch_dev), jnp.bfloat16)],
         compiler_params=pltpu.CompilerParams(vmem_limit_bytes=SPECTRA_VMEM_LIMIT),
         cost_estimate=pl.CostEstimate(
@@ -251,111 +265,131 @@
     refs = list(refs)
     sum_ref = refs.pop(0) if with_sum else None
     if last:
-        high_ref, low_ref, out_ref, done_ref, wide, spread, total = refs
+        table_ref, out_ref, done_ref, wide, spread, staged, lags, total, sems = refs
         done_ref[...] = jnp.zeros_like(done_ref)
     else:
-        out_ref, wide, spread = refs
-        total = out_ref
+        total, wide, spread, staged = refs
     windows, own_count = spread.shape[:2]
     ch_dev = wide.shape[1] // 2
     base = pl.multiple_of(where_ref[1] * own_count, 8)
 
     def widen(w, carry):
         if local_windows:
-            wide[w, :ch_dev, :] = first_ref[w].astype(jnp.float32)
-            wide[w, ch_dev:, :] = second_ref[w].astype(jnp.float32)
+            wide[w, :ch_dev, :] = first_ref[w]
+            wide[w, ch_dev:, :] = second_ref[w]
         else:
             shared = ch_dev - own_count
-            wide[w, shared:ch_dev, :] = first_ref[w].astype(jnp.float32)
-            rows = second_ref[w].astype(jnp.float32)
-            for tile in range(ch_dev // 8):
-                at = base + 8 * tile
-                at = pl.multiple_of(jnp.where(at < shared, at, at + own_count), 8)
-                wide[w, pl.ds(at, 8), :] = rows[8 * tile : 8 * tile + 8]
-        for tile in range(own_count // 8):
-            rows = wide[w, pl.ds(pl.multiple_of(base + 8 * tile, 8), 8), :]
+            if own_count % 16 == 0:
+                height, rows, place = 16, wide.at[w], second_ref.at[w]
+                wide[w, shared:ch_dev, :] = first_ref[w]
+            else:
+                height, rows, place = 8, staged, second_ref[w].astype(jnp.float32)
+                staged[shared:ch_dev, :] = first_ref[w].astype(jnp.float32)
+            for tile in range(ch_dev // height):
+                at = base + height * tile
+                at = pl.multiple_of(jnp.where(at < shared, at, at + own_count), height)
+                rows[pl.ds(at, height), :] = place[height * tile : height * (tile + 1), :]
+            if own_count % 16:
+                wide[w] = staged[...].astype(jnp.bfloat16)
+        for eight in range(own_count // 8):
+            at = base + 8 * eight
+            rows = wide[w, pl.ds(pl.multiple_of(at // 16 * 16, 16), 16), :].astype(jnp.float32)
+            rows = jnp.where(at % 16 == 0, rows[:8], rows[8:])
             for i in range(8):
                 for q in range(4):
-                    spread[w, 8 * tile + i, q] = jnp.broadcast_to(rows[i : i + 1, q * H : (q + 1) * H], (8, H))
+                    row = jnp.broadcast_to(rows[i : i + 1, q * H : (q + 1) * H], (16, H))
+                    spread[w, 8 * eight + i, q] = row.astype(jnp.bfloat16)
         return carry
 
     lax.fori_loop(0, windows, widen, 0)
 
-    group, tiles = 4, 3
-    rounds = SPAN // (8 * tiles)
+    group = 4
+    rounds = SPAN // 16
 
     def block(index, carry):
         g = index // rounds
         j = index % rounds
-        start = pl.multiple_of(base + 8 * (g // 2) + 8 * tiles * j, 8)
-
-        def add_window(w, sums):
-            sums = list(sums)
-            right = [
-                [wide[w, pl.ds(pl.multiple_of(start + 8 * t, 8), 8), q * H : (q + 1) * H] for q in range(4)]
-                for t in range(tiles)
-            ]
-            for i in range(group):
-                left = [spread[w, group * g + i, q] for q in range(4)]
-                for t in range(tiles):
-                    at = 3 * (i * tiles + t)
-                    r = right[t]
-                    sums[at] = sums[at] + (left[0] * r[0] + left[1] * r[1])
-                    sums[at + 1] = sums[at + 1] + (left[2] * r[2] + left[3] * r[3])
-                    sums[at + 2] = sums[at + 2] + ((left[1] * r[0] - left[0] * r[1]) + (left[2] * r[3] - left[3] * r[2]))
-            return tuple(sums)
-
-        zero = jnp.zeros((8, H), jnp.float32)
-        sums = lax.fori_loop(0, windows, add_window, (zero,) * (3 * group * tiles), unroll=2)
+        start = pl.multiple_of((base + group * g) // 16 * 16 + 16 * j, 16)
+
+        def add_windows(part, sums):
+            short = [None] * (3 * group)
+            for n in range(FLUSH):
+                w = part * FLUSH + n
+                r = [wide[w, pl.ds(start, 16), q * H : (q + 1) * H] for q in range(4)]
+                for i in range(group):
+                    l = [spread[w, group * g + i, q] for q in range(4)]
+                    terms = (
+                        l[0] * r[0] + l[1] * r[1],
+                        l[2] * r[2] + l[3] * r[3],
+                        (l[1] * r[0] - l[0] * r[1]) + (l[2] * r[3] - l[3] * r[2]),
+                    )
+                    for k in range(3):
+                        at = 3 * i + k
+                        short[at] = terms[k] if n == 0 else short[at] + terms[k]
+            return tuple(total + term.astype(jnp.float32) for total, term in zip(sums, short))
+
+        zero = jnp.zeros((16, H), jnp.float32)
+        sums = lax.fori_loop(0, windows // FLUSH, add_windows, (zero,) * (3 * group))
         for i in range(group):
-            for t in range(tiles):
-                at = 3 * (i * tiles + t)
-                real, imag = fold_columns(sums[at], sums[at + 1], sums[at + 2])
-                where = pl.ds(pl.multiple_of(8 * tiles * j + 8 * t, 8), 8)
-                if with_sum:
-                    real = real + sum_ref[group * g + i, where, :H]
-                    imag = imag + sum_ref[group * g + i, where, H:]
-                total[group * g + i, where, :H] = real
-                total[group * g + i, where, H:] = imag
+            real, imag = fold_columns(*sums[3 * i : 3 * i + 3])
+            where = pl.ds(pl.multiple_of(16 * j, 16), 16)
+            if with_sum:
+                real = real + sum_ref[group * g + i, where, :H]
+                imag = imag + sum_ref[group * g + i, where, H:]
+            total[group * g + i, where, :H] = real
+            total[group * g + i, where, H:] = imag
         return carry
 
     lax.fori_loop(0, own_count // group * rounds, block, 0)
 
     if last:
-
-        def finish(eight, carry):
-            first = pl.multiple_of(8 * eight, 8)
-            stacks = total[pl.ds(first, 8)].reshape(8 * SPAN, F)
-            lagged = lag_transform(stacks, high_ref[...], low_ref[...]).reshape(8, SPAN, NLAG)
+        copies = []
+        height = REACH + 8
+        for eight in range(own_count // 8):
+            first = 8 * eight
+            skip = pl.multiple_of((base + first) % 16, 8)
+            stacks = total[first : first + 8, pl.ds(skip, height), :].reshape(8 * height, F)
+            lagged = jnp.dot(stacks.astype(jnp.bfloat16), table_ref[...], preferred_element_type=jnp.float32)
+            lagged = lagged.reshape(8, height, NLAG)
             for i in range(8):
-                out_ref[first + i] = lagged[i, i + 1 : i + 1 + REACH, :]
-            return carry
-
-        lax.fori_loop(0, own_count // 8, finish, 0)
-
-
-def cross_call(where, first, second, ch_dev, own_count, sums, tables, local_windows):
+                lags[first + i] = lagged[i, i + 1 : i + 1 + REACH, :]
+            some = pl.ds(first, 8)
+            copies.append(pltpu.make_async_copy(lags.at[some], out_ref.at[some], sems.at[eight]))
+            copies[-1].start()
+        for copy in copies:
+            copy.wait()
+
+
+def cross_call(where, first, second, ch_dev, own_count, sums, table, local_windows):
     windows, _, columns = first.shape
-    last = tables is not None
+    last = table is not None
     with_sum = sums is not None
     operands = [where, first, second]
     if with_sum:
         operands.append(sums)
     scratch = [
-        pltpu.VMEM((windows, 2 * ch_dev, columns), jnp.float32),
-        pltpu.VMEM((windows, own_count, 4, 8, H), jnp.float32),
+        pltpu.VMEM((windows, 2 * ch_dev, columns), jnp.bfloat16),
+        pltpu.VMEM((windows, own_count, 4, 16, H), jnp.bfloat16),
+        pltpu.VMEM((2 * ch_dev, columns), jnp.float32),
     ]
+    sums_shape = (own_count, SPAN, F)
     if last:
-        operands += list(tables)
-        scratch.append(pltpu.VMEM((own_count, SPAN, F), jnp.float32))
-    shape = (own_count, REACH, NLAG) if last else (own_count, SPAN, F)
-    out_shape = [jax.ShapeDtypeStruct(shape, jnp.float32)]
-    if last:
-        out_shape.append(jax.ShapeDtypeStruct((8, H), jnp.float32))
+        operands.append(table)
+        lags_shape = (own_count, REACH, NLAG)
+        scratch += [
+            pltpu.VMEM(lags_shape, jnp.float32),
+            pltpu.VMEM(sums_shape, jnp.float32),
+            pltpu.SemaphoreType.DMA((own_count // 8,)),
+        ]
+        out_shape = [jax.ShapeDtypeStruct(lags_shape, jnp.float32), jax.ShapeDtypeStruct((8, H), jnp.float32)]
+        out_specs = [pl.BlockSpec(memory_space=pl.ANY), vmem_spec()]
+    else:
+        out_shape = [jax.ShapeDtypeStruct(sums_shape, jnp.float32)]
+        out_specs = [vmem_spec()]
     return pl.pallas_call(
         functools.partial(cross_kernel, last, with_sum, local_windows),
         in_specs=[smem_spec()] + [vmem_spec()] * (len(operands) - 1),
-        out_specs=[vmem_spec()] * len(out_shape),
+        out_specs=out_specs,
         out_shape=out_shape,
         scratch_shapes=scratch,
         compiler_params=pltpu.CompilerParams(vmem_limit_bytes=VMEM_LIMIT),
@@ -466,8 +500,8 @@
     flat = spectra_call(traces.reshape(win_dev * ch_dev, length), quality.reshape(1, ch_dev))
     whitened = flat.reshape(win_dev, ch_dev, 2 * F)
     upper = from_above(whitened)
-    common = [round_win(whitened[:, shared:], shift) for shift in range(1, win_count)]
-    outgoing = select_call(where, flat, owners, places, chan_count, ch_dev)
+    outgoing, shared_rows = select_call(where, flat, owners, places, chan_count, ch_dev, own_count)
+    common = [round_win(shared_rows, shift) for shift in range(1, win_count)]
     incoming = lax.all_to_all(outgoing, "chan", split_axis=0, concat_axis=0, tiled=True)
     offered = jnp.concatenate([whitened[:, :shared], upper], axis=1)
     special = [
@@ -479,7 +513,7 @@
     arrived = [(whitened, upper)] + list(zip(common, special))
     sums = None
     for n, (first, second) in enumerate(arrived):
-        ends = tables if n == win_count - 1 else None
+        ends = tables[0] if n == win_count - 1 else None
         sums, *done = cross_call(where, first, second, ch_dev, own_count, sums, ends, n == 0)
     share = fold_call(where, incoming, flat, owners, ch_dev, tables, done[0])
     fold = lax.dynamic_slice_in_dim(share, window_part * own_count, own_count, 0)

time: 67.6 us -> 74.3 us (1.099)
  waiting for transfers between devices: 11.3 us -> 16.1 us
  Pallas kernels: 37.6 us -> 40 us
  starting transfers between devices: 12.3 us -> 13.2 us
  local copies, waits for them, and re-layouts: 3.88 us -> 3.1 us
    ppermute x3, waiting for transfers between devices: 11.3 us -> 16.1 us  [round_win(): lax.ppermute(block, 'win', [(i, (i + shift) % count) for i in range(count)])]
    all_to_all x1, starting transfers between devices: 6.55 us -> 8.16 us  [local(): lax.all_to_all(outgoing, 'chan', split_axis=0, concat_axis=0, tiled=True)]
    pallas_call x2, Pallas kernels: 25.6 us -> 27 us  [cross_call(): pl.pallas_call(functools.partial(cross_kernel, last, with_sum, local_wind...]
    pallas_call x1, Pallas kernels: 1.88 us -> 2.85 us  [select_call(): pl.pallas_call(select_kernel, grid=(ROW_STEPS,), in_specs=[smem_spec(), p...]
    slice x1, local copies, waits for them, and re-layouts: 0.8 us -> 0.03 us  [local(): offered = jnp.concatenate([whitened[:, :shared], upper], axis=1)]
    ppermute x3, starting transfers between devices: 4.48 us -> 3.71 us  [round_win(): lax.ppermute(block, 'win', [(i, (i + shift) % count) for i in range(count)])]
  transfers between devices with their start and end apart: 5 -> 5, of which waited for: 2 -> 2; matrix products, arithmetic and copies ran while one was open for 2% -> 0% of each run, Pallas kernels for 41% -> 40%
where the time goes in v4:
time: 74.3 us; the launch traced here: 74 us
  Pallas kernels  40 us (54%)
  waiting for transfers between devices  16.1 us (22%)
  starting transfers between devices  13.2 us (18%)
  local copies, waits for them, and re-layouts  3.1 us (4%)
  other arithmetic  0.9 us (1%)
  between operations  0.78 us (1%)
    pallas_call x2, Pallas kernels, cross_call(): pl.pallas_call(functools.partial(cross_kernel, last, with_sum, local_wind...  27 us
    ppermute x3, waiting for transfers between devices, round_win(): lax.ppermute(block, 'win', [(i, (i + shift) % count) for i in range(count)])  16.1 us
    all_to_all x1, starting transfers between devices, local(): lax.all_to_all(outgoing, 'chan', split_axis=0, concat_axis=0, tiled=True)  8.16 us
    pallas_call x1, Pallas kernels, spectra_call(): pl.pallas_call(spectra_kernel, in_specs=[anywhere, anywhere, anywhere], o...  7.73 us
    ppermute x3, starting transfers between devices, round_win(): lax.ppermute(block, 'win', [(i, (i + shift) % count) for i in range(count)])  3.71 us
    unnamed x14, local copies, waits for them, and re-layouts  3.06 us
    pallas_call x1, Pallas kernels, select_call(): pl.pallas_call(select_kernel, grid=(ROW_STEPS,), in_specs=[smem_spec(), p...  2.85 us
    pallas_call x1, Pallas kernels, fold_call(): pl.pallas_call(fold_kernel, grid=(pairs,), in_specs=[smem_spec(), pl.Bloc...  2.4 us
  transfers between devices with their start and end apart: 5, of which 2 were waited for; matrix products, arithmetic and copies ran while one was open for 0% of the time, Pallas kernels for 40%

profile of v4, /device:TPU:0, one launch (start us, length us, event | category | flops | bytes accessed | tf_op | source)
XLA Modules:
  0.0 74.0 jit_solution(9255889478910276482)
XLA Ops:
  0.6 0.0 copy-start.5
  0.6 0.6 copy-done.5
  1.3 0.0 copy-start.6
  1.3 1.2 %copy-done.6 = bf16[1024,512]{1,0:T(8,128)(2,1)S(1)} copy-done((bf16[1024,512]{1,0:T(8,128)(2,1)S(1)}, bf16[1024,512]{1,0:T(8,128)(2,1)}, u32[]{:S(2)}) %copy-start.6) | copy-done | bytes 1048600
  2.5 0.0 copy-start.3
  2.5 0.0 copy-start.4
  2.5 7.7 %spectra.1.whitened_ref.own_ref = bf16[768,512]{1,0:T(8,128)(2,1)S(1)} custom-call(bf16[768,4096]{1,0:T(8,128)(2,1)} %bitcast.14, bf16[1024,512]{1,0:T(8,128)(2,1)S(1)} %copy-done.6, s32[1,64]{1,0:T(1,128)S(1)} %bitcast.13), custom_call_target="tpu_custom_call" | custom-call | flops 3221225472 | bytes 6291456 | tf_op jit(solution)/shard_map/spectra/pallas_call | solution.py:220
  10.3 1.3 %collective-permute-start.1 = (bf16[12,64,512]{2,1,0:T(8,128)(2,1)S(1)}, bf16[12,64,512]{2,1,0:T(8,128)(2,1)S(1)}, u32[]{:S(2)}, u32[]{:S(2)}) collective-permute-start(bf16[12,64,512]{2,1,0:T(8,128)(2,1)S(1)} %bitcast.7), channel_id=1, source_target_pairs={{2,0},{4,2},{6,4},{8,6},{10,8},{12,10},{14,12},{16,14},{18,16},{20... | collective-permute-start | bytes 2359304 | tf_op jit(solution)/shard_map/ppermute | solution.py:481
  11.6 0.1 pad_add_fusion.where_ref
  11.6 0.0 copy-done.3
  11.6 0.0 copy-done.4
  11.6 2.9 %select.3 = (bf16[16,96,512]{2,1,0:T(8,128)(2,1)S(1)}, bf16[12,32,512]{2,1,0:T(8,128)(2,1)}) custom-call(s32[2]{0:T(128)S(1)} %pad_add_fusion.where_ref, bf16[768,512]{1,0:T(8,128)(2,1)S(1)} %spectra.1.whitened_ref.own_ref, s32[8,128]{1,0:T(8,128)S(1)} %bitcast.10, s32[8,128]{1,0:T(8,128)S(1)} %bitcast.12), custom_call_target="tpu_custom_call" | custom-call | flops 402653184 | bytes 2359296 | tf_op jit(solution)/shard_map/select/pallas_call | solution.py:243
  14.5 0.0 copy-start
  14.5 1.2 %copy-done = bf16[16,96,512]{2,1,0:T(8,128)(2,1)} copy-done((bf16[16,96,512]{2,1,0:T(8,128)(2,1)}, bf16[16,96,512]{2,1,0:T(8,128)(2,1)S(1)}, u32[]{:S(2)}) %copy-start) | copy-done | bytes 1572888
  15.7 8.2 %all-to-all-start = ((bf16[16,96,512]{2,1,0:T(8,128)(2,1)}), bf16[16,96,512]{2,1,0:T(8,128)(2,1)S(1)}, u32[]{:S(2)}, u32[]{:S(2)}) async-start(bf16[16,96,512]{2,1,0:T(8,128)(2,1)} %copy-done), calls=%async_computation | async-start | bytes 3145728 | tf_op jit(solution)/shard_map/all_to_all | solution.py:505
  23.8 1.6 %collective-permute-start = (bf16[12,32,512]{2,1,0:T(8,128)(2,1)}, bf16[12,32,512]{2,1,0:T(8,128)(2,1)}, u32[]{:S(2)}, u32[]{:S(2)}) collective-permute-start(bf16[12,32,512]{2,1,0:T(8,128)(2,1)} %get-tuple-element.6), channel_id=1, source_target_pairs={{0,1},{1,0},{2,3},{3,2},{4,5},{5,4},{6,7},{7,6},{8,9},{9,8},{10,11... | collective-permute-start | bytes 1179656 | tf_op jit(solution)/shard_map/ppermute | solution.py:486
  25.4 0.0 collective-permute-done.1.second_ref
  25.5 0.2 fusion
  25.7 0.0 copy-start.1
  25.7 0.6 collective-permute-start.2
  26.3 12.4 %cross.2.refs_0_ = f32[32,80,256]{2,1,0:T(8,128)S(1)} custom-call(s32[2]{0:T(128)S(1)} %pad_add_fusion.where_ref, bf16[12,64,512]{2,1,0:T(8,128)(2,1)S(1)} %bitcast.9, bf16[12,64,512]{2,1,0:T(8,128)(2,1)S(1)} %collective-permute-done.1.second_ref), custom_call_target="tpu_custom_call" | custom-call | flops 30000001024 | bytes 4194304 | tf_op jit(solution)/shard_map/cross/pallas_call | solution.py:389
  38.7 0.0 copy-start.2
  38.7 0.0 collective-permute-done.first_ref
  38.7 13.6 %collective-permute-done.2.second_ref = bf16[12,64,512]{2,1,0:T(8,128)(2,1)S(1)} collective-permute-done((bf16[12,64,512]{2,1,0:T(8,128)(2,1)S(1)}, bf16[12,64,512]{2,1,0:T(8,128)(2,1)S(1)}, u32[]{:S(2)}, u32[]{:S(2)}) %collective-permute-start.2) | collective-permute-done | bytes 786464 | tf_op jit(solution)/shard_map/ppermute | solution.py:486
  52.3 0.0 copy-done.1
  52.3 14.6 %cross.3 = (f32[32,64,256]{2,1,0:T(8,128)}, f32[8,128]{1,0:T(8,128)S(1)}) custom-call(s32[2]{0:T(128)S(1)} %pad_add_fusion.where_ref, bf16[12,32,512]{2,1,0:T(8,128)(2,1)} %collective-permute-done.first_ref, bf16[12,64,512]{2,1,0:T(8,128)(2,1)S(1)} %collective-permute-done.2.second_ref, f32[32,80,256]{2,1,0:T(8,128)S(1)} %cross.2.refs_0_, ...), custom_call_target="tpu_custom_call" | custom-call | flops 30000001024 | bytes 4194304 | tf_op jit(solution)/shard_map/cross/pallas_call | solution.py:389
  67.0 0.0 all-to-all-done.incoming_ref
  67.0 0.0 copy-done.2
  67.0 2.4 %fold.1 = f32[64,256]{1,0:T(8,128)S(1)} custom-call(s32[2]{0:T(128)S(1)} %pad_add_fusion.where_ref, bf16[16,96,512]{2,1,0:T(8,128)(2,1)S(1)} %all-to-all-done.incoming_ref, bf16[768,512]{1,0:T(8,128)(2,1)S(1)} %spectra.1.whitened_ref.own_ref, s32[8,128]{1,0:T(8,128)S(1)} %bitcast.11, bf16[256,256]{1,0:T(8,128)(2,1)S(1)} %copy-done.1, ...), custom_call_target="tpu_custom_call" | custom-call | flops 201326592 | bytes 2359296 | tf_op jit(solution)/shard_map/fold/pallas_call | solution.py:451
  69.4 1.5 %collective-permute-start.3 = (f32[32,256]{1,0:T(8,128)S(1)}, f32[32,256]{1,0:T(8,128)S(1)}, u32[]{:S(2)}, u32[]{:S(2)}) collective-permute-start(f32[32,256]{1,0:T(8,128)S(1)} %constant_dynamic-slice_fusion), channel_id=1, source_target_pairs={{0,1},{1,0},{2,3},{3,2},{4,5},{5,4},{6,7},{7,6},{8,9},{9,8},{10,11... | collective-permute-start | bytes 98312 | tf_op jit(solution)/shard_map/ppermute | solution.py:486
  71.0 2.4 %collective-permute-done.3 = f32[32,256]{1,0:T(8,128)S(1)} collective-permute-done((f32[32,256]{1,0:T(8,128)S(1)}, f32[32,256]{1,0:T(8,128)S(1)}, u32[]{:S(2)}, u32[]{:S(2)}) %collective-permute-start.3) | collective-permute-done | bytes 32800 | tf_op jit(solution)/shard_map/ppermute | solution.py:486
  73.4 0.6 dynamic-slice_add_fusion
  (2 shorter events, 0.0 us)
Async XLA Ops:
  0.6 0.7 copy-start.5
  1.3 1.2 %copy-start.6 = (bf16[1024,512]{1,0:T(8,128)(2,1)S(1)}, bf16[1024,512]{1,0:T(8,128)(2,1)}, u32[]{:S(2)}) copy-start(bf16[1024,512]{1,0:T(8,128)(2,1)} %constant.39.clone.table_ref) | copy-start | bytes 3145732
  2.5 9.1 %copy-start.3 = (s32[1024,1]{0,1:T(1,128)S(1)}, s32[1024,1]{0,1:T(1,128)}, u32[]{:S(2)}) copy-start(s32[1024,1]{0,1:T(1,128)} %param.9) | copy-start | bytes 12292
  2.5 9.1 %copy-start.4 = (s32[1024]{0:T(1024)S(1)}, s32[1024]{0:T(1024)}, u32[]{:S(2)}) copy-start(s32[1024]{0:T(1024)} %param.10) | copy-start | bytes 12292
  10.3 15.2 %collective-permute-start.1 = (bf16[12,64,512]{2,1,0:T(8,128)(2,1)S(1)}, bf16[12,64,512]{2,1,0:T(8,128)(2,1)S(1)}, u32[]{:S(2)}, u32[]{:S(2)}) collective-permute-start(bf16[12,64,512]{2,1,0:T(8,128)(2,1)S(1)} %bitcast.7), channel_id=1, source_target_pairs={{2,0},{4,2},{6,4},{8,6},{10,8},{12,10},{14,12},{16,14},{18,16},{20... | collective-permute-start | bytes 2359304 | tf_op jit(solution)/shard_map/ppermute | solution.py:481
  14.5 1.2 %copy-start = (bf16[16,96,512]{2,1,0:T(8,128)(2,1)}, bf16[16,96,512]{2,1,0:T(8,128)(2,1)S(1)}, u32[]{:S(2)}) copy-start(bf16[16,96,512]{2,1,0:T(8,128)(2,1)S(1)} %get-tuple-element.8) | copy-start | bytes 4718596
  15.7 51.3 %all-to-all-start = ((bf16[16,96,512]{2,1,0:T(8,128)(2,1)}), bf16[16,96,512]{2,1,0:T(8,128)(2,1)S(1)}, u32[]{:S(2)}, u32[]{:S(2)}) async-start(bf16[16,96,512]{2,1,0:T(8,128)(2,1)} %copy-done), calls=%async_computation | async-start | bytes 3145728 | tf_op jit(solution)/shard_map/all_to_all | solution.py:505
  23.8 14.8 %collective-permute-start = (bf16[12,32,512]{2,1,0:T(8,128)(2,1)}, bf16[12,32,512]{2,1,0:T(8,128)(2,1)}, u32[]{:S(2)}, u32[]{:S(2)}) collective-permute-start(bf16[12,32,512]{2,1,0:T(8,128)(2,1)} %get-tuple-element.6), channel_id=1, source_target_pairs={{0,1},{1,0},{2,3},{3,2},{4,5},{5,4},{6,7},{7,6},{8,9},{9,8},{10,11... | collective-permute-start | bytes 1179656 | tf_op jit(solution)/shard_map/ppermute | solution.py:486
  25.7 26.7 %copy-start.1 = (bf16[256,256]{1,0:T(8,128)(2,1)S(1)}, bf16[256,256]{1,0:T(8,128)(2,1)}, u32[]{:S(2)}) copy-start(bf16[256,256]{1,0:T(8,128)(2,1)} %constant.37.clone.refs_1_.high_ref) | copy-start | bytes 393220
  25.7 26.6 %collective-permute-start.2 = (bf16[12,64,512]{2,1,0:T(8,128)(2,1)S(1)}, bf16[12,64,512]{2,1,0:T(8,128)(2,1)S(1)}, u32[]{:S(2)}, u32[]{:S(2)}) collective-permute-start(bf16[12,64,512]{2,1,0:T(8,128)(2,1)S(1)} %fusion), channel_id=1, source_target_pairs={{0,1},{1,0},{2,3},{3,2},{4,5},{5,4},{6,7},{7,6},{8,9},{9,8},{10,11... | collective-permute-start | bytes 2359304 | tf_op jit(solution)/shard_map/ppermute | solution.py:486
  38.7 28.3 %copy-start.2 = (bf16[256,256]{1,0:T(8,128)(2,1)S(1)}, bf16[256,256]{1,0:T(8,128)(2,1)}, u32[]{:S(2)}) copy-start(bf16[256,256]{1,0:T(8,128)(2,1)} %constant.38.clone.low_ref) | copy-start | bytes 393220
  69.4 4.0 %collective-permute-start.3 = (f32[32,256]{1,0:T(8,128)S(1)}, f32[32,256]{1,0:T(8,128)S(1)}, u32[]{:S(2)}, u32[]{:S(2)}) collective-permute-start(f32[32,256]{1,0:T(8,128)S(1)} %constant_dynamic-slice_fusion), channel_id=1, source_target_pairs={{0,1},{1,0},{2,3},{3,2},{4,5},{5,4},{6,7},{7,6},{8,9},{9,8},{10,11... | collective-permute-start | bytes 98312 | tf_op jit(solution)/shard_map/ppermute | solution.py:486

commit v5 on v3

--- a/solution.py
+++ b/solution.py
@@ -21,7 +21,7 @@
 QUARTERS = 4
 VMEM_LIMIT = 24 * 1024 * 1024
 FOLD_VMEM_LIMIT = 16 * 1024 * 1024
-SPECTRA_VMEM_LIMIT = 50 * 1024 * 1024
+SPECTRA_VMEM_LIMIT = 59 * 1024 * 1024
 
 
 def bin_order():
@@ -128,32 +128,44 @@
     )
 
 
-def spectra_kernel(traces_ref, table_ref, quality_ref, whitened_ref, traces, table, sems):
+def spectra_kernel(chan_ref, traces_ref, table_ref, quality_ref, owners_ref, places_ref, *refs):
+    whitened_ref, outgoing_ref, *shared_ref = refs[:-10]
+    traces, table, quality, owners, places, white, sent, selector, sems, out_sems = refs[-10:]
     row_parts, chunks, rows, depth = traces.shape
-    ch_dev = quality_ref.shape[1]
+    ch_dev = quality.shape[1]
+    pair = 2 * ch_dev
+    count = outgoing_ref.shape[0]
+    slots = sent.shape[2]
 
     def traces_copy(part, k):
         source = traces_ref.at[pl.ds(part * rows, rows), pl.ds(k * depth, depth)]
         return pltpu.make_async_copy(source, traces.at[part, k], sems.at[part, k])
 
-    table_copy = pltpu.make_async_copy(table_ref, table, sems.at[row_parts, 0])
-    table_copy.start()
+    small = [
+        pltpu.make_async_copy(source, target, sems.at[row_parts, k])
+        for k, (source, target) in enumerate(
+            ((table_ref, table), (quality_ref, quality), (owners_ref, owners), (places_ref, places))
+        )
+    ]
+    for copy in small:
+        copy.start()
     for part in range(row_parts):
         for k in range(chunks):
             traces_copy(part, k).start()
 
     band = band_matrix()
+    for copy in small[1:]:
+        copy.wait()
     shape = (rows, ch_dev)
     keep = jnp.sum(
-        jnp.where(rows_of(shape) % ch_dev == lanes_of(shape), quality_ref[...].astype(jnp.float32), 0.0),
+        jnp.where(rows_of(shape) % ch_dev == lanes_of(shape), quality[...].astype(jnp.float32), 0.0),
         axis=1, keepdims=True,
     )
-
-    def whiten(part, carry):
-        @pl.when(part == 0)
-        def _():
-            table_copy.wait()
-
+    selector[...] = slot_selector(owners[...], places[...], chan_ref[0], ch_dev)
+    small[0].wait()
+
+    leaving = []
+    for part in range(row_parts):
         quarters = []
         for k in range(chunks):
             traces_copy(part, k).wait()
@@ -170,28 +182,38 @@
         water = jnp.sum(energy, axis=1, keepdims=True) * (1.0 / F)
         scaling = lax.rsqrt(smooth * (1.0 / (2.0 * smooth_reach + 1.0)) + (0.1 * water + 1e-06)) * keep
         near, far = scaling[:, :H], scaling[:, H:]
-        white = [parts[0] * near, parts[1] * near, parts[2] * far, parts[3] * far]
-        at = pl.ds(pl.multiple_of(part * rows, rows), rows)
-        for q in range(4):
-            whitened_ref[at, q * H : (q + 1) * H] = white[q].astype(jnp.bfloat16)
-        return carry
-
-    lax.fori_loop(0, row_parts, whiten, 0)
-
-
-def select_kernel(where_ref, whitened_ref, owners_ref, places_ref, outgoing_ref, selector):
-    rows = selector.shape[1]
-
-    @pl.when(pl.program_id(0) == 0)
-    def _():
-        selector[...] = slot_selector(owners_ref[...], places_ref[...], where_ref[0], rows // 2)
-
-    count, slots, columns = outgoing_ref.shape
-    for n in range(slots // (2 * CAP)):
-        sent = jnp.dot(
-            selector[...], whitened_ref[rows * n : rows * (n + 1), :], preferred_element_type=jnp.float32
-        ).astype(jnp.bfloat16)
-        outgoing_ref[:, 2 * CAP * n : 2 * CAP * (n + 1), :] = sent.reshape(count, 2 * CAP, columns)
+        for q, values in enumerate((parts[0] * near, parts[1] * near, parts[2] * far, parts[3] * far)):
+            white[part, :, q * H : (q + 1) * H] = values.astype(jnp.bfloat16)
+        leaving.append(
+            pltpu.make_async_copy(
+                white.at[part], whitened_ref.at[pl.ds(part * rows, rows), :], out_sems.at[part, 0]
+            )
+        )
+        leaving[-1].start()
+        if shared_ref:
+            height = shared_ref[0].shape[1]
+            for w in range(rows // ch_dev):
+                leaving.append(
+                    pltpu.make_async_copy(
+                        white.at[part, pl.ds((w + 1) * ch_dev - height, height), :],
+                        shared_ref[0].at[part * (rows // ch_dev) + w],
+                        out_sems.at[part, 2 + w],
+                    )
+                )
+                leaving[-1].start()
+        for n in range(rows // pair):
+            chosen = jnp.dot(
+                selector[...], white[part, pair * n : pair * (n + 1), :], preferred_element_type=jnp.float32
+            ).astype(jnp.bfloat16)
+            sent[part, :, 2 * CAP * n : 2 * CAP * (n + 1), :] = chosen.reshape(count, 2 * CAP, chosen.shape[-1])
+        leaving.append(
+            pltpu.make_async_copy(
+                sent.at[part], outgoing_ref.at[:, pl.ds(part * slots, slots), :], out_sems.at[part, 1]
+            )
+        )
+        leaving[-1].start()
+    for copy in leaving:
+        copy.wait()
 
 
 def vmem_spec():
@@ -206,59 +228,55 @@
     return pl.BlockSpec(array.shape, lambda s: (0,) * array.ndim)
 
 
-def spectra_call(traces, quality):
+def spectra_call(chan, traces, quality, owners, places, chan_count, own_count):
     rows, length = traces.shape
+    ch_dev = quality.shape[1]
     part, depth = rows // ROW_STEPS, length // QUARTERS
+    slots = part // (2 * ch_dev) * 2 * CAP
     anywhere = pl.BlockSpec(memory_space=pl.ANY)
+    out_shape = [
+        jax.ShapeDtypeStruct((rows, 2 * F), jnp.bfloat16),
+        jax.ShapeDtypeStruct((chan_count, ROW_STEPS * slots, 2 * F), jnp.bfloat16),
+    ]
+    if own_count % 16 == 0:
+        out_shape.append(jax.ShapeDtypeStruct((rows // ch_dev, own_count, 2 * F), jnp.bfloat16))
     return pl.pallas_call(
         spectra_kernel,
-        in_specs=[anywhere, anywhere, vmem_spec()],
-        out_specs=vmem_spec(),
-        out_shape=jax.ShapeDtypeStruct((rows, 2 * F), jnp.bfloat16),
+        in_specs=[smem_spec()] + [anywhere] * 5,
+        out_specs=[anywhere] * len(out_shape),
+        out_shape=out_shape,
         scratch_shapes=[
             pltpu.VMEM((ROW_STEPS, QUARTERS, part, depth), jnp.bfloat16),
             pltpu.VMEM((depth, 2 * F), jnp.bfloat16),
+            pltpu.VMEM(quality.shape, jnp.int32),
+            pltpu.VMEM(owners.shape, jnp.int32),
+            pltpu.VMEM(places.shape, jnp.int32),
+            pltpu.VMEM((ROW_STEPS, part, 2 * F), jnp.bfloat16),
+            pltpu.VMEM((ROW_STEPS, chan_count, slots, 2 * F), jnp.bfloat16),
+            pltpu.VMEM((chan_count * 2 * CAP, 2 * ch_dev), jnp.bfloat16),
             pltpu.SemaphoreType.DMA((ROW_STEPS + 1, QUARTERS)),
+            pltpu.SemaphoreType.DMA((ROW_STEPS, 2 + part // ch_dev)),
         ],
         compiler_params=pltpu.CompilerParams(vmem_limit_bytes=SPECTRA_VMEM_LIMIT),
         cost_estimate=pl.CostEstimate(
             flops=2 * rows * length * 2 * F, bytes_accessed=2 * rows * length, transcendentals=rows * F
         ),
         name="spectra",
-    )(traces, jnp.asarray(forward_table(length)), quality)
-
-
-def select_call(where, whitened, owners, places, chan_count, ch_dev):
-    rows, columns = whitened.shape
-    block = rows // ROW_STEPS
-    slots = block // (2 * ch_dev) * 2 * CAP
-    return pl.pallas_call(
-        select_kernel,
-        grid=(ROW_STEPS,),
-        in_specs=[smem_spec(), pl.BlockSpec((block, columns), lambda s: (s, 0)), whole(owners), whole(places)],
-        out_specs=pl.BlockSpec((chan_count, slots, columns), lambda s: (0, s, 0)),
-        out_shape=jax.ShapeDtypeStruct((chan_count, ROW_STEPS * slots, columns), jnp.bfloat16),
-        scratch_shapes=[pltpu.VMEM((chan_count * 2 * CAP, 2 * ch_dev), jnp.bfloat16)],
-        compiler_params=pltpu.CompilerParams(vmem_limit_bytes=SPECTRA_VMEM_LIMIT),
-        cost_estimate=pl.CostEstimate(
-            flops=4 * rows * chan_count * 2 * CAP * columns, bytes_accessed=2 * rows * columns * 3, transcendentals=0
-        ),
-        name="select",
-    )(where, whitened, owners, places)
-
-
-def cross_kernel(last, with_sum, local_windows, where_ref, first_ref, second_ref, *refs):
+    )(chan, traces, jnp.asarray(forward_table(length)), quality, owners, places)
+
+
+def cross_kernel(last, with_sum, local_windows, win_ref, first_ref, second_ref, *refs):
     refs = list(refs)
     sum_ref = refs.pop(0) if with_sum else None
     if last:
-        high_ref, low_ref, out_ref, done_ref, wide, spread, total = refs
+        table_ref, out_ref, done_ref, wide, spread, total, lags, sems = refs
         done_ref[...] = jnp.zeros_like(done_ref)
     else:
         out_ref, wide, spread = refs
         total = out_ref
     windows, own_count = spread.shape[:2]
     ch_dev = wide.shape[1] // 2
-    base = pl.multiple_of(where_ref[1] * own_count, 8)
+    base = pl.multiple_of(win_ref[0] * own_count, 8)
 
     def widen(w, carry):
         if local_windows:
@@ -322,23 +340,25 @@
     lax.fori_loop(0, own_count // group * rounds, block, 0)
 
     if last:
-
-        def finish(eight, carry):
-            first = pl.multiple_of(8 * eight, 8)
-            stacks = total[pl.ds(first, 8)].reshape(8 * SPAN, F)
-            lagged = lag_transform(stacks, high_ref[...], low_ref[...]).reshape(8, SPAN, NLAG)
+        copies = []
+        for eight in range(own_count // 8):
+            first = 8 * eight
+            stacks = total[first : first + 8].reshape(8 * SPAN, F).astype(jnp.bfloat16)
+            lagged = jnp.dot(stacks, table_ref[...], preferred_element_type=jnp.float32).reshape(8, SPAN, NLAG)
             for i in range(8):
-                out_ref[first + i] = lagged[i, i + 1 : i + 1 + REACH, :]
-            return carry
-
-        lax.fori_loop(0, own_count // 8, finish, 0)
-
-
-def cross_call(where, first, second, ch_dev, own_count, sums, tables, local_windows):
+                lags[first + i] = lagged[i, i + 1 : i + 1 + REACH, :]
+            some = pl.ds(first, 8)
+            copies.append(pltpu.make_async_copy(lags.at[some], out_ref.at[some], sems.at[eight]))
+            copies[-1].start()
+        for copy in copies:
+            copy.wait()
+
+
+def cross_call(win, first, second, ch_dev, own_count, sums, table, local_windows):
     windows, _, columns = first.shape
-    last = tables is not None
+    last = table is not None
     with_sum = sums is not None
-    operands = [where, first, second]
+    operands = [win, first, second]
     if with_sum:
         operands.append(sums)
     scratch = [
@@ -346,16 +366,21 @@
         pltpu.VMEM((windows, own_count, 4, 8, H), jnp.float32),
     ]
     if last:
-        operands += list(tables)
-        scratch.append(pltpu.VMEM((own_count, SPAN, F), jnp.float32))
+        operands.append(table)
+        scratch += [
+            pltpu.VMEM((own_count, SPAN, F), jnp.float32),
+            pltpu.VMEM((own_count, REACH, NLAG), jnp.float32),
+            pltpu.SemaphoreType.DMA((own_count // 8,)),
+        ]
     shape = (own_count, REACH, NLAG) if last else (own_count, SPAN, F)
-    out_shape = [jax.ShapeDtypeStruct(shape, jnp.float32)]
+    out_shape, out_specs = [jax.ShapeDtypeStruct(shape, jnp.float32)], [vmem_spec()]
     if last:
         out_shape.append(jax.ShapeDtypeStruct((8, H), jnp.float32))
+        out_specs = [pl.BlockSpec(memory_space=pl.ANY), vmem_spec()]
     return pl.pallas_call(
         functools.partial(cross_kernel, last, with_sum, local_windows),
         in_specs=[smem_spec()] + [vmem_spec()] * (len(operands) - 1),
-        out_specs=[vmem_spec()] * len(out_shape),
+        out_specs=out_specs,
         out_shape=out_shape,
         scratch_shapes=scratch,
         compiler_params=pltpu.CompilerParams(vmem_limit_bytes=VMEM_LIMIT),
@@ -366,80 +391,56 @@
     )(*operands)
 
 
-def fold_kernel(where_ref, incoming_ref, own_ref, owners_ref, high_ref, low_ref, earlier_ref, out_ref, sums, picker):
-    step = pl.program_id(0)
-    rows = own_ref.shape[0]
-    ch_dev = rows // 2
-
-    @pl.when(step == 0)
-    def _():
-        sums[...] = jnp.zeros_like(sums)
-        owners = owners_ref[...].astype(jnp.float32)
-        per_row = owners.shape[1] // ch_dev
-        device = where_ref[0]
-        line = jnp.sum(jnp.where(rows_of(owners.shape) == device // per_row, owners, 0.0), axis=0, keepdims=True)
-        shape = (rows, owners.shape[1])
-        line = jnp.broadcast_to(line, shape)
-        first = device % per_row * ch_dev
-        place = first + rows_of(shape) % ch_dev
-        lane = lanes_of(shape)
-        owner = jnp.sum(jnp.where(lane == place, line, 0.0), axis=1, keepdims=True)
-        earlier = (lane >= first) & (lane < place) & (line == owner)
-        rank = jnp.sum(earlier.astype(jnp.float32), axis=1, keepdims=True)
-        source = (2 * CAP * owner + rank).astype(jnp.int32)
-        shape = picker.shape
-        target = source + CAP * (rows_of(shape) // ch_dev)
-        picker[...] = (lanes_of(shape) == target).astype(jnp.float32).astype(jnp.bfloat16)
-
+def fold_kernel(chan_ref, incoming_ref, own_ref, owners_ref, high_ref, low_ref, earlier_ref, out_ref):
+    ch_dev = out_ref.shape[0]
+    rows = 2 * ch_dev
+    pairs = own_ref.shape[0] // rows
     count, slots, columns = incoming_ref.shape
-    right = jnp.dot(
-        picker[...], incoming_ref[...].reshape(count * slots, columns), preferred_element_type=jnp.float32
-    )
-    left = own_ref[...].astype(jnp.float32)
-    l = [left[:, q * H : (q + 1) * H] for q in range(4)]
-    r = [right[:, q * H : (q + 1) * H] for q in range(4)]
-    first = l[0] * r[0] + l[1] * r[1]
-    second = l[2] * r[2] + l[3] * r[3]
-    imag = (l[1] * r[0] - l[0] * r[1]) + (l[2] * r[3] - l[3] * r[2])
-    for n, term in enumerate((first, second, imag)):
-        sums[n] += term[:ch_dev] + term[ch_dev:]
-
-    @pl.when(step == pl.num_programs(0) - 1)
-    def _():
-        stacks = jnp.concatenate(fold_columns(sums[0], sums[1], sums[2]), axis=1)
-        out_ref[...] = lag_transform(stacks, high_ref[...], low_ref[...])
-
-
-def fold_call(where, incoming, own, owners, ch_dev, tables, earlier):
-    count, slots, columns = incoming.shape
-    rows = 2 * ch_dev
-    pairs = own.shape[0] // rows
+    owners = owners_ref[...].astype(jnp.float32)
+    per_row = owners.shape[1] // ch_dev
+    device = chan_ref[0]
+    line = jnp.sum(jnp.where(rows_of(owners.shape) == device // per_row, owners, 0.0), axis=0, keepdims=True)
+    shape = (rows, owners.shape[1])
+    line = jnp.broadcast_to(line, shape)
+    first = device % per_row * ch_dev
+    place = first + rows_of(shape) % ch_dev
+    lane = lanes_of(shape)
+    owner = jnp.sum(jnp.where(lane == place, line, 0.0), axis=1, keepdims=True)
+    earlier = (lane >= first) & (lane < place) & (line == owner)
+    rank = jnp.sum(earlier.astype(jnp.float32), axis=1, keepdims=True)
+    source = (2 * CAP * owner + rank).astype(jnp.int32)
+    shape = (rows, count * 2 * CAP)
+    target = source + CAP * (rows_of(shape) // ch_dev)
+    picker = (lanes_of(shape) == target).astype(jnp.float32).astype(jnp.bfloat16)
+    sums = None
+    for n in range(pairs):
+        arrived = incoming_ref[:, 2 * CAP * n : 2 * CAP * (n + 1), :].reshape(count * 2 * CAP, columns)
+        right = jnp.dot(picker, arrived, preferred_element_type=jnp.float32)
+        left = own_ref[rows * n : rows * (n + 1), :].astype(jnp.float32)
+        l = [left[:, q * H : (q + 1) * H] for q in range(4)]
+        r = [right[:, q * H : (q + 1) * H] for q in range(4)]
+        terms = [
+            l[0] * r[0] + l[1] * r[1],
+            l[2] * r[2] + l[3] * r[3],
+            (l[1] * r[0] - l[0] * r[1]) + (l[2] * r[3] - l[3] * r[2]),
+        ]
+        sums = terms if sums is None else [total + term for total, term in zip(sums, terms)]
+    stacks = jnp.concatenate(fold_columns(*[total[:ch_dev] + total[ch_dev:] for total in sums]), axis=1)
+    out_ref[...] = lag_transform(stacks, high_ref[...], low_ref[...])
+
+
+def fold_call(chan, incoming, own, owners, ch_dev, tables, earlier):
     return pl.pallas_call(
         fold_kernel,
-        grid=(pairs,),
-        in_specs=[
-            smem_spec(),
-            pl.BlockSpec((count, slots // pairs, columns), lambda s: (0, s, 0)),
-            pl.BlockSpec((rows, columns), lambda s: (s, 0)),
-            whole(owners),
-            whole(tables[0]),
-            whole(tables[1]),
-            pl.BlockSpec(memory_space=pl.ANY),
-        ],
-        out_specs=pl.BlockSpec((ch_dev, NLAG), lambda s: (0, 0)),
+        in_specs=[smem_spec()] + [vmem_spec()] * 5 + [pl.BlockSpec(memory_space=pl.ANY)],
+        out_specs=vmem_spec(),
         out_shape=jax.ShapeDtypeStruct((ch_dev, NLAG), jnp.float32),
-        scratch_shapes=[
-            pltpu.VMEM((3, ch_dev, H), jnp.float32),
-            pltpu.VMEM((rows, count * slots // pairs), jnp.bfloat16),
-        ],
         compiler_params=pltpu.CompilerParams(vmem_limit_bytes=FOLD_VMEM_LIMIT),
         cost_estimate=pl.CostEstimate(
-            flops=2 * rows * pairs * count * 2 * CAP * columns,
-            bytes_accessed=2 * (incoming.size + own.size),
-            transcendentals=0,
+            flops=4 * ch_dev * incoming.size, bytes_accessed=2 * (incoming.size + own.size), transcendentals=0
         ),
         name="fold",
-    )(where, incoming, own, owners, *tables, earlier)
+    )(chan, incoming, own, owners, *tables, earlier)
 
 
 def from_above(block):
@@ -459,15 +460,18 @@
     window_part = lax.axis_index("win")
     own_count = ch_dev // win_count
     shared = ch_dev - own_count
-    where = jnp.stack([lax.axis_index("chan"), window_part]).astype(jnp.int32)
+    chan = lax.axis_index("chan").astype(jnp.int32).reshape(1)
+    win = window_part.astype(jnp.int32).reshape(1)
     tables = [jnp.asarray(t) for t in inverse_tables(1.0 / math.sqrt(F * win_dev * win_count))]
     owners = fold_block.reshape(-1, 2 * ch_dev)
     places = fold_offset.reshape(-1, 2 * ch_dev)
-    flat = spectra_call(traces.reshape(win_dev * ch_dev, length), quality.reshape(1, ch_dev))
+    flat, outgoing, *ready = spectra_call(
+        chan, traces.reshape(win_dev * ch_dev, length), quality.reshape(1, ch_dev), owners, places, chan_count, own_count
+    )
     whitened = flat.reshape(win_dev, ch_dev, 2 * F)
     upper = from_above(whitened)
-    common = [round_win(whitened[:, shared:], shift) for shift in range(1, win_count)]
-    outgoing = select_call(where, flat, owners, places, chan_count, ch_dev)
+    ready = ready[0] if ready else whitened[:, shared:]
+    common = [round_win(ready, shift) for shift in range(1, win_count)]
     incoming = lax.all_to_all(outgoing, "chan", split_axis=0, concat_axis=0, tiled=True)
     offered = jnp.concatenate([whitened[:, :shared], upper], axis=1)
     special = [
@@ -479,9 +483,9 @@
     arrived = [(whitened, upper)] + list(zip(common, special))
     sums = None
     for n, (first, second) in enumerate(arrived):
-        ends = tables if n == win_count - 1 else None
-        sums, *done = cross_call(where, first, second, ch_dev, own_count, sums, ends, n == 0)
-    share = fold_call(where, incoming, flat, owners, ch_dev, tables, done[0])
+        ends = tables[0] if n == win_count - 1 else None
+        sums, *done = cross_call(win, first, second, ch_dev, own_count, sums, ends, n == 0)
+    share = fold_call(chan, incoming, flat, owners, ch_dev, tables, done[0])
     fold = lax.dynamic_slice_in_dim(share, window_part * own_count, own_count, 0)
     for shift in range(1, win_count):
         target = (window_part + shift) % win_count * own_count

time: 67.6 us -> 68.2 us (level)
  the two profiles are of different devices: /device:TPU:0 before, /device:TPU:13 now
where the time goes in v5:
time: 68.2 us; the launch traced here: 68 us
  Pallas kernels  34.2 us (50%)
  waiting for transfers between devices  20.5 us (30%)
  starting transfers between devices  11.6 us (17%)
  other arithmetic  0.81 us (1%)
  between operations  0.79 us (1%)
    pallas_call x2, Pallas kernels, cross_call(): pl.pallas_call(functools.partial(cross_kernel, last, with_sum, local_wind...  23.8 us
    ppermute x1, waiting for transfers between devices, from_above(): return lax.ppermute(block, 'chan', [(i, i - 1) for i in range(1, count)])  18 us
    pallas_call x1, Pallas kernels, spectra_call(): pl.pallas_call(spectra_kernel, in_specs=[smem_spec()] + [anywhere] * 5, o...  9.68 us
    all_to_all x1, starting transfers between devices, local(): lax.all_to_all(outgoing, 'chan', split_axis=0, concat_axis=0, tiled=True)  6.18 us
    ppermute x3, starting transfers between devices, round_win(): lax.ppermute(block, 'win', [(i, (i + shift) % count) for i in range(count)])  2.83 us
    ppermute x1, starting transfers between devices, from_above(): return lax.ppermute(block, 'chan', [(i, i - 1) for i in range(1, count)])  2.58 us
    ppermute x3, waiting for transfers between devices, round_win(): lax.ppermute(block, 'win', [(i, (i + shift) % count) for i in range(count)])  2.49 us
  transfers between devices with their start and end apart: 5, of which 2 were waited for; matrix products, arithmetic and copies ran while one was open for 0% of the time, Pallas kernels for 35%

profile of v5, /device:TPU:13, one launch (start us, length us, event | category | flops | bytes accessed | tf_op | source)
XLA Modules:
  0.0 68.0 jit_solution(12659828528094504252)
XLA Ops:
  0.6 9.7 %spectra.1 = (bf16[768,512]{1,0:T(8,128)(2,1)}, bf16[16,96,512]{2,1,0:T(8,128)(2,1)}, bf16[12,32,512]{2,1,0:T(8,128)(2,1)}) custom-call(s32[1]{0:T(128)} %bitcast.1.chan_ref, bf16[768,4096]{1,0:T(8,128)(2,1)} %bitcast.12, bf16[1024,512]{1,0:T(8,128)(2,1)} %constant.39.clone.table_ref, s32[1,64]{1,0:T(1,128)} %bitcast.14, s32[8,128]{1,0:T(8,128)} %bitcast.10, ...), custom_call_target="tpu_custom_call" | custom-call | flops 3221225472 | bytes 6291456 | tf_op jit(solution)/shard_map/spectra/pallas_call | solution.py:243
  10.3 2.6 %collective-permute-start.1 = (bf16[12,64,512]{2,1,0:T(8,128)(2,1)}, bf16[12,64,512]{2,1,0:T(8,128)(2,1)S(1)}, u32[]{:S(2)}, u32[]{:S(2)}) collective-permute-start(bf16[12,64,512]{2,1,0:T(8,128)(2,1)} %bitcast.7), channel_id=1, source_target_pairs={{2,0},{4,2},{6,4},{8,6},{10,8},{12,10},{14,12},{16,14},{18,16},{20... | collective-permute-start | bytes 2359304 | tf_op jit(solution)/shard_map/ppermute | solution.py:448
  12.9 0.0 copy-start
  12.9 6.2 %all-to-all-start = ((bf16[16,96,512]{2,1,0:T(8,128)(2,1)}), bf16[16,96,512]{2,1,0:T(8,128)(2,1)S(1)}, u32[]{:S(2)}, u32[]{:S(2)}) async-start(bf16[16,96,512]{2,1,0:T(8,128)(2,1)} %get-tuple-element.10), calls=%async_computation | async-start | bytes 3145728 | tf_op jit(solution)/shard_map/all_to_all | solution.py:475
  19.1 1.2 %collective-permute-start = (bf16[12,32,512]{2,1,0:T(8,128)(2,1)}, bf16[12,32,512]{2,1,0:T(8,128)(2,1)}, u32[]{:S(2)}, u32[]{:S(2)}) collective-permute-start(bf16[12,32,512]{2,1,0:T(8,128)(2,1)} %get-tuple-element.7), channel_id=1, source_target_pairs={{0,1},{1,0},{2,3},{3,2},{4,5},{5,4},{6,7},{7,6},{8,9},{9,8},{10,11... | collective-permute-start | bytes 1179656 | tf_op jit(solution)/shard_map/ppermute | solution.py:453
  20.3 0.0 copy-done
  20.4 18.0 %collective-permute-done.1.second_ref = bf16[12,64,512]{2,1,0:T(8,128)(2,1)S(1)} collective-permute-done((bf16[12,64,512]{2,1,0:T(8,128)(2,1)}, bf16[12,64,512]{2,1,0:T(8,128)(2,1)S(1)}, u32[]{:S(2)}, u32[]{:S(2)}) %collective-permute-start.1) | collective-permute-done | bytes 786464 | tf_op jit(solution)/shard_map/ppermute | solution.py:448
  38.4 0.2 fusion
  38.6 1.3 %collective-permute-start.2 = (bf16[12,64,512]{2,1,0:T(8,128)(2,1)S(1)}, bf16[12,64,512]{2,1,0:T(8,128)(2,1)S(1)}, u32[]{:S(2)}, u32[]{:S(2)}) collective-permute-start(bf16[12,64,512]{2,1,0:T(8,128)(2,1)S(1)} %fusion), channel_id=1, source_target_pairs={{0,1},{1,0},{2,3},{3,2},{4,5},{5,4},{6,7},{7,6},{8,9},{9,8},{10,11... | collective-permute-start | bytes 2359304 | tf_op jit(solution)/shard_map/ppermute | solution.py:453
  39.8 0.0 copy-start.1
  39.8 10.5 %cross.2.refs_0_ = f32[32,72,256]{2,1,0:T(8,128)S(1)} custom-call(s32[1]{0:T(128)} %bitcast.win_ref, bf16[12,64,512]{2,1,0:T(8,128)(2,1)S(1)} %bitcast.9, bf16[12,64,512]{2,1,0:T(8,128)(2,1)S(1)} %collective-permute-done.1.second_ref), custom_call_target="tpu_custom_call" | custom-call | flops 30000001024 | bytes 3932160 | tf_op jit(solution)/shard_map/cross/pallas_call | solution.py:380
  50.3 0.0 copy-start.2
  50.3 0.0 copy-start.3
  50.3 0.0 collective-permute-done.first_ref
  50.3 0.0 collective-permute-done.2.second_ref
  50.4 0.0 copy-done.1
  50.4 13.3 %cross.3 = (f32[32,64,256]{2,1,0:T(8,128)}, f32[8,128]{1,0:T(8,128)S(1)}) custom-call(s32[1]{0:T(128)} %bitcast.win_ref, bf16[12,32,512]{2,1,0:T(8,128)(2,1)} %collective-permute-done.first_ref, bf16[12,64,512]{2,1,0:T(8,128)(2,1)S(1)} %collective-permute-done.2.second_ref, f32[32,72,256]{2,1,0:T(8,128)S(1)} %cross.2.refs_0_, bf16[256,256]{1,0:T(8,128)(2,1)S(1)} %copy-done.1), custom_call_target="tpu_custom_call" | custom-call | flops 30000001024 | bytes 3932160 | tf_op jit(solution)/shard_map/cross/pallas_call | solution.py:380
  63.7 0.0 all-to-all-done.incoming_ref
  63.7 0.0 copy-done.2
  63.7 0.0 copy-done.3
  63.7 0.8 %fold.1 = f32[64,256]{1,0:T(8,128)S(1)} custom-call(s32[1]{0:T(128)} %bitcast.1.chan_ref, bf16[16,96,512]{2,1,0:T(8,128)(2,1)S(1)} %all-to-all-done.incoming_ref, bf16[768,512]{1,0:T(8,128)(2,1)S(1)} %copy-done, s32[8,128]{1,0:T(8,128)S(1)} %bitcast.11, bf16[256,256]{1,0:T(8,128)(2,1)S(1)} %copy-done.1, bf16[256,256]{1,0:T(8,128)(2,1)S(1)} %copy-done.2, ...), custom_call_target="tpu_custom_call" | custom-call | flops 201326592 | bytes 2359296 | tf_op jit(solution)/shard_map/fold/pallas_call | solution.py:433
  64.5 0.3 collective-permute-start.3
  64.9 2.5 %collective-permute-done.3 = f32[32,256]{1,0:T(8,128)S(1)} collective-permute-done((f32[32,256]{1,0:T(8,128)S(1)}, f32[32,256]{1,0:T(8,128)S(1)}, u32[]{:S(2)}, u32[]{:S(2)}) %collective-permute-start.3) | collective-permute-done | bytes 32800 | tf_op jit(solution)/shard_map/ppermute | solution.py:453
  67.3 0.6 dynamic-slice_add_fusion
  (2 shorter events, 0.0 us)
Async XLA Ops:
  10.3 28.0 %collective-permute-start.1 = (bf16[12,64,512]{2,1,0:T(8,128)(2,1)}, bf16[12,64,512]{2,1,0:T(8,128)(2,1)S(1)}, u32[]{:S(2)}, u32[]{:S(2)}) collective-permute-start(bf16[12,64,512]{2,1,0:T(8,128)(2,1)} %bitcast.7), channel_id=1, source_target_pairs={{2,0},{4,2},{6,4},{8,6},{10,8},{12,10},{14,12},{16,14},{18,16},{20... | collective-permute-start | bytes 2359304 | tf_op jit(solution)/shard_map/ppermute | solution.py:448
  12.9 7.4 %copy-start = (bf16[768,512]{1,0:T(8,128)(2,1)S(1)}, bf16[768,512]{1,0:T(8,128)(2,1)}, u32[]{:S(2)}) copy-start(bf16[768,512]{1,0:T(8,128)(2,1)} %get-tuple-element.8.own_ref) | copy-start | bytes 2359300
  12.9 50.7 %all-to-all-start = ((bf16[16,96,512]{2,1,0:T(8,128)(2,1)}), bf16[16,96,512]{2,1,0:T(8,128)(2,1)S(1)}, u32[]{:S(2)}, u32[]{:S(2)}) async-start(bf16[16,96,512]{2,1,0:T(8,128)(2,1)} %get-tuple-element.10), calls=%async_computation | async-start | bytes 3145728 | tf_op jit(solution)/shard_map/all_to_all | solution.py:475
  19.1 31.2 %collective-permute-start = (bf16[12,32,512]{2,1,0:T(8,128)(2,1)}, bf16[12,32,512]{2,1,0:T(8,128)(2,1)}, u32[]{:S(2)}, u32[]{:S(2)}) collective-permute-start(bf16[12,32,512]{2,1,0:T(8,128)(2,1)} %get-tuple-element.7), channel_id=1, source_target_pairs={{0,1},{1,0},{2,3},{3,2},{4,5},{5,4},{6,7},{7,6},{8,9},{9,8},{10,11... | collective-permute-start | bytes 1179656 | tf_op jit(solution)/shard_map/ppermute | solution.py:453
  38.6 11.8 %collective-permute-start.2 = (bf16[12,64,512]{2,1,0:T(8,128)(2,1)S(1)}, bf16[12,64,512]{2,1,0:T(8,128)(2,1)S(1)}, u32[]{:S(2)}, u32[]{:S(2)}) collective-permute-start(bf16[12,64,512]{2,1,0:T(8,128)(2,1)S(1)} %fusion), channel_id=1, source_target_pairs={{0,1},{1,0},{2,3},{3,2},{4,5},{5,4},{6,7},{7,6},{8,9},{9,8},{10,11... | collective-permute-start | bytes 2359304 | tf_op jit(solution)/shard_map/ppermute | solution.py:453
  39.8 10.5 %copy-start.1 = (bf16[256,256]{1,0:T(8,128)(2,1)S(1)}, bf16[256,256]{1,0:T(8,128)(2,1)}, u32[]{:S(2)}) copy-start(bf16[256,256]{1,0:T(8,128)(2,1)} %constant.37.clone.refs_1_.high_ref) | copy-start | bytes 393220
  50.3 13.4 %copy-start.2 = (bf16[256,256]{1,0:T(8,128)(2,1)S(1)}, bf16[256,256]{1,0:T(8,128)(2,1)}, u32[]{:S(2)}) copy-start(bf16[256,256]{1,0:T(8,128)(2,1)} %constant.38.clone.low_ref) | copy-start | bytes 393220
  50.3 13.4 %copy-start.3 = (s32[1024,1]{0,1:T(1,128)S(1)}, s32[1024,1]{0,1:T(1,128)}, u32[]{:S(2)}) copy-start(s32[1024,1]{0,1:T(1,128)} %param.9) | copy-start | bytes 12292
  64.5 2.8 %collective-permute-start.3 = (f32[32,256]{1,0:T(8,128)S(1)}, f32[32,256]{1,0:T(8,128)S(1)}, u32[]{:S(2)}, u32[]{:S(2)}) collective-permute-start(f32[32,256]{1,0:T(8,128)S(1)} %constant_dynamic-slice_fusion), channel_id=1, source_target_pairs={{0,1},{1,0},{2,3},{3,2},{4,5},{5,4},{6,7},{7,6},{8,9},{9,8},{10,11... | collective-permute-start | bytes 98312 | tf_op jit(solution)/shard_map/ppermute | solution.py:453

commit v6 on v5

--- a/solution.py
+++ b/solution.py
@@ -129,7 +129,7 @@
 
 
 def spectra_kernel(chan_ref, traces_ref, table_ref, quality_ref, owners_ref, places_ref, *refs):
-    whitened_ref, outgoing_ref, *shared_ref = refs[:-10]
+    whitened_ref, outgoing_ref, near_ref, far_ref, *shared_ref = refs[:-10]
     traces, table, quality, owners, places, white, sent, selector, sems, out_sems = refs[-10:]
     row_parts, chunks, rows, depth = traces.shape
     ch_dev = quality.shape[1]
@@ -190,6 +190,15 @@
             )
         )
         leaving[-1].start()
+        for half, target in enumerate((near_ref, far_ref)):
+            leaving.append(
+                pltpu.make_async_copy(
+                    white.at[part, :, pl.ds(half * F, F)],
+                    target.at[pl.ds(part * rows, rows), :],
+                    out_sems.at[part, 2 + half],
+                )
+            )
+            leaving[-1].start()
         if shared_ref:
             height = shared_ref[0].shape[1]
             for w in range(rows // ch_dev):
@@ -197,7 +206,7 @@
                     pltpu.make_async_copy(
                         white.at[part, pl.ds((w + 1) * ch_dev - height, height), :],
                         shared_ref[0].at[part * (rows // ch_dev) + w],
-                        out_sems.at[part, 2 + w],
+                        out_sems.at[part, 4 + w],
                     )
                 )
                 leaving[-1].start()
@@ -237,6 +246,8 @@
     out_shape = [
         jax.ShapeDtypeStruct((rows, 2 * F), jnp.bfloat16),
         jax.ShapeDtypeStruct((chan_count, ROW_STEPS * slots, 2 * F), jnp.bfloat16),
+        jax.ShapeDtypeStruct((rows, F), jnp.bfloat16),
+        jax.ShapeDtypeStruct((rows, F), jnp.bfloat16),
     ]
     if own_count % 16 == 0:
         out_shape.append(jax.ShapeDtypeStruct((rows // ch_dev, own_count, 2 * F), jnp.bfloat16))
@@ -255,7 +266,7 @@
             pltpu.VMEM((ROW_STEPS, chan_count, slots, 2 * F), jnp.bfloat16),
             pltpu.VMEM((chan_count * 2 * CAP, 2 * ch_dev), jnp.bfloat16),
             pltpu.SemaphoreType.DMA((ROW_STEPS + 1, QUARTERS)),
-            pltpu.SemaphoreType.DMA((ROW_STEPS, 2 + part // ch_dev)),
+            pltpu.SemaphoreType.DMA((ROW_STEPS, 4 + part // ch_dev)),
         ],
         compiler_params=pltpu.CompilerParams(vmem_limit_bytes=SPECTRA_VMEM_LIMIT),
         cost_estimate=pl.CostEstimate(
@@ -265,8 +276,10 @@
     )(chan, traces, jnp.asarray(forward_table(length)), quality, owners, places)
 
 
-def cross_kernel(last, with_sum, local_windows, win_ref, first_ref, second_ref, *refs):
+def cross_kernel(last, with_sum, local_windows, awaited, win_ref, first_ref, second_ref, *refs):
     refs = list(refs)
+    far_ref = refs.pop(0) if local_windows else None
+    refs = refs[awaited:]
     sum_ref = refs.pop(0) if with_sum else None
     if last:
         table_ref, out_ref, done_ref, wide, spread, total, lags, sems = refs
@@ -281,7 +294,8 @@
     def widen(w, carry):
         if local_windows:
             wide[w, :ch_dev, :] = first_ref[w].astype(jnp.float32)
-            wide[w, ch_dev:, :] = second_ref[w].astype(jnp.float32)
+            wide[w, ch_dev:, :F] = second_ref[w].astype(jnp.float32)
+            wide[w, ch_dev:, F:] = far_ref[w].astype(jnp.float32)
         else:
             shared = ch_dev - own_count
             wide[w, shared:ch_dev, :] = first_ref[w].astype(jnp.float32)
@@ -354,11 +368,13 @@
             copy.wait()
 
 
-def cross_call(win, first, second, ch_dev, own_count, sums, table, local_windows):
+def cross_call(win, first, second, ch_dev, own_count, sums, table, awaited=()):
+    local_windows = len(second) == 2
     windows, _, columns = first.shape
     last = table is not None
     with_sum = sums is not None
-    operands = [win, first, second]
+    operands = [win, first, *second, *awaited]
+    in_specs = [smem_spec()] + [vmem_spec()] * (1 + len(second)) + [pl.BlockSpec(memory_space=pl.ANY)] * len(awaited)
     if with_sum:
         operands.append(sums)
     scratch = [
@@ -378,8 +394,8 @@
         out_shape.append(jax.ShapeDtypeStruct((8, H), jnp.float32))
         out_specs = [pl.BlockSpec(memory_space=pl.ANY), vmem_spec()]
     return pl.pallas_call(
-        functools.partial(cross_kernel, last, with_sum, local_windows),
-        in_specs=[smem_spec()] + [vmem_spec()] * (len(operands) - 1),
+        functools.partial(cross_kernel, last, with_sum, local_windows, len(awaited)),
+        in_specs=in_specs + [vmem_spec()] * (len(operands) - len(in_specs)),
         out_specs=out_specs,
         out_shape=out_shape,
         scratch_shapes=scratch,
@@ -465,26 +481,26 @@
     tables = [jnp.asarray(t) for t in inverse_tables(1.0 / math.sqrt(F * win_dev * win_count))]
     owners = fold_block.reshape(-1, 2 * ch_dev)
     places = fold_offset.reshape(-1, 2 * ch_dev)
-    flat, outgoing, *ready = spectra_call(
+    flat, outgoing, near, far, *ready = spectra_call(
         chan, traces.reshape(win_dev * ch_dev, length), quality.reshape(1, ch_dev), owners, places, chan_count, own_count
     )
     whitened = flat.reshape(win_dev, ch_dev, 2 * F)
-    upper = from_above(whitened)
+    upper = [from_above(half.reshape(win_dev, ch_dev, F)) for half in (near, far)]
     ready = ready[0] if ready else whitened[:, shared:]
     common = [round_win(ready, shift) for shift in range(1, win_count)]
     incoming = lax.all_to_all(outgoing, "chan", split_axis=0, concat_axis=0, tiled=True)
-    offered = jnp.concatenate([whitened[:, :shared], upper], axis=1)
+    offered = jnp.concatenate([whitened[:, :shared], jnp.concatenate(upper, axis=2)], axis=1)
     special = [
         round_win(
             lax.dynamic_slice_in_dim(offered, (window_part + shift) % win_count * own_count, ch_dev, 1), shift
         )
         for shift in range(1, win_count)
     ]
-    arrived = [(whitened, upper)] + list(zip(common, special))
+    arrived = [(whitened, upper, common)] + [(rows, [others], []) for rows, others in zip(common, special)]
     sums = None
-    for n, (first, second) in enumerate(arrived):
+    for n, (first, second, awaited) in enumerate(arrived):
         ends = tables[0] if n == win_count - 1 else None
-        sums, *done = cross_call(win, first, second, ch_dev, own_count, sums, ends, n == 0)
+        sums, *done = cross_call(win, first, second, ch_dev, own_count, sums, ends, awaited)
     share = fold_call(chan, incoming, flat, owners, ch_dev, tables, done[0])
     fold = lax.dynamic_slice_in_dim(share, window_part * own_count, own_count, 0)
     for shift in range(1, win_count):

time: 68.2 us -> 64.8 us (0.950)
  the two profiles are of different devices: /device:TPU:13 before, /device:TPU:16 now
where the time goes in v6:
time: 64.8 us; the launch traced here: 64.6 us
  Pallas kernels  33.3 us (51%)
  starting transfers between devices  14.7 us (23%)
  waiting for transfers between devices  13.2 us (20%)
  local copies, waits for them, and re-layouts  1.8 us (3%)
  other arithmetic  0.82 us (1%)
  between operations  0.74 us (1%)
    pallas_call x2, Pallas kernels, cross_call(): pl.pallas_call(functools.partial(cross_kernel, last, with_sum, local_wind...  22.7 us
    pallas_call x1, Pallas kernels, spectra_call(): pl.pallas_call(spectra_kernel, in_specs=[smem_spec()] + [anywhere] * 5, o...  9.75 us
    ppermute x3, waiting for transfers between devices, round_win(): lax.ppermute(block, 'win', [(i, (i + shift) % count) for i in range(count)])  9.7 us
    all_to_all x1, starting transfers between devices, local(): lax.all_to_all(outgoing, 'chan', split_axis=0, concat_axis=0, tiled=True)  5.42 us
    ppermute x2, starting transfers between devices, from_above(): return lax.ppermute(block, 'chan', [(i, i - 1) for i in range(1, count)])  5.34 us
    ppermute x3, starting transfers between devices, round_win(): lax.ppermute(block, 'win', [(i, (i + shift) % count) for i in range(count)])  3.98 us
    all_to_all x1, waiting for transfers between devices, local(): lax.all_to_all(outgoing, 'chan', split_axis=0, concat_axis=0, tiled=True)  3.29 us
    unnamed x14, local copies, waits for them, and re-layouts  1.76 us
  transfers between devices with their start and end apart: 6, of which 5 were waited for; matrix products, arithmetic and copies ran while one was open for 0% of the time, Pallas kernels for 35%

profile of v6, /device:TPU:16, one launch (start us, length us, event | category | flops | bytes accessed | tf_op | source)
XLA Modules:
  0.0 64.6 jit_solution(7415282742776318420)
XLA Ops:
  0.6 9.8 %spectra.1 = (bf16[768,512]{1,0:T(8,128)(2,1)}, bf16[16,96,512]{2,1,0:T(8,128)(2,1)}, bf16[768,256]{1,0:T(8,128)(2,1)}, bf16[768,256]{1,0:T(8,128)(2,1)}, bf16[12,32,512]{2,1,0:T(8,128)(2,1)}) custom-call(s32[1]{0:T(128)} %bitcast.1.chan_ref, bf16[768,4096]{1,0:T(8,128)(2,1)} %bitcast.13, bf16[1024,512]{1,0:T(8,128)(2,1)} %constant.39.clone.table_ref, ...), custom_call_target="tpu_custom_call" | custom-call | flops 3221225472 | bytes 6291456 | tf_op jit(solution)/shard_map/spectra/pallas_call | solution.py:254
  10.4 2.8 %collective-permute-start.1 = (bf16[12,64,256]{2,1,0:T(8,128)(2,1)}, bf16[12,64,256]{2,1,0:T(8,128)(2,1)S(1)}, u32[]{:S(2)}, u32[]{:S(2)}) collective-permute-start(bf16[12,64,256]{2,1,0:T(8,128)(2,1)} %bitcast.15), channel_id=1, source_target_pairs={{2,0},{4,2},{6,4},{8,6},{10,8},{12,10},{14,12},{16,14},{18,16},{20... | collective-permute-start | bytes 1179656 | tf_op jit(solution)/shard_map/ppermute | solution.py:464
  13.2 2.6 %collective-permute-start.2 = (bf16[12,64,256]{2,1,0:T(8,128)(2,1)}, bf16[12,64,256]{2,1,0:T(8,128)(2,1)S(1)}, u32[]{:S(2)}, u32[]{:S(2)}) collective-permute-start(bf16[12,64,256]{2,1,0:T(8,128)(2,1)} %bitcast.14), channel_id=1, source_target_pairs={{2,0},{4,2},{6,4},{8,6},{10,8},{12,10},{14,12},{16,14},{18,16},{20... | collective-permute-start | bytes 1179656 | tf_op jit(solution)/shard_map/ppermute | solution.py:464
  15.7 1.6 %collective-permute-start = (bf16[12,32,512]{2,1,0:T(8,128)(2,1)}, bf16[12,32,512]{2,1,0:T(8,128)(2,1)S(1)}, u32[]{:S(2)}, u32[]{:S(2)}) collective-permute-start(bf16[12,32,512]{2,1,0:T(8,128)(2,1)} %get-tuple-element.9), channel_id=1, source_target_pairs={{0,1},{1,0},{2,3},{3,2},{4,5},{5,4},{6,7},{7,6},{8,9},{9,8},{10,11... | collective-permute-start | bytes 1179656 | tf_op jit(solution)/shard_map/ppermute | solution.py:469
  17.3 0.0 copy-start
  17.3 5.4 %all-to-all-start = ((bf16[16,96,512]{2,1,0:T(8,128)(2,1)}), bf16[16,96,512]{2,1,0:T(8,128)(2,1)S(1)}, u32[]{:S(2)}, u32[]{:S(2)}) async-start(bf16[16,96,512]{2,1,0:T(8,128)(2,1)} %get-tuple-element.14), calls=%async_computation | async-start | bytes 3145728 | tf_op jit(solution)/shard_map/all_to_all | solution.py:491
  22.7 0.0 copy-done
  22.8 0.0 collective-permute-done.1.second_ref
  22.8 0.2 collective-permute-done.2.refs_0_
  23.0 0.2 fusion
  23.2 1.8 %collective-permute-start.3 = (bf16[12,64,512]{2,1,0:T(8,128)(2,1)S(1)}, bf16[12,64,512]{2,1,0:T(8,128)(2,1)S(1)}, u32[]{:S(2)}, u32[]{:S(2)}) collective-permute-start(bf16[12,64,512]{2,1,0:T(8,128)(2,1)S(1)} %fusion), channel_id=1, source_target_pairs={{0,1},{1,0},{2,3},{3,2},{4,5},{5,4},{6,7},{7,6},{8,9},{9,8},{10,11... | collective-permute-start | bytes 2359304 | tf_op jit(solution)/shard_map/ppermute | solution.py:469
  25.0 1.9 %collective-permute-done.refs_1_.first_ref = bf16[12,32,512]{2,1,0:T(8,128)(2,1)S(1)} collective-permute-done((bf16[12,32,512]{2,1,0:T(8,128)(2,1)}, bf16[12,32,512]{2,1,0:T(8,128)(2,1)S(1)}, u32[]{:S(2)}, u32[]{:S(2)}) %collective-permute-start) | collective-permute-done | bytes 393248 | tf_op jit(solution)/shard_map/ppermute | solution.py:469
  26.9 0.0 copy-start.4
  26.9 0.7 %copy-done.4 = bf16[12,32,512]{2,1,0:T(8,128)(2,1)} copy-done((bf16[12,32,512]{2,1,0:T(8,128)(2,1)}, bf16[12,32,512]{2,1,0:T(8,128)(2,1)S(1)}, u32[]{:S(2)}) %copy-start.4) | copy-done | bytes 393240
  27.6 0.0 copy-start.5
  27.6 1.0 %copy-done.5 = bf16[12,32,512]{2,1,0:T(8,128)(2,1)S(1)} copy-done((bf16[12,32,512]{2,1,0:T(8,128)(2,1)S(1)}, bf16[12,32,512]{2,1,0:T(8,128)(2,1)}, u32[]{:S(2)}) %copy-start.5) | copy-done | bytes 393240
  28.6 0.0 copy-start.1
  28.6 0.0 copy-start.6
  28.6 10.5 %cross.2.refs_0_ = f32[32,72,256]{2,1,0:T(8,128)S(1)} custom-call(s32[1]{0:T(128)} %bitcast.win_ref, bf16[12,64,512]{2,1,0:T(8,128)(2,1)S(1)} %bitcast.10, bf16[12,64,256]{2,1,0:T(8,128)(2,1)S(1)} %collective-permute-done.1.second_ref, bf16[12,64,256]{2,1,0:T(8,128)(2,1)S(1)} %collective-permute-done.2.refs_0_, bf16[12,32,512]{2,1,0:T(8,128)(2,1)S(1)} %copy-done.5), custom_call_target="tpu_custom_call" | custom-call | flops 30000001024 | bytes 3932160 | tf_op jit(solution)/shard_map/cross/pallas_call | solution.py:396
  39.1 0.0 copy-start.2
  39.1 0.0 copy-start.3
  39.1 4.4 %collective-permute-done.3.second_ref = bf16[12,64,512]{2,1,0:T(8,128)(2,1)S(1)} collective-permute-done((bf16[12,64,512]{2,1,0:T(8,128)(2,1)S(1)}, bf16[12,64,512]{2,1,0:T(8,128)(2,1)S(1)}, u32[]{:S(2)}, u32[]{:S(2)}) %collective-permute-start.3) | collective-permute-done | bytes 786464 | tf_op jit(solution)/shard_map/ppermute | solution.py:469
  43.6 0.0 copy-done.1
  43.6 0.0 copy-done.6
  43.6 12.3 %cross.3 = (f32[32,64,256]{2,1,0:T(8,128)}, f32[8,128]{1,0:T(8,128)S(1)}) custom-call(s32[1]{0:T(128)} %bitcast.win_ref, bf16[12,32,512]{2,1,0:T(8,128)(2,1)S(1)} %copy-done.6, bf16[12,64,512]{2,1,0:T(8,128)(2,1)S(1)} %collective-permute-done.3.second_ref, f32[32,72,256]{2,1,0:T(8,128)S(1)} %cross.2.refs_0_, bf16[256,256]{1,0:T(8,128)(2,1)S(1)} %copy-done.1), custom_call_target="tpu_custom_call" | custom-call | flops 30000001024 | bytes 3932160 | tf_op jit(solution)/shard_map/cross/pallas_call | solution.py:396
  55.8 3.3 %all-to-all-done.incoming_ref = bf16[16,96,512]{2,1,0:T(8,128)(2,1)S(1)} async-done(((bf16[16,96,512]{2,1,0:T(8,128)(2,1)}), bf16[16,96,512]{2,1,0:T(8,128)(2,1)S(1)}, u32[]{:S(2)}, u32[]{:S(2)}) %all-to-all-start) | async-done | bytes 1572896 | tf_op jit(solution)/shard_map/all_to_all | solution.py:491
  59.1 0.0 copy-done.2
  59.1 0.0 copy-done.3
  59.1 0.8 %fold.1 = f32[64,256]{1,0:T(8,128)S(1)} custom-call(s32[1]{0:T(128)} %bitcast.1.chan_ref, bf16[16,96,512]{2,1,0:T(8,128)(2,1)S(1)} %all-to-all-done.incoming_ref, bf16[768,512]{1,0:T(8,128)(2,1)S(1)} %copy-done, s32[8,128]{1,0:T(8,128)S(1)} %bitcast.12, bf16[256,256]{1,0:T(8,128)(2,1)S(1)} %copy-done.1, bf16[256,256]{1,0:T(8,128)(2,1)S(1)} %copy-done.2, ...), custom_call_target="tpu_custom_call" | custom-call | flops 201326592 | bytes 2359296 | tf_op jit(solution)/shard_map/fold/pallas_call | solution.py:449
  60.0 0.6 collective-permute-start.4
  60.6 3.4 %collective-permute-done.4 = f32[32,256]{1,0:T(8,128)S(1)} collective-permute-done((f32[32,256]{1,0:T(8,128)S(1)}, f32[32,256]{1,0:T(8,128)S(1)}, u32[]{:S(2)}, u32[]{:S(2)}) %collective-permute-start.4) | collective-permute-done | bytes 32800 | tf_op jit(solution)/shard_map/ppermute | solution.py:469
  63.9 0.6 dynamic-slice_add_fusion
  (2 shorter events, 0.0 us)
Async XLA Ops:
  10.4 12.4 %collective-permute-start.1 = (bf16[12,64,256]{2,1,0:T(8,128)(2,1)}, bf16[12,64,256]{2,1,0:T(8,128)(2,1)S(1)}, u32[]{:S(2)}, u32[]{:S(2)}) collective-permute-start(bf16[12,64,256]{2,1,0:T(8,128)(2,1)} %bitcast.15), channel_id=1, source_target_pairs={{2,0},{4,2},{6,4},{8,6},{10,8},{12,10},{14,12},{16,14},{18,16},{20... | collective-permute-start | bytes 1179656 | tf_op jit(solution)/shard_map/ppermute | solution.py:464
  13.2 9.8 %collective-permute-start.2 = (bf16[12,64,256]{2,1,0:T(8,128)(2,1)}, bf16[12,64,256]{2,1,0:T(8,128)(2,1)S(1)}, u32[]{:S(2)}, u32[]{:S(2)}) collective-permute-start(bf16[12,64,256]{2,1,0:T(8,128)(2,1)} %bitcast.14), channel_id=1, source_target_pairs={{2,0},{4,2},{6,4},{8,6},{10,8},{12,10},{14,12},{16,14},{18,16},{20... | collective-permute-start | bytes 1179656 | tf_op jit(solution)/shard_map/ppermute | solution.py:464
  15.7 11.1 %collective-permute-start = (bf16[12,32,512]{2,1,0:T(8,128)(2,1)}, bf16[12,32,512]{2,1,0:T(8,128)(2,1)S(1)}, u32[]{:S(2)}, u32[]{:S(2)}) collective-permute-start(bf16[12,32,512]{2,1,0:T(8,128)(2,1)} %get-tuple-element.9), channel_id=1, source_target_pairs={{0,1},{1,0},{2,3},{3,2},{4,5},{5,4},{6,7},{7,6},{8,9},{9,8},{10,11... | collective-permute-start | bytes 1179656 | tf_op jit(solution)/shard_map/ppermute | solution.py:469
  17.3 5.4 %copy-start = (bf16[768,512]{1,0:T(8,128)(2,1)S(1)}, bf16[768,512]{1,0:T(8,128)(2,1)}, u32[]{:S(2)}) copy-start(bf16[768,512]{1,0:T(8,128)(2,1)} %get-tuple-element.10.own_ref) | copy-start | bytes 2359300
  17.3 41.8 %all-to-all-start = ((bf16[16,96,512]{2,1,0:T(8,128)(2,1)}), bf16[16,96,512]{2,1,0:T(8,128)(2,1)S(1)}, u32[]{:S(2)}, u32[]{:S(2)}) async-start(bf16[16,96,512]{2,1,0:T(8,128)(2,1)} %get-tuple-element.14), calls=%async_computation | async-start | bytes 3145728 | tf_op jit(solution)/shard_map/all_to_all | solution.py:491
  23.2 20.4 %collective-permute-start.3 = (bf16[12,64,512]{2,1,0:T(8,128)(2,1)S(1)}, bf16[12,64,512]{2,1,0:T(8,128)(2,1)S(1)}, u32[]{:S(2)}, u32[]{:S(2)}) collective-permute-start(bf16[12,64,512]{2,1,0:T(8,128)(2,1)S(1)} %fusion), channel_id=1, source_target_pairs={{0,1},{1,0},{2,3},{3,2},{4,5},{5,4},{6,7},{7,6},{8,9},{9,8},{10,11... | collective-permute-start | bytes 2359304 | tf_op jit(solution)/shard_map/ppermute | solution.py:469
  26.9 0.7 %copy-start.4 = (bf16[12,32,512]{2,1,0:T(8,128)(2,1)}, bf16[12,32,512]{2,1,0:T(8,128)(2,1)S(1)}, u32[]{:S(2)}) copy-start(bf16[12,32,512]{2,1,0:T(8,128)(2,1)S(1)} %collective-permute-done.refs_1_.first_ref) | copy-start | bytes 1179652
  27.6 1.0 %copy-start.5 = (bf16[12,32,512]{2,1,0:T(8,128)(2,1)S(1)}, bf16[12,32,512]{2,1,0:T(8,128)(2,1)}, u32[]{:S(2)}) copy-start(bf16[12,32,512]{2,1,0:T(8,128)(2,1)} %copy-done.4) | copy-start | bytes 1179652
  28.6 14.9 %copy-start.1 = (bf16[256,256]{1,0:T(8,128)(2,1)S(1)}, bf16[256,256]{1,0:T(8,128)(2,1)}, u32[]{:S(2)}) copy-start(bf16[256,256]{1,0:T(8,128)(2,1)} %constant.37.clone.refs_1_.high_ref) | copy-start | bytes 393220
  28.6 14.9 %copy-start.6 = (bf16[12,32,512]{2,1,0:T(8,128)(2,1)S(1)}, bf16[12,32,512]{2,1,0:T(8,128)(2,1)}, u32[]{:S(2)}) copy-start(bf16[12,32,512]{2,1,0:T(8,128)(2,1)} %copy-done.4) | copy-start | bytes 1179652
  39.1 20.0 %copy-start.2 = (bf16[256,256]{1,0:T(8,128)(2,1)S(1)}, bf16[256,256]{1,0:T(8,128)(2,1)}, u32[]{:S(2)}) copy-start(bf16[256,256]{1,0:T(8,128)(2,1)} %constant.38.clone.low_ref) | copy-start | bytes 393220
  39.1 20.0 %copy-start.3 = (s32[1024,1]{0,1:T(1,128)S(1)}, s32[1024,1]{0,1:T(1,128)}, u32[]{:S(2)}) copy-start(s32[1024,1]{0,1:T(1,128)} %param.9) | copy-start | bytes 12292
  60.0 4.0 %collective-permute-start.4 = (f32[32,256]{1,0:T(8,128)S(1)}, f32[32,256]{1,0:T(8,128)S(1)}, u32[]{:S(2)}, u32[]{:S(2)}) collective-permute-start(f32[32,256]{1,0:T(8,128)S(1)} %constant_dynamic-slice_fusion), channel_id=1, source_target_pairs={{0,1},{1,0},{2,3},{3,2},{4,5},{5,4},{6,7},{7,6},{8,9},{9,8},{10,11... | collective-permute-start | bytes 98312 | tf_op jit(solution)/shard_map/ppermute | solution.py:469

commit v7 on v5

--- a/solution.py
+++ b/solution.py
@@ -149,9 +149,8 @@
     ]
     for copy in small:
         copy.start()
-    for part in range(row_parts):
-        for k in range(chunks):
-            traces_copy(part, k).start()
+    for k in range(chunks):
+        traces_copy(0, k).start()
 
     band = band_matrix()
     for copy in small[1:]:
@@ -169,6 +168,8 @@
         quarters = []
         for k in range(chunks):
             traces_copy(part, k).wait()
+            if part + 1 < row_parts:
+                traces_copy(part + 1, k).start()
             quarters.append(jnp.dot(traces[part, k], table[...], preferred_element_type=jnp.float32))
         parts = turned_sum(quarters, 0, 1, False) + turned_sum(quarters, 2, 3, True)
         energy = jnp.concatenate(
@@ -265,8 +266,9 @@
     )(chan, traces, jnp.asarray(forward_table(length)), quality, owners, places)
 
 
-def cross_kernel(last, with_sum, local_windows, win_ref, first_ref, second_ref, *refs):
+def cross_kernel(last, with_sum, local_windows, awaited, win_ref, first_ref, second_ref, *refs):
     refs = list(refs)
+    refs = refs[awaited:]
     sum_ref = refs.pop(0) if with_sum else None
     if last:
         table_ref, out_ref, done_ref, wide, spread, total, lags, sems = refs
@@ -354,11 +356,13 @@
             copy.wait()
 
 
-def cross_call(win, first, second, ch_dev, own_count, sums, table, local_windows):
+def cross_call(win, first, second, ch_dev, own_count, sums, table, awaited):
+    local_windows = sums is None
     windows, _, columns = first.shape
     last = table is not None
     with_sum = sums is not None
-    operands = [win, first, second]
+    operands = [win, first, second, *awaited]
+    in_specs = [smem_spec(), vmem_spec(), vmem_spec()] + [pl.BlockSpec(memory_space=pl.ANY)] * len(awaited)
     if with_sum:
         operands.append(sums)
     scratch = [
@@ -378,8 +382,8 @@
         out_shape.append(jax.ShapeDtypeStruct((8, H), jnp.float32))
         out_specs = [pl.BlockSpec(memory_space=pl.ANY), vmem_spec()]
     return pl.pallas_call(
-        functools.partial(cross_kernel, last, with_sum, local_windows),
-        in_specs=[smem_spec()] + [vmem_spec()] * (len(operands) - 1),
+        functools.partial(cross_kernel, last, with_sum, local_windows, len(awaited)),
+        in_specs=in_specs + [vmem_spec()] * (len(operands) - len(in_specs)),
         out_specs=out_specs,
         out_shape=out_shape,
         scratch_shapes=scratch,
@@ -480,11 +484,11 @@
         )
         for shift in range(1, win_count)
     ]
-    arrived = [(whitened, upper)] + list(zip(common, special))
+    arrived = [(whitened, upper, common)] + [(rows, others, []) for rows, others in zip(common, special)]
     sums = None
-    for n, (first, second) in enumerate(arrived):
+    for n, (first, second, awaited) in enumerate(arrived):
         ends = tables[0] if n == win_count - 1 else None
-        sums, *done = cross_call(win, first, second, ch_dev, own_count, sums, ends, n == 0)
+        sums, *done = cross_call(win, first, second, ch_dev, own_count, sums, ends, awaited)
     share = fold_call(chan, incoming, flat, owners, ch_dev, tables, done[0])
     fold = lax.dynamic_slice_in_dim(share, window_part * own_count, own_count, 0)
     for shift in range(1, win_count):

time: 68.2 us -> 66.9 us (0.981)
  the two profiles are of different devices: /device:TPU:13 before, /device:TPU:18 now
where the time goes in v7:
time: 66.9 us; the launch traced here: 66.6 us
  Pallas kernels  33.3 us (50%)
  waiting for transfers between devices  19 us (28%)
  starting transfers between devices  9.26 us (14%)
  local copies, waits for them, and re-layouts  2.56 us (4%)
  other arithmetic  1.78 us (3%)
  between operations  0.76 us (1%)
    pallas_call x2, Pallas kernels, cross_call(): pl.pallas_call(functools.partial(cross_kernel, last, with_sum, local_wind...  22.7 us
    ppermute x1, waiting for transfers between devices, from_above(): return lax.ppermute(block, 'chan', [(i, i - 1) for i in range(1, count)])  12.5 us
    pallas_call x1, Pallas kernels, spectra_call(): pl.pallas_call(spectra_kernel, in_specs=[smem_spec()] + [anywhere] * 5, o...  9.72 us
    ppermute x3, waiting for transfers between devices, round_win(): lax.ppermute(block, 'win', [(i, (i + shift) % count) for i in range(count)])  6.52 us
    all_to_all x1, starting transfers between devices, local(): lax.all_to_all(outgoing, 'chan', split_axis=0, concat_axis=0, tiled=True)  5.48 us
    ppermute x1, starting transfers between devices, from_above(): return lax.ppermute(block, 'chan', [(i, i - 1) for i in range(1, count)])  2.75 us
    unnamed x14, local copies, waits for them, and re-layouts  1.76 us
  transfers between devices with their start and end apart: 5, of which 3 were waited for; matrix products, arithmetic and copies ran while one was open for 3% of the time, Pallas kernels for 34%

profile of v7, /device:TPU:18, one launch (start us, length us, event | category | flops | bytes accessed | tf_op | source)
XLA Modules:
  0.0 66.6 jit_solution(3969215421401890589)
XLA Ops:
  0.6 9.7 %spectra.1 = (bf16[768,512]{1,0:T(8,128)(2,1)}, bf16[16,96,512]{2,1,0:T(8,128)(2,1)}, bf16[12,32,512]{2,1,0:T(8,128)(2,1)}) custom-call(s32[1]{0:T(128)} %bitcast.1.chan_ref, bf16[768,4096]{1,0:T(8,128)(2,1)} %bitcast.12, bf16[1024,512]{1,0:T(8,128)(2,1)} %constant.39.clone.table_ref, s32[1,64]{1,0:T(1,128)} %bitcast.14, s32[8,128]{1,0:T(8,128)} %bitcast.10, ...), custom_call_target="tpu_custom_call" | custom-call | flops 3221225472 | bytes 6291456 | tf_op jit(solution)/shard_map/spectra/pallas_call | solution.py:244
  10.4 2.8 %collective-permute-start.1 = (bf16[12,64,512]{2,1,0:T(8,128)(2,1)}, bf16[12,64,512]{2,1,0:T(8,128)(2,1)S(1)}, u32[]{:S(2)}, u32[]{:S(2)}) collective-permute-start(bf16[12,64,512]{2,1,0:T(8,128)(2,1)} %bitcast.7), channel_id=1, source_target_pairs={{2,0},{4,2},{6,4},{8,6},{10,8},{12,10},{14,12},{16,14},{18,16},{20... | collective-permute-start | bytes 2359304 | tf_op jit(solution)/shard_map/ppermute | solution.py:452
  13.1 0.6 collective-permute-start
  13.7 0.0 copy-start
  13.7 5.5 %all-to-all-start = ((bf16[16,96,512]{2,1,0:T(8,128)(2,1)}), bf16[16,96,512]{2,1,0:T(8,128)(2,1)S(1)}, u32[]{:S(2)}, u32[]{:S(2)}) async-start(bf16[16,96,512]{2,1,0:T(8,128)(2,1)} %get-tuple-element.10), calls=%async_computation | async-start | bytes 3145728 | tf_op jit(solution)/shard_map/all_to_all | solution.py:479
  19.2 0.0 copy-done
  19.2 0.8 %slice.4 = bf16[12,32,512]{2,1,0:T(8,128)(2,1)} slice(bf16[12,64,512]{2,1,0:T(8,128)(2,1)S(1)} %bitcast.8), slice={[0:12], [0:32], [0:512]} | slice | bytes 786432 | tf_op jit(solution)/shard_map/slice | solution.py:480
  20.0 12.5 %collective-permute-done.1.second_ref = bf16[12,64,512]{2,1,0:T(8,128)(2,1)S(1)} collective-permute-done((bf16[12,64,512]{2,1,0:T(8,128)(2,1)}, bf16[12,64,512]{2,1,0:T(8,128)(2,1)S(1)}, u32[]{:S(2)}, u32[]{:S(2)}) %collective-permute-start.1) | collective-permute-done | bytes 786464 | tf_op jit(solution)/shard_map/ppermute | solution.py:452
  32.5 1.2 %fusion = bf16[12,64,512]{2,1,0:T(8,128)(2,1)S(1)} fusion(s32[]{:T(128)S(6)} %select_n.19, bf16[12,32,512]{2,1,0:T(8,128)(2,1)} %slice.4, bf16[12,64,512]{2,1,0:T(8,128)(2,1)S(1)} %collective-permute-done.1.second_ref), kind=kLoop, calls=%fused_computation.2 | loop fusion | flops 1572864 | bytes 1966084 | tf_op jit(solution)/shard_map/concatenate | solution.py:480
  33.7 0.1 collective-permute-start.2
  33.7 0.0 collective-permute-done.refs_0_.first_ref
  33.7 0.0 copy-start.4
  33.8 0.7 %copy-done.4 = bf16[12,32,512]{2,1,0:T(8,128)(2,1)} copy-done((bf16[12,32,512]{2,1,0:T(8,128)(2,1)}, bf16[12,32,512]{2,1,0:T(8,128)(2,1)S(1)}, u32[]{:S(2)}) %copy-start.4) | copy-done | bytes 393240
  34.5 0.0 copy-start.5
  34.5 1.0 %copy-done.5 = bf16[12,32,512]{2,1,0:T(8,128)(2,1)S(1)} copy-done((bf16[12,32,512]{2,1,0:T(8,128)(2,1)S(1)}, bf16[12,32,512]{2,1,0:T(8,128)(2,1)}, u32[]{:S(2)}) %copy-start.5) | copy-done | bytes 393240
  35.5 0.0 copy-start.1
  35.5 0.0 copy-start.6
  35.5 10.5 %cross.2.refs_0_ = f32[32,72,256]{2,1,0:T(8,128)S(1)} custom-call(s32[1]{0:T(128)} %bitcast.win_ref, bf16[12,64,512]{2,1,0:T(8,128)(2,1)S(1)} %bitcast.9, bf16[12,64,512]{2,1,0:T(8,128)(2,1)S(1)} %collective-permute-done.1.second_ref, bf16[12,32,512]{2,1,0:T(8,128)(2,1)S(1)} %copy-done.5), custom_call_target="tpu_custom_call" | custom-call | flops 30000001024 | bytes 3932160 | tf_op jit(solution)/shard_map/cross/pallas_call | solution.py:384
  46.0 0.0 copy-start.2
  46.0 0.0 copy-start.3
  46.0 2.9 %collective-permute-done.2.second_ref = bf16[12,64,512]{2,1,0:T(8,128)(2,1)S(1)} collective-permute-done((bf16[12,64,512]{2,1,0:T(8,128)(2,1)S(1)}, bf16[12,64,512]{2,1,0:T(8,128)(2,1)S(1)}, u32[]{:S(2)}, u32[]{:S(2)}) %collective-permute-start.2) | collective-permute-done | bytes 786464 | tf_op jit(solution)/shard_map/ppermute | solution.py:457
  48.9 0.0 copy-done.1
  48.9 0.0 copy-done.6
  48.9 12.3 %cross.3 = (f32[32,64,256]{2,1,0:T(8,128)}, f32[8,128]{1,0:T(8,128)S(1)}) custom-call(s32[1]{0:T(128)} %bitcast.win_ref, bf16[12,32,512]{2,1,0:T(8,128)(2,1)S(1)} %copy-done.6, bf16[12,64,512]{2,1,0:T(8,128)(2,1)S(1)} %collective-permute-done.2.second_ref, f32[32,72,256]{2,1,0:T(8,128)S(1)} %cross.2.refs_0_, bf16[256,256]{1,0:T(8,128)(2,1)S(1)} %copy-done.1), custom_call_target="tpu_custom_call" | custom-call | flops 30000001024 | bytes 3932160 | tf_op jit(solution)/shard_map/cross/pallas_call | solution.py:384
  61.2 0.0 all-to-all-done.incoming_ref
  61.2 0.0 copy-done.2
  61.2 0.0 copy-done.3
  61.2 0.8 %fold.1 = f32[64,256]{1,0:T(8,128)S(1)} custom-call(s32[1]{0:T(128)} %bitcast.1.chan_ref, bf16[16,96,512]{2,1,0:T(8,128)(2,1)S(1)} %all-to-all-done.incoming_ref, bf16[768,512]{1,0:T(8,128)(2,1)S(1)} %copy-done, s32[8,128]{1,0:T(8,128)S(1)} %bitcast.11, bf16[256,256]{1,0:T(8,128)(2,1)S(1)} %copy-done.1, bf16[256,256]{1,0:T(8,128)(2,1)S(1)} %copy-done.2, ...), custom_call_target="tpu_custom_call" | custom-call | flops 201326592 | bytes 2359296 | tf_op jit(solution)/shard_map/fold/pallas_call | solution.py:437
  62.0 0.4 collective-permute-start.3
  62.4 3.6 %collective-permute-done.3 = f32[32,256]{1,0:T(8,128)S(1)} collective-permute-done((f32[32,256]{1,0:T(8,128)S(1)}, f32[32,256]{1,0:T(8,128)S(1)}, u32[]{:S(2)}, u32[]{:S(2)}) %collective-permute-start.3) | collective-permute-done | bytes 32800 | tf_op jit(solution)/shard_map/ppermute | solution.py:457
  66.0 0.6 dynamic-slice_add_fusion
  (1 shorter events, 0.0 us)
Async XLA Ops:
  10.4 22.1 %collective-permute-start.1 = (bf16[12,64,512]{2,1,0:T(8,128)(2,1)}, bf16[12,64,512]{2,1,0:T(8,128)(2,1)S(1)}, u32[]{:S(2)}, u32[]{:S(2)}) collective-permute-start(bf16[12,64,512]{2,1,0:T(8,128)(2,1)} %bitcast.7), channel_id=1, source_target_pairs={{2,0},{4,2},{6,4},{8,6},{10,8},{12,10},{14,12},{16,14},{18,16},{20... | collective-permute-start | bytes 2359304 | tf_op jit(solution)/shard_map/ppermute | solution.py:452
  13.1 20.6 %collective-permute-start = (bf16[12,32,512]{2,1,0:T(8,128)(2,1)}, bf16[12,32,512]{2,1,0:T(8,128)(2,1)S(1)}, u32[]{:S(2)}, u32[]{:S(2)}) collective-permute-start(bf16[12,32,512]{2,1,0:T(8,128)(2,1)} %get-tuple-element.7), channel_id=1, source_target_pairs={{0,1},{1,0},{2,3},{3,2},{4,5},{5,4},{6,7},{7,6},{8,9},{9,8},{10,11... | collective-permute-start | bytes 1179656 | tf_op jit(solution)/shard_map/ppermute | solution.py:457
  13.7 5.5 %copy-start = (bf16[768,512]{1,0:T(8,128)(2,1)S(1)}, bf16[768,512]{1,0:T(8,128)(2,1)}, u32[]{:S(2)}) copy-start(bf16[768,512]{1,0:T(8,128)(2,1)} %get-tuple-element.8.own_ref) | copy-start | bytes 2359300
  13.7 47.4 %all-to-all-start = ((bf16[16,96,512]{2,1,0:T(8,128)(2,1)}), bf16[16,96,512]{2,1,0:T(8,128)(2,1)S(1)}, u32[]{:S(2)}, u32[]{:S(2)}) async-start(bf16[16,96,512]{2,1,0:T(8,128)(2,1)} %get-tuple-element.10), calls=%async_computation | async-start | bytes 3145728 | tf_op jit(solution)/shard_map/all_to_all | solution.py:479
  33.7 15.2 %collective-permute-start.2 = (bf16[12,64,512]{2,1,0:T(8,128)(2,1)S(1)}, bf16[12,64,512]{2,1,0:T(8,128)(2,1)S(1)}, u32[]{:S(2)}, u32[]{:S(2)}) collective-permute-start(bf16[12,64,512]{2,1,0:T(8,128)(2,1)S(1)} %fusion), channel_id=1, source_target_pairs={{0,1},{1,0},{2,3},{3,2},{4,5},{5,4},{6,7},{7,6},{8,9},{9,8},{10,11... | collective-permute-start | bytes 2359304 | tf_op jit(solution)/shard_map/ppermute | solution.py:457
  33.7 0.7 %copy-start.4 = (bf16[12,32,512]{2,1,0:T(8,128)(2,1)}, bf16[12,32,512]{2,1,0:T(8,128)(2,1)S(1)}, u32[]{:S(2)}) copy-start(bf16[12,32,512]{2,1,0:T(8,128)(2,1)S(1)} %collective-permute-done.refs_0_.first_ref) | copy-start | bytes 1179652
  34.5 1.0 %copy-start.5 = (bf16[12,32,512]{2,1,0:T(8,128)(2,1)S(1)}, bf16[12,32,512]{2,1,0:T(8,128)(2,1)}, u32[]{:S(2)}) copy-start(bf16[12,32,512]{2,1,0:T(8,128)(2,1)} %copy-done.4) | copy-start | bytes 1179652
  35.5 13.4 %copy-start.1 = (bf16[256,256]{1,0:T(8,128)(2,1)S(1)}, bf16[256,256]{1,0:T(8,128)(2,1)}, u32[]{:S(2)}) copy-start(bf16[256,256]{1,0:T(8,128)(2,1)} %constant.37.clone.refs_1_.high_ref) | copy-start | bytes 393220
  35.5 13.4 %copy-start.6 = (bf16[12,32,512]{2,1,0:T(8,128)(2,1)S(1)}, bf16[12,32,512]{2,1,0:T(8,128)(2,1)}, u32[]{:S(2)}) copy-start(bf16[12,32,512]{2,1,0:T(8,128)(2,1)} %copy-done.4) | copy-start | bytes 1179652
  46.0 15.2 %copy-start.2 = (bf16[256,256]{1,0:T(8,128)(2,1)S(1)}, bf16[256,256]{1,0:T(8,128)(2,1)}, u32[]{:S(2)}) copy-start(bf16[256,256]{1,0:T(8,128)(2,1)} %constant.38.clone.low_ref) | copy-start | bytes 393220
  46.0 15.2 %copy-start.3 = (s32[1024,1]{0,1:T(1,128)S(1)}, s32[1024,1]{0,1:T(1,128)}, u32[]{:S(2)}) copy-start(s32[1024,1]{0,1:T(1,128)} %param.9) | copy-start | bytes 12292
  62.0 4.0 %collective-permute-start.3 = (f32[32,256]{1,0:T(8,128)S(1)}, f32[32,256]{1,0:T(8,128)S(1)}, u32[]{:S(2)}, u32[]{:S(2)}) collective-permute-start(f32[32,256]{1,0:T(8,128)S(1)} %constant_dynamic-slice_fusion), channel_id=1, source_target_pairs={{0,1},{1,0},{2,3},{3,2},{4,5},{5,4},{6,7},{7,6},{8,9},{9,8},{10,11... | collective-permute-start | bytes 98312 | tf_op jit(solution)/shard_map/ppermute | solution.py:457
